TPU v7x, 32 devices: a whole 2x2x4 slice. The times are simulated.
32 devices in a mesh: dom: 32 (over z, y, x, core).
Axes of the slice: x: 2, y: 2, z: 4, core: 2. Of those that a mesh axis runs over, the one named last changes fastest.
Arguments:
- features: bfloat16 [8192, 2048], P('dom'), may hold values from -6 to 6
- weight: bfloat16 [2048, 2048], replicated, may hold values from -0.125 to 0.125
- bias: float32 [2048], replicated, may hold values from -1 to 1
- gamma: float32 [2048], replicated, may hold values from 0.1 to 1.9
- beta: float32 [2048], replicated, may hold values from -3 to 3
- neighbours: int32 [8192, 16], P('dom'), may hold values from 0 to 1279
- edge_mask: int32 [8192, 16], P('dom'), may hold values from 0 to 1, as said below
- node_mask: int32 [8192], P('dom'), may hold values from 0 to 1, as said below
- send_rows: int32 [1024], P('dom'), may hold values from 0 to 255
- send_mask: int32 [1024], P('dom'), may hold values from 0 to 1, as said below
- cotangent: bfloat16 [8192, 2048], P('dom'), may hold values from -6 to 6
Outputs:
- activations: bfloat16 [8192, 2048], P('dom')
- grad_features: bfloat16 [8192, 2048], P('dom')
- grad_weight: float32 [2048, 2048], replicated
- grad_bias: float32 [2048], replicated
- scale_gradient: float32 [2048], replicated
- shift_gradient: float32 [2048], replicated
Inputs may be any that keep to these rules, and one draw needn't show every extreme that they name: `edge_mask`: each node's edges fill the first slots of its list; a node has 16, 8, 4, 2 or 1 edges. `node_mask`: the last partition's nodes are all valid. `send_mask`: the live slots of a partition come first; a partition has 32 or 24 live; the first partition has all 32 live.
All inputs are finite; a program needn't handle non-finite values.
Results may differ from a plain program's by a relative error of at most 0.02.
Values may be sent and summed in bfloat16 or wider, within the bound.
No kernel may reach another device: no remote copies, remote signals or barrier semaphores. Data moves between devices by JAX's collectives and lax.ppermute only.
A program may use at most 192 MiB of HBM per device.

v0:
```python
import jax
import jax.numpy as jnp
from jax import lax
from jax.sharding import PartitionSpec as P


def on_device(
    features,
    weight,
    bias,
    gamma,
    beta,
    neighbours,
    edge_mask,
    node_mask,
    send_rows,
    send_mask,
    cotangent,
):
    nodes = features.shape[0]
    width = features.shape[1]
    slots = neighbours.shape[1]
    emask = edge_mask.astype(jnp.float32)
    inverse = 1.0 / (jnp.sum(emask, axis=1) + 1.0)
    valid_rows_mask = node_mask.astype(jnp.float32)[:, None]
    live = send_mask.astype(jnp.float32)[:, None]
    outgoing = features[send_rows] * send_mask.astype(jnp.bfloat16)[:, None]
    halo = lax.all_gather(outgoing, "dom", axis=0, tiled=True)
    table = jnp.concatenate([features, halo], axis=0)
    picked = table[neighbours]
    summed = jnp.einsum(
        "ne,nef->nf", edge_mask.astype(jnp.bfloat16), picked, preferred_element_type=jnp.float32
    )
    total = 2.0 * features.astype(jnp.float32) + summed
    agg = (total * inverse[:, None]).astype(jnp.bfloat16)
    zval = jnp.dot(agg, weight, preferred_element_type=jnp.float32) + bias
    sigma = jax.nn.sigmoid(zval)
    yval = zval * sigma
    valid_count, column_sum = lax.psum(
        (jnp.sum(valid_rows_mask), jnp.sum(yval * valid_rows_mask, axis=0)), "dom"
    )
    mean = column_sum / valid_count
    centered_values = yval - mean
    var = (
        lax.psum(jnp.sum(centered_values * centered_values * valid_rows_mask, axis=0), "dom")
        / valid_count
    )
    inverse_deviation = lax.rsqrt(var + 1e-05)
    normalized_input = centered_values * inverse_deviation
    activations = (valid_rows_mask * (gamma * normalized_input + beta)).astype(jnp.bfloat16)
    incoming_gradient = cotangent.astype(jnp.float32) * valid_rows_mask
    shift_gradient, scale_gradient = lax.psum(
        (jnp.sum(incoming_gradient, axis=0), jnp.sum(incoming_gradient * normalized_input, axis=0)),
        "dom",
    )
    output_gradient = (
        valid_rows_mask
        * gamma
        * inverse_deviation
        * (
            incoming_gradient
            - shift_gradient / valid_count
            - normalized_input * scale_gradient / valid_count
        )
    )
    dzval = (output_gradient * (sigma + zval * sigma * (1.0 - sigma))).astype(jnp.bfloat16)
    weight_part = lax.dot_general(
        agg, dzval, (((0,), (0,)), ((), ())), preferred_element_type=jnp.float32
    )
    bias_part = jnp.sum(dzval.astype(jnp.float32), axis=0)
    grad_weight, grad_bias = lax.psum((weight_part, bias_part), "dom")
    back_agg = lax.dot_general(
        dzval, weight, (((1,), (1,)), ((), ())), preferred_element_type=jnp.float32
    )
    scaled = back_agg * inverse[:, None]
    updates = (emask[:, :, None] * scaled[:, None, :]).reshape(nodes * slots, width)
    grad_table = (
        jnp.zeros((table.shape[0], width), jnp.float32).at[neighbours.reshape(-1)].add(updates)
    )
    grad_local = 2.0 * scaled + grad_table[:nodes]
    halo_part = grad_table[nodes:]
    returned = lax.psum_scatter(halo_part, "dom", scatter_dimension=0, tiled=True)
    grad_local = grad_local.at[send_rows].add(returned * live)
    return (
        activations,
        grad_local.astype(jnp.bfloat16),
        grad_weight,
        grad_bias,
        scale_gradient,
        shift_gradient,
    )


def solution(mesh):
    return jax.shard_map(
        on_device,
        mesh=mesh,
        in_specs=(
            P("dom", None),
            P(),
            P(),
            P(),
            P(),
            P("dom", None),
            P("dom", None),
            P("dom"),
            P("dom"),
            P("dom"),
            P("dom", None),
        ),
        out_specs=(P("dom", None), P("dom", None), P(), P(), P(), P()),
        check_vma=False,
    )
```

profile of v0, /device:TPU:0, one launch (start us, length us, event | category | flops | bytes accessed | tf_op | source)
XLA Modules:
  0.0 789.9 jit_solution(11282826133308076524)
XLA Ops:
  7.2 0.8 fusion.10
  8.0 2.1 gather_fusion
  10.2 0.7 broadcast_multiply_fusion
  11.0 0.8 copy.18
  11.8 0.7 compare_select_fusion.1
  12.7 0.8 fusion.9
  14.7 61.6 %all-gather.2.cloned.1.call-done = bf16[1024,2048]{1,0:T(8,128)(2,1)} async-done(((bf16[32,2048]{1,0:T(8,128)(2,1)}), bf16[1024,2048]{1,0:T(8,128)(2,1)}) %all-gather.2.cloned.1.call-update) | async-done | bytes 4194320 | tf_op jit(solution)/shard_map/all_gather | solution.py:28
  76.3 5.3 pad_maximum_fusion
  81.6 34.5 %gather_fusion.1 = bf16[4096,2048]{1,0:T(8,128)(2,1)} fusion(bf16[1280,2048]{1,0:T(8,128)(2,1)} %pad_maximum_fusion, s32[4096]{0:T(1024)S(1)} %broadcast_clamp_fusion), kind=kCustom, calls=%fused_computation.1 | custom fusion | bytes 33570816 | tf_op jit(solution)/shard_map/gather | solution.py:30
  116.1 7.2 fusion.11
  123.3 1.3 fusion.3
  124.6 6.1 multiply_reduce_fusion.2
  130.7 39.4 %all-reduce.1 = (f32[2048]{0:T(1024)S(1)}, f32[]{:T(128)}) all-reduce(f32[2048]{0:T(1024)S(1)} %get-tuple-element.19, f32[]{:T(128)} %convert_reduce_fusion.2), channel_id=1, replica_groups=mesh['dom'=32] {'dom'}, use_global_device_ids=true, to_apply=%region_2.0 | all-reduce | flops 2049 | bytes 16392 | tf_op jit(solution)/shard_map/psum | solution.py:39
  170.7 0.7 multiply_reduce_fusion.1
  171.5 40.5 %psum.51 = f32[2048]{0:T(1024)S(1)} all-reduce(f32[2048]{0:T(1024)S(1)} %multiply_reduce_fusion.1), channel_id=1, replica_groups=mesh['dom'=32] {'dom'}, use_global_device_ids=true, to_apply=%region_6.0 | all-reduce | flops 2048 | bytes 16384 | tf_op jit(solution)/shard_map/psum | solution.py:45
  211.9 0.7 add_rsqrt_fusion
  212.6 2.1 fusion.4
  214.7 40.3 %all-reduce = (f32[2048]{0:T(1024)S(1)}, f32[2048]{0:T(1024)S(1)}) all-reduce(f32[2048]{0:T(1024)S(1)} %get-tuple-element.7, f32[2048]{0:T(1024)S(1)} %get-tuple-element.6), channel_id=1, replica_groups=mesh['dom'=32] {'dom'}, use_global_device_ids=true, to_apply=%region_10.0 | all-reduce | flops 4096 | bytes 32768 | tf_op jit(solution)/shard_map/psum | solution.py:52
  255.1 0.7 broadcast_divide_fusion
  255.8 4.4 convert_reduce_fusion
  260.1 6.1 convolution_multiply_fusion
  266.3 11.2 %bitcast_multiply_fusion = f32[4096,2048]{1,0:T(8,128)} fusion(f32[256,2048]{1,0:T(8,128)S(1)} %convolution_multiply_fusion, f32[4096]{0:T(1024)S(1)} %mul.164), kind=kLoop, calls=%fused_computation.4 | loop fusion | flops 8388608 | bytes 35667968 | tf_op jit(solution)/shard_map/mul | solution.py:76
  277.5 56.6 %scatter_custom_fusion = f32[1280,2048]{1,0:T(8,128)} fusion(s32[4096]{0:T(1024)S(1)} %bitcast.21, f32[4096,2048]{1,0:T(8,128)} %bitcast_multiply_fusion, f32[]{:T(128)} %constant.0.clone.1), kind=kCustom, calls=%fused_computation.6 | custom fusion | flops 8388608 | bytes 10486272 | tf_op jit(solution)/shard_map/scatter-add | solution.py:78
  334.1 7.7 slice.13
  341.9 9.8 %fusion.12 = f32[2048,2048]{1,0:T(8,128)} fusion(bf16[256,2048]{1,0:T(8,128)(2,1)S(1)} %fusion.3, bf16[256,2048]{1,0:T(8,128)(2,1)} %copy-done.1), kind=kOutput, calls=%fused_computation.44 | convolution fusion | flops 2147483648 | bytes 18874368 | tf_op jit(solution)/shard_map/dot_general | solution.py:67
  351.7 42.7 %psum.55 = f32[2048]{0:T(1024)} all-reduce(f32[2048]{0:T(1024)S(1)} %get-tuple-element.12), channel_id=1, replica_groups=mesh['dom'=32] {'dom'}, use_global_device_ids=true, to_apply=%region_16.0 | all-reduce | flops 2048 | bytes 16384 | tf_op jit(solution)/shard_map/psum | solution.py:71
  394.4 3.3 slice_add_fusion
  397.7 93.4 %reduce-scatter.2.cloned.1.call-done = f32[32,2048]{1,0:T(8,128)} async-done(((f32[1024,2048]{1,0:T(8,128)}), f32[32,2048]{1,0:T(8,128)}) %reduce-scatter.2.cloned.1.call-update) | async-done | bytes 262160 | tf_op jit(solution)/shard_map/reduce_scatter | solution.py:82
  491.1 4.4 scatter_custom_fusion.1
  495.5 2.7 convert_element_type.46
  498.2 273.4 %all-reduce.4.cloned.1.call-done = f32[2048,2048]{1,0:T(8,128)} async-done(((f32[2048,2048]{1,0:T(8,128)}), f32[2048,2048]{1,0:T(8,128)}) %all-reduce.4.cloned.1.call-update) | async-done | bytes 16777232 | tf_op jit(solution)/shard_map/psum | solution.py:71
  771.6 11.8 %copy.25 = f32[2048,2048]{1,0:T(8,128)} copy(f32[2048,2048]{1,0:T(8,128)} %all-reduce.4.cloned.1.call-done) | data formatting | bytes 33554432
  (38 shorter events, 2.2 us)
Async XLA Ops:
  7.2 69.1 %copy-start = (bf16[256,2048]{1,0:T(8,128)(2,1)S(1)}, bf16[256,2048]{1,0:T(8,128)(2,1)}, u32[]{:S(2)}) copy-start(bf16[256,2048]{1,0:T(8,128)(2,1)} %param.11) | copy-start | bytes 3145732
  7.2 7.4 copy-start.2
  7.2 6.5 copy-start.7
  7.2 69.1 %all-gather.2.cloned.1.call-start = ((), (), s32[]{:S(2)}) async-start(), calls=%async_computation.1 | async-start | bytes 4325376 | tf_op jit(solution)/shard_map/all_gather | solution.py:28
  10.9 480.2 %reduce-scatter.2.cloned.1.call-start = ((), (), s32[]{:S(2)}) async-start(), calls=%async_computation.2 | async-start | bytes 8650752 | tf_op jit(solution)/shard_map/reduce_scatter | solution.py:82
  123.3 1.3 copy-start.8
  171.5 84.3 %copy-start.3 = (f32[2048]{0:T(1024)S(1)}, f32[2048]{0:T(1024)}, u32[]{:S(2)}) copy-start(f32[2048]{0:T(1024)} %param.14) | copy-start | bytes 24580
  171.5 84.3 %copy-start.4 = (f32[2048]{0:T(1024)S(1)}, f32[2048]{0:T(1024)}, u32[]{:S(2)}) copy-start(f32[2048]{0:T(1024)} %param.15) | copy-start | bytes 24580
  255.1 5.1 copy-start.5
  255.1 5.1 copy-start.6
  260.1 6.1 copy-start.1
  341.9 429.8 %all-reduce.4.cloned.1.call-start = ((), (), s32[]{:S(2)}) async-start(), calls=%async_computation.3 | async-start | bytes 33554432 | tf_op jit(solution)/shard_map/psum | solution.py:71
Sparse Core Ops, SparseCore 0:
  11.5 64.7 all-gather.1
  342.0 149.1 reduce-scatter.1
  497.7 273.8 all-reduce.3
where the time goes:
time: 791 us; the launch traced here: 790 us
  waiting for transfers between devices  428 us (54%)
  blocking collectives  163 us (21%)
  other arithmetic  97.8 us (12%)
  local copies, waits for them, and re-layouts  57.6 us (7%)
  matrix products  29.2 us (4%)
  between operations  14 us (2%)
    psum x1, waiting for transfers between devices, on_device(): grad_weight, grad_bias = lax.psum((weight_part, bias_part), 'dom')  273 us
    reduce_scatter x1, waiting for transfers between devices, on_device(): lax.psum_scatter(halo_part, 'dom', scatter_dimension=0, tiled=True)  93.4 us
    all_gather x1, waiting for transfers between devices, on_device(): halo = lax.all_gather(outgoing, 'dom', axis=0, tiled=True)  61.6 us
    scatter-add x1, other arithmetic, on_device(): jnp.zeros((table.shape[0], width), jnp.float32).at[neighbours.reshape(-1)]  56.6 us
    psum x1, blocking collectives, on_device(): grad_weight, grad_bias = lax.psum((weight_part, bias_part), 'dom')  42.7 us
    psum x1, blocking collectives, on_device(): lax.psum(jnp.sum(centered_values * centered_values * valid_rows_mask, axi...  40.5 us
    psum x1, blocking collectives, on_device(): lax.psum((jnp.sum(incoming_gradient, axis=0), jnp.sum(incoming_gradient *...  40.3 us
    psum x1, blocking collectives, on_device(): lax.psum((jnp.sum(valid_rows_mask), jnp.sum(yval * valid_rows_mask, axis=...  39.4 us
  transfers between devices with their start and end apart: 3, of which 3 were waited for; matrix products, arithmetic and copies ran while one was open for 3% of the time, Pallas kernels for 0%

commit v1 on v0

v1 whole, which is shorter than its diff:
```python
import functools

import jax
import jax.numpy as jnp
from jax import lax
from jax.experimental import pallas as pl
from jax.experimental.pallas import tpu as pltpu
from jax.sharding import PartitionSpec as P

BF = jnp.bfloat16
F32 = jnp.float32


def dot(a, b, dims=((1,), (0,))):
    return lax.dot_general(a, b, (dims, ((), ())), preferred_element_type=F32)


def place_kernel(where, piece, total, out):
    out[...] = piece[...].astype(out.dtype)


def place(total, piece, row_xor, column_block, blocks, shape):
    rows, w = piece.shape
    block = rows // blocks
    where = jnp.stack([row_xor, column_block]).astype(jnp.int32)
    operands = [where, piece]
    in_specs = [pl.BlockSpec((block, w), lambda i, s: (i ^ s[0], 0))]
    aliases = {}
    if total is not None:
        operands.append(total)
        in_specs.append(pl.BlockSpec(memory_space=pl.ANY))
        aliases = {2: 0}
        body = place_kernel
    else:
        def body(where, piece, out):
            place_kernel(where, piece, None, out)
    return pl.pallas_call(
        body,
        out_shape=jax.ShapeDtypeStruct(shape, F32),
        grid_spec=pltpu.PrefetchScalarGridSpec(
            num_scalar_prefetch=1,
            grid=(blocks,),
            in_specs=in_specs,
            out_specs=pl.BlockSpec((block, w), lambda i, s: (i, s[1])),
        ),
        input_output_aliases=aliases,
        name="place",
    )(*operands)


def on_device(
    size,
    features,
    weight,
    bias,
    gamma,
    beta,
    neighbours,
    edge_mask,
    node_mask,
    send_rows,
    send_mask,
    cotangent,
):
    nodes, width = features.shape
    slots = neighbours.shape[1]
    sends = send_rows.shape[0]
    half = width // 2
    quarter = width // 4
    rest = list(range(3, size.bit_length() - 1))

    me = lax.axis_index("dom")
    core = me & 1
    is0 = core == 0
    b1, b2 = (me >> 1) & 1, (me >> 2) & 1
    first = jnp.where(is0, b1, b2)
    second = jnp.where(is0, b2, b1)
    first_weight = jnp.where(is0, 2, 4)
    second_weight = 6 - first_weight

    def bit(b):
        return (me >> b) & 1

    core_perm = [(i, i ^ 1) for i in range(size)]
    first_perm = [(i, i ^ (4 if i & 1 else 2)) for i in range(size)]
    second_perm = [(i, i ^ (2 if i & 1 else 4)) for i in range(size)]

    def send(x, perm):
        return lax.ppermute(x, "dom", perm)

    def swap(x):
        return send(x, core_perm)

    def along(x, b):
        return send(x, [(i, i ^ (1 << b)) for i in range(size)])

    def mine(x):
        return lax.dynamic_slice_in_dim(x, core * half, half, x.ndim - 1)

    def other(x):
        return lax.dynamic_slice_in_dim(x, (1 - core) * half, half, x.ndim - 1)

    def ordered(own, sibling, axis):
        return jnp.where(
            is0, jnp.concatenate([own, sibling], axis), jnp.concatenate([sibling, own], axis)
        )

    live_row = jnp.where(send_mask > 0, send_rows, -1)
    rows_hot = (live_row[:, None] == jnp.arange(nodes)[None, :]).astype(BF)
    outgoing = dot(rows_hot, features).astype(BF)
    halo = jnp.concatenate([mine(outgoing), swap(other(outgoing))], 0)
    for b in reversed(rest):
        halo = jnp.concatenate([halo, along(halo, b)], 0)
    halo = jnp.concatenate([halo, send(halo, second_perm)], 0)
    halo = jnp.concatenate([halo, send(halo, first_perm)], 0)

    live_neighbour = jnp.where(edge_mask > 0, neighbours, -1)
    packed = jnp.concatenate([live_neighbour, node_mask[:, None]], 1)
    packed = ordered(packed, swap(packed), 0)
    chip_neighbours, valid = packed[:, :slots], packed[:, slots:].astype(F32)
    inverse = 1.0 / (jnp.sum((chip_neighbours >= 0).astype(F32), 1, keepdims=True) + 1.0)
    chip_features = ordered(mine(features), swap(other(features)), 0)
    grad_in = ordered(mine(cotangent), swap(other(cotangent)), 0)

    halo_rows = sends * size
    place_of = jnp.arange(halo_rows)
    chip, row = place_of // (2 * sends), place_of % (2 * sends)
    levels = len(rest)
    relative = ((chip >> (levels + 1)) & 1) * first_weight + ((chip >> levels) & 1) * second_weight
    for k, b in enumerate(rest):
        relative = relative + (((chip >> (levels - 1 - k)) & 1) << b)
    owner = (me ^ relative) ^ (row // sends)
    label = nodes + owner * sends + row % sends

    def counts(lists, labels):
        total = 0.0
        for e in range(slots):
            total = total + jnp.where(lists[:, e : e + 1] == labels[None, :], 1.0, 0.0)
        return total

    halo_count = counts(chip_neighbours, label).astype(BF)
    local = jnp.arange(nodes)
    own_count = counts(chip_neighbours, local) + jnp.where(
        jnp.arange(2 * nodes)[:, None] % nodes == local[None, :], 2.0, 0.0
    )
    own_count = own_count.astype(BF).reshape(2, nodes, nodes)

    def per_core(a, b, contract):
        return lax.dot_general(
            a, b.reshape(2, nodes, half), (((contract,), (1,)), ((0,), (0,))), preferred_element_type=F32
        ).reshape(2 * nodes, half)

    own_sum = per_core(own_count, chip_features, 2)
    agg_mine = ((dot(halo_count, halo) + own_sum) * inverse).astype(BF)
    agg_other = swap(agg_mine)
    weight_mine = lax.dynamic_slice(weight, (core * half, core * half), (half, half))
    weight_other = lax.dynamic_slice(weight, ((1 - core) * half, core * half), (half, half))
    z = dot(agg_mine, weight_mine) + dot(agg_other, weight_other) + mine(bias)
    sigma = jax.nn.sigmoid(z)
    y = z * sigma
    slope = sigma * (1.0 + z * (1.0 - sigma)) * valid
    g = grad_in.astype(F32) * valid

    count = jnp.sum(valid)
    y_sum = jnp.sum(y * valid, 0)
    centred = (y - y_sum / jnp.maximum(count, 1.0)) * valid
    stats = jnp.stack(
        [
            jnp.full((half,), count),
            y_sum,
            jnp.sum(centred * centred, 0),
            jnp.sum(g, 0),
            jnp.sum(g * centred, 0),
            jnp.sum(slope * g, 0),
            jnp.sum(slope, 0),
            jnp.sum(slope * centred, 0),
        ]
    )

    def merge(own, received, upper):
        a, b = jnp.where(upper, received, own), jnp.where(upper, own, received)
        na, nb = a[0], b[0]
        n = na + nb
        ma, mb = a[1] / jnp.maximum(na, 1.0), b[1] / jnp.maximum(nb, 1.0)
        m = (a[1] + b[1]) / jnp.maximum(n, 1.0)
        da, db = ma - m, mb - m
        return jnp.stack(
            [
                n,
                a[1] + b[1],
                (a[2] + na * da * da) + (b[2] + nb * db * db),
                a[3] + b[3],
                (a[4] + da * a[3]) + (b[4] + db * b[3]),
                a[5] + b[5],
                a[6] + b[6],
                (a[7] + da * a[6]) + (b[7] + db * b[6]),
            ]
        )

    for b in rest:
        stats = merge(stats, along(stats, b), bit(b) == 1)
    stats = merge(stats, send(stats, first_perm), first == 1)
    stats = merge(stats, send(stats, second_perm), second == 1)
    n = stats[0]
    mean = stats[1] / n
    inverse_deviation = lax.rsqrt(stats[2] / n + 1e-05)
    shift_gradient = stats[3]
    scale_gradient = inverse_deviation * stats[4]
    gain = mine(gamma) * inverse_deviation
    bias_gradient = gain * (
        stats[5] - shift_gradient / n * stats[6] - inverse_deviation * scale_gradient / n * stats[7]
    )
    vectors = jnp.stack([bias_gradient, scale_gradient, shift_gradient])
    vectors = ordered(vectors, swap(vectors), 1)

    normalized = (y - mean) * inverse_deviation
    activations = (valid * (mine(gamma) * normalized + mine(beta))).astype(BF)
    dy = gain * (g - shift_gradient / n - normalized * (scale_gradient / n))
    dz_wide = dy * slope
    dz = dz_wide.astype(BF)
    dz_scaled = (dz_wide * inverse).astype(BF)

    def rows_of(x, k):
        return lax.dynamic_slice_in_dim(x, k * nodes, nodes, 0)

    activations = ordered(rows_of(activations, core), swap(rows_of(activations, 1 - core)), 1)

    same = second == core
    agg_keep = jnp.where(same, agg_mine, agg_other)
    agg_send = jnp.where(same, agg_other, agg_mine)
    agg_keep = jnp.concatenate([agg_keep, send(agg_keep, first_perm)], 0)
    agg_send = jnp.concatenate([agg_send, send(agg_send, first_perm)], 0)
    dz_keep = lax.dynamic_slice_in_dim(dz, first * quarter, quarter, 1)
    dz_send = lax.dynamic_slice_in_dim(dz, (1 - first) * quarter, quarter, 1)
    dz_pair = jnp.concatenate([dz_keep, send(dz_send, first_perm)], 0)
    by_rows = ((0,), (0,))
    received = send(dot(agg_send, dz_pair, by_rows).astype(BF), second_perm)
    part = (dot(agg_keep, dz_pair, by_rows) + received.astype(F32)).astype(BF)
    for b in rest:
        rows = part.shape[0] // 2
        out = lax.dynamic_slice_in_dim(part, (1 - bit(b)) * rows, rows, 0)
        keep = lax.dynamic_slice_in_dim(part, bit(b) * rows, rows, 0)
        part = (keep.astype(F32) + along(out, b).astype(F32)).astype(BF)
    for b in reversed(rest):
        part = jnp.concatenate([part, along(part, b)], 0)
    part = jnp.concatenate([part, send(part, second_perm)], 0)
    blocks = size // 4
    low = 0
    for k, b in enumerate(rest):
        low = low + (bit(b) << (levels - 1 - k))
    own_xor, sibling_xor = (second << levels) + low, (first << levels) + low
    pair = send(part, first_perm)
    shape = (width, width)
    total = place(None, part, own_xor, core * 2 + first, blocks, shape)
    total = place(total, swap(part), sibling_xor, (1 - core) * 2 + second, blocks, shape)
    total = place(total, pair, own_xor, core * 2 + 1 - first, blocks, shape)
    total = place(total, swap(pair), sibling_xor, (1 - core) * 2 + 1 - second, blocks, shape)

    cut = halo_rows // 2
    received = send(dot(halo_count[:, cut:], dz_scaled, by_rows).astype(BF), first_perm)
    back = dot(halo_count[:, :cut], dz_scaled, by_rows) + received.astype(F32)
    for hop in [second_perm] + [[(i, i ^ (1 << b)) for i in range(size)] for b in rest]:
        cut = cut // 2
        back = back[:cut] + send(back[cut:].astype(BF), hop).astype(F32)
    back = back.astype(BF)
    own_back = per_core(own_count, dz_scaled, 1)
    back_rows = ordered(back[:sends], swap(back[sends:]), 1)
    own_rows = ordered(
        rows_of(own_back, core).astype(BF), swap(rows_of(own_back, 1 - core).astype(BF)), 1
    )
    table_back = (own_rows.astype(F32) + dot(rows_hot, back_rows, by_rows)).astype(BF)
    grad_features = dot(table_back, weight, ((1,), (1,))).astype(BF)
    return activations, grad_features, total, vectors[0], vectors[1], vectors[2]


def solution(mesh):
    size = mesh.shape["dom"]
    return jax.shard_map(
        functools.partial(on_device, size),
        mesh=mesh,
        in_specs=(
            P("dom", None),
            P(),
            P(),
            P(),
            P(),
            P("dom", None),
            P("dom", None),
            P("dom"),
            P("dom"),
            P("dom"),
            P("dom", None),
        ),
        out_specs=(P("dom", None), P("dom", None), P(), P(), P(), P()),
        check_vma=False,
    )
```

time: 791 us -> 299 us (0.38)
  waiting for transfers between devices: 428 us -> 163 us
  blocking collectives: 163 us -> 0 us
  other arithmetic: 97.8 us -> 28.7 us
  local copies, waits for them, and re-layouts: 57.6 us -> 13.5 us
  starting transfers between devices: 0.12 us -> 31 us
  Pallas kernels: 0 us -> 26.6 us
  between operations: 14 us -> 2.12 us
    psum x1 -> x0, waiting for transfers between devices: 273 us -> none  [on_device(): grad_weight, grad_bias = lax.psum((weight_part, bias_part), 'dom')]
    ppermute x0 -> x33, waiting for transfers between devices: none -> 163 us  [send(): return lax.ppermute(x, 'dom', perm)]
    psum x4 -> x0, blocking collectives: 163 us -> none  [the longest x1 42.7 us: on_device(): grad_weight, grad_bias = lax.psum((weight_part, bias_part), 'dom')]
    reduce_scatter x1 -> x0, waiting for transfers between devices: 93.4 us -> none  [on_device(): lax.psum_scatter(halo_part, 'dom', scatter_dimension=0, tiled=True)]
    all_gather x1 -> x0, waiting for transfers between devices: 61.6 us -> none  [on_device(): halo = lax.all_gather(outgoing, 'dom', axis=0, tiled=True)]
    scatter-add x2 -> x0, other arithmetic: 61 us -> none  [the longest x1 56.6 us: on_device(): jnp.zeros((table.shape[0], width), jnp.float32).at[neighbours.reshape(-1)]]
    gather x2 -> x0, local copies, waits for them, and re-layouts: 36.6 us -> none  [the longest x1 34.5 us: on_device(): picked = table[neighbours]]
    ppermute x0 -> x33, starting transfers between devices: none -> 31 us  [send(): return lax.ppermute(x, 'dom', perm)]
  transfers between devices with their start and end apart: 3 -> 33, of which waited for: 3 -> 17; matrix products, arithmetic and copies ran while one was open for 3% -> 17% of each run, Pallas kernels for 0% -> 7%
where the time goes in v1:
time: 299 us; the launch traced here: 298 us
  waiting for transfers between devices  163 us (55%)
  matrix products  33 us (11%)
  starting transfers between devices  31 us (10%)
  other arithmetic  28.7 us (10%)
  Pallas kernels  26.6 us (9%)
  local copies, waits for them, and re-layouts  13.5 us (5%)
    ppermute x33, waiting for transfers between devices, send(): return lax.ppermute(x, 'dom', perm)  163 us
    ppermute x33, starting transfers between devices, send(): return lax.ppermute(x, 'dom', perm)  31 us
    dot_general x9, matrix products, dot(): return lax.dot_general(a, b, (dims, ((), ())), preferred_element_type=F32)  30.3 us
    pallas_call x4, Pallas kernels, place(): pl.pallas_call(body, out_shape=jax.ShapeDtypeStruct(shape, F32), grid_spe...  26.6 us
    unnamed x61, local copies, waits for them, and re-layouts  8.03 us
  transfers between devices with their start and end apart: 33, of which 17 were waited for; matrix products, arithmetic and copies ran while one was open for 17% of the time, Pallas kernels for 7%

profile of v1, /device:TPU:0, one launch (start us, length us, event | category | flops | bytes accessed | tf_op | source)
XLA Modules:
  0.0 298.2 jit_solution(10170576679093293032)
XLA Ops:
  5.1 4.1 %collective-permute-start.2 = (bf16[64,1024]{1,0:T(8,128)(2,1)S(1)}, bf16[64,1024]{1,0:T(8,128)(2,1)S(1)}, u32[]{:S(2)}, u32[]{:S(2)}) collective-permute-start(bf16[64,1024]{1,0:T(8,128)(2,1)S(1)} %pad_maximum_fusion.8), channel_id=1, source_target_pairs={{0,16},{1,17},{2,18},{3,19},{4,20},{5,21},{6,22},{7,23},{8,24},{9,... | collective-permute-start | bytes 393224 | tf_op jit(solution)/shard_map/ppermute | solution.py:89
  9.9 5.8 %collective-permute-done.2 = bf16[64,1024]{1,0:T(8,128)(2,1)S(1)} collective-permute-done((bf16[64,1024]{1,0:T(8,128)(2,1)S(1)}, bf16[64,1024]{1,0:T(8,128)(2,1)S(1)}, u32[]{:S(2)}, u32[]{:S(2)}) %collective-permute-start.2) | collective-permute-done | bytes 131104 | tf_op jit(solution)/shard_map/ppermute | solution.py:89
  16.5 6.9 %collective-permute-done.3 = bf16[128,1024]{1,0:T(8,128)(2,1)S(1)} collective-permute-done((bf16[128,1024]{1,0:T(8,128)(2,1)S(1)}, bf16[128,1024]{1,0:T(8,128)(2,1)S(1)}, u32[]{:S(2)}, u32[]{:S(2)}) %collective-permute-start.3) | collective-permute-done | bytes 262176 | tf_op jit(solution)/shard_map/ppermute | solution.py:89
  27.4 5.3 %collective-permute-done.4 = bf16[256,1024]{1,0:T(8,128)(2,1)S(1)} collective-permute-done((bf16[256,1024]{1,0:T(8,128)(2,1)S(1)}, bf16[256,1024]{1,0:T(8,128)(2,1)S(1)}, u32[]{:S(2)}, u32[]{:S(2)}) %collective-permute-start.4) | collective-permute-done | bytes 524320 | tf_op jit(solution)/shard_map/ppermute | solution.py:89
  37.1 11.8 %collective-permute-done.5 = bf16[512,1024]{1,0:T(8,128)(2,1)S(1)} collective-permute-done((bf16[512,1024]{1,0:T(8,128)(2,1)}, bf16[512,1024]{1,0:T(8,128)(2,1)S(1)}, u32[]{:S(2)}, u32[]{:S(2)}) %collective-permute-start.5) | collective-permute-done | bytes 1048608 | tf_op jit(solution)/shard_map/ppermute | solution.py:89
  48.9 5.7 %fusion.9 = bf16[512,1024]{1,0:T(8,128)(2,1)S(1)} fusion(f32[2,256,1024]{2,1,0:T(8,128)S(1)} %fusion.120, bf16[1024,1024]{1,0:T(8,128)(2,1)S(1)} %constant_dynamic-update-slice_fusion.5, f32[512]{0:T(512)S(1)} %add_divide_fusion.1, s32[1024]{0:T(1024)S(1)} %fusion.61, s32[512]{0:T(512)S(1)} %bitcast.115, s32[512]{0:T(512)S(1)} %bitcast.117, ...), kind=kOutput, calls=%fused_computation.13 | convolution fusion | flops 1100480512 | bytes 5281792 | tf_op jit(solution)/shard_map/dot_general | solution.py:15
  57.4 2.8 fusion.14
  61.3 3.6 %multiply_reduce_fusion.4 = (f32[1024]{0:T(1024)S(1)}, f32[512,1024]{1,0:T(8,128)S(1)}) fusion(f32[512]{0:T(512)S(1)} %bitcast.81, f32[1024]{0:T(1024)S(1)} %dynamic-slice-done, f32[512,1024]{1,0:T(8,128)S(1)} %fusion.14, bf16[512,1024]{1,0:T(8,128)(2,1)} %copy-done.7, bf16[2048,2048]{1,0:T(8,128)(2,1)} %param.12, s32[]{:T(128)S(6)} %select_n.365, ...), kind=kOutput, calls=%fused_computation.29 | convolution fusion | flops 1077935104 | bytes 7350788 | tf_op jit(solution)/shard_map/dot_general | solution.py:15
  64.9 3.9 %multiply_reduce_fusion = (f32[1024]{0:T(1024)S(1)}, f32[1024]{0:T(1024)S(1)}, f32[1024]{0:T(1024)S(1)}, f32[1024]{0:T(1024)S(1)}, f32[1024]{0:T(1024)S(1)}, /*index=5*/f32[1024]{0:T(1024)S(1)}, f32[512,1024]{1,0:T(8,128)}) fusion(f32[1024]{0:T(1024)S(1)} %broadcast_divide_fusion, f32[512]{0:T(512)S(1)} %bitcast.82, f32[512,1024]{1,0:T(8,128)S(1)} %get-tuple-element.151, ...), kind=kLoop, calls=%fused_computation.21 | loop fusion | flops 16771072 | bytes 5273601 | tf_op jit(solution)/shard_map/reduce_sum | solution.py:176
  70.8 2.6 collective-permute-done.9
  73.7 3.0 collective-permute-start.10
  84.6 2.6 broadcast_select_fusion.1
  89.0 3.4 %fusion.121 = (bf16[512,1024]{1,0:T(8,128)(2,1)S(1)}, bf16[512,1024]{1,0:T(8,128)(2,1)}) fusion(f32[512,1024]{1,0:T(8,128)S(1)} %copy-done, f32[1024]{0:T(1024)S(1)} %bitcast.86, f32[1024]{0:T(1024)S(1)} %bitcast.75, f32[1024]{0:T(1024)S(1)} %bitcast.77, f32[1024]{0:T(1024)S(1)} %bitcast.85, f32[512]{0:T(512)S(1)} %bitcast.83, ...), kind=kLoop, calls=%fused_computation.300 | loop fusion | flops 13107200 | bytes 7364609 | tf_op jit(solution)/shard_map/convert_element_type | solution.py:220
  94.6 13.1 %collective-permute-done.21 = bf16[512,512]{1,0:T(8,128)(2,1)S(1)} collective-permute-done((bf16[512,512]{1,0:T(8,128)(2,1)S(1)}, bf16[512,512]{1,0:T(8,128)(2,1)S(1)}, u32[]{:S(2)}, u32[]{:S(2)}) %collective-permute-start.21) | collective-permute-done | bytes 524320 | tf_op jit(solution)/shard_map/ppermute | solution.py:89
  110.5 18.5 %collective-permute-done.20 = bf16[512,1024]{1,0:T(8,128)(2,1)} collective-permute-done((bf16[512,1024]{1,0:T(8,128)(2,1)}, bf16[512,1024]{1,0:T(8,128)(2,1)}, u32[]{:S(2)}, u32[]{:S(2)}) %collective-permute-start.20) | collective-permute-done | bytes 1048608 | tf_op jit(solution)/shard_map/ppermute | solution.py:89
  129.0 3.1 %add_convert_fusion = bf16[1024,512]{1,0:T(8,128)(2,1)S(1)} fusion(bf16[1024,512]{1,0:T(8,128)(2,1)} %collective-permute-done.23, bf16[512,1024]{1,0:T(8,128)(2,1)} %collective-permute-done.20, bf16[512,1024]{1,0:T(8,128)(2,1)} %get-tuple-element.62, bf16[512,512]{1,0:T(8,128)(2,1)S(1)} %collective-permute-done.21, bf16[512,512]{1,0:T(8,128)(2,1)S(1)} %get-tuple-element.64), kind=kOutput, calls=%fused_computation.14 | convolution fusion | flops 1081606144 | bytes 5242880 | tf_op jit(solution)/shard_map/dot_general | solution.py:15
  134.9 12.9 %collective-permute-done.24 = bf16[512,512]{1,0:T(8,128)(2,1)S(1)} collective-permute-done((bf16[512,512]{1,0:T(8,128)(2,1)S(1)}, bf16[512,512]{1,0:T(8,128)(2,1)S(1)}, u32[]{:S(2)}, u32[]{:S(2)}) %collective-permute-start.24) | collective-permute-done | bytes 524320 | tf_op jit(solution)/shard_map/ppermute | solution.py:89
  149.1 3.6 %collective-permute-start.25 = (bf16[256,512]{1,0:T(8,128)(2,1)S(1)}, bf16[256,512]{1,0:T(8,128)(2,1)S(1)}, u32[]{:S(2)}, u32[]{:S(2)}) collective-permute-start(bf16[256,512]{1,0:T(8,128)(2,1)S(1)} %constant_dynamic-slice_fusion), channel_id=1, source_target_pairs={{0,16},{1,17},{2,18},{3,19},{4,20},{5,21},{6,22},{7,23},{8,24},{9,... | collective-permute-start | bytes 786440 | tf_op jit(solution)/shard_map/ppermute | solution.py:89
  152.6 11.9 %collective-permute-done.25 = bf16[256,512]{1,0:T(8,128)(2,1)S(1)} collective-permute-done((bf16[256,512]{1,0:T(8,128)(2,1)S(1)}, bf16[256,512]{1,0:T(8,128)(2,1)S(1)}, u32[]{:S(2)}, u32[]{:S(2)}) %collective-permute-start.25) | collective-permute-done | bytes 262176 | tf_op jit(solution)/shard_map/ppermute | solution.py:89
  164.8 14.0 %collective-permute-done.26 = bf16[256,512]{1,0:T(8,128)(2,1)S(1)} collective-permute-done((bf16[256,512]{1,0:T(8,128)(2,1)S(1)}, bf16[256,512]{1,0:T(8,128)(2,1)S(1)}, u32[]{:S(2)}, u32[]{:S(2)}) %collective-permute-start.26) | collective-permute-done | bytes 262176 | tf_op jit(solution)/shard_map/ppermute | solution.py:89
  180.9 11.9 %collective-permute-done.27 = bf16[512,512]{1,0:T(8,128)(2,1)} collective-permute-done((bf16[512,512]{1,0:T(8,128)(2,1)}, bf16[512,512]{1,0:T(8,128)(2,1)}, u32[]{:S(2)}, u32[]{:S(2)}) %collective-permute-start.27) | collective-permute-done | bytes 524320 | tf_op jit(solution)/shard_map/ppermute | solution.py:89
  195.9 4.1 %add_convert_fusion.2 = bf16[512,1024]{1,0:T(8,128)(2,1)S(1)} fusion(s32[1024]{0:T(1024)S(1)} %fusion.61, s32[512]{0:T(512)S(1)} %bitcast.116, s32[512]{0:T(512)S(1)} %bitcast.118, s32[512]{0:T(512)S(1)} %bitcast.120, s32[512]{0:T(512)S(1)} %bitcast.122, s32[512]{0:T(512)S(1)} %bitcast.124, s32[512]{0:T(512)S(1)} %bitcast.126, s32[512]{0:T(512)S(1)} %bitcast.128, ...), kind=kLoop, calls=%fused_computation.37 | loop fusion | flops 25165824 | bytes 1085440 | tf_op jit(solution)/shard_map/convert_element_type | solution.py:141
  205.4 12.2 %collective-permute-done.28 = bf16[1024,512]{1,0:T(8,128)(2,1)} collective-permute-done((bf16[1024,512]{1,0:T(8,128)(2,1)}, bf16[1024,512]{1,0:T(8,128)(2,1)}, u32[]{:S(2)}, u32[]{:S(2)}) %collective-permute-start.28) | collective-permute-done | bytes 1048608 | tf_op jit(solution)/shard_map/ppermute | solution.py:89
  217.6 2.9 pad_maximum_fusion.piece
  228.0 11.7 %collective-permute-done.16 = bf16[256,1024]{1,0:T(8,128)(2,1)S(1)} collective-permute-done((bf16[256,1024]{1,0:T(8,128)(2,1)S(1)}, bf16[256,1024]{1,0:T(8,128)(2,1)S(1)}, u32[]{:S(2)}, u32[]{:S(2)}) %collective-permute-start.16) | collective-permute-done | bytes 524320 | tf_op jit(solution)/shard_map/ppermute | solution.py:89
  240.7 11.7 %collective-permute-done.29.piece = bf16[2048,512]{1,0:T(8,128)(2,1)} collective-permute-done((bf16[2048,512]{1,0:T(8,128)(2,1)}, bf16[2048,512]{1,0:T(8,128)(2,1)}, u32[]{:S(2)}, u32[]{:S(2)}) %collective-permute-start.29) | collective-permute-done | bytes 2097184 | tf_op jit(solution)/shard_map/ppermute | solution.py:89
  253.2 8.4 %collective-permute-done.18 = bf16[64,1024]{1,0:T(8,128)(2,1)S(1)} collective-permute-done((bf16[64,1024]{1,0:T(8,128)(2,1)S(1)}, bf16[64,1024]{1,0:T(8,128)(2,1)S(1)}, u32[]{:S(2)}, u32[]{:S(2)}) %collective-permute-start.18) | collective-permute-done | bytes 131104 | tf_op jit(solution)/shard_map/ppermute | solution.py:89
  264.0 7.6 %convolution_convert_fusion = bf16[256,2048]{1,0:T(8,128)(2,1)} fusion(bf16[2048,2048]{1,0:T(8,128)(2,1)} %param.12, bf16[256,1024]{1,0:T(8,128)(2,1)} %copy-done.27, bf16[256,1024]{1,0:T(8,128)(2,1)S(1)} %get-tuple-element.66, pred[]{:T(512)S(6)} %eq.516, bf16[32,1024]{1,0:T(8,128)(2,1)S(1)} %collective-permute-done.19, ...), kind=kOutput, calls=%fused_computation | convolution fusion | flops 2188451840 | bytes 10616961 | tf_op jit(solution)/shard_map/dot_general | solution.py:15
  271.6 6.6 %place.4.total = f32[2048,2048]{1,0:T(8,128)} custom-call(s32[2]{0:T(128)} %pad_add_fusion.4.where, bf16[2048,512]{1,0:T(8,128)(2,1)} %pad_maximum_fusion.piece), custom_call_target="tpu_custom_call" | custom-call | tf_op jit(solution)/shard_map/place/pallas_call | solution.py:37
  278.3 6.6 %place.5.total = f32[2048,2048]{1,0:T(8,128)} custom-call(s32[2]{0:T(128)} %pad_add_fusion.3.where, bf16[2048,512]{1,0:T(8,128)(2,1)} %collective-permute-done.31.piece, f32[2048,2048]{1,0:T(8,128)} %place.4.total), custom_call_target="tpu_custom_call", output_to_operand_aliasing={{}: (2, {})} | custom-call | tf_op jit(solution)/shard_map/place/pallas_call | solution.py:37
  284.9 6.6 %place.6.total = f32[2048,2048]{1,0:T(8,128)} custom-call(s32[2]{0:T(128)} %pad_add_fusion.2.where, bf16[2048,512]{1,0:T(8,128)(2,1)} %collective-permute-done.29.piece, f32[2048,2048]{1,0:T(8,128)} %place.5.total), custom_call_target="tpu_custom_call", output_to_operand_aliasing={{}: (2, {})} | custom-call | tf_op jit(solution)/shard_map/place/pallas_call | solution.py:37
  291.6 6.6 %place.7 = f32[2048,2048]{1,0:T(8,128)} custom-call(s32[2]{0:T(128)} %pad_add_fusion.1.where, bf16[2048,512]{1,0:T(8,128)(2,1)} %collective-permute-done.30.piece, f32[2048,2048]{1,0:T(8,128)} %place.6.total), custom_call_target="tpu_custom_call", output_to_operand_aliasing={{}: (2, {})} | custom-call | tf_op jit(solution)/shard_map/place/pallas_call | solution.py:37
  (202 shorter events, 60.4 us)
Async XLA Ops:
  5.0 30.2 %collective-permute-start.6 = (bf16[256,1024]{1,0:T(8,128)(2,1)}, bf16[256,1024]{1,0:T(8,128)(2,1)S(1)}, u32[]{:S(2)}, u32[]{:S(2)}) collective-permute-start(bf16[256,1024]{1,0:T(8,128)(2,1)} %get-tuple-element.73), channel_id=1, source_target_pairs={{0,1},{1,0},{2,3},{3,2},{4,5},{5,4},{6,7},{7,6},{8,9},{9,8},{10,11... | collective-permute-start | bytes 1572872 | tf_op jit(solution)/shard_map/ppermute | solution.py:89
  5.1 10.6 %collective-permute-start.2 = (bf16[64,1024]{1,0:T(8,128)(2,1)S(1)}, bf16[64,1024]{1,0:T(8,128)(2,1)S(1)}, u32[]{:S(2)}, u32[]{:S(2)}) collective-permute-start(bf16[64,1024]{1,0:T(8,128)(2,1)S(1)} %pad_maximum_fusion.8), channel_id=1, source_target_pairs={{0,16},{1,17},{2,18},{3,19},{4,20},{5,21},{6,22},{7,23},{8,24},{9,... | collective-permute-start | bytes 393224 | tf_op jit(solution)/shard_map/ppermute | solution.py:89
  9.2 7.3 %collective-permute-start = (s32[256,17]{0,1:T(8,128)S(1)}, s32[256,17]{0,1:T(8,128)S(1)}, u32[]{:S(2)}, u32[]{:S(2)}) collective-permute-start(s32[256,17]{0,1:T(8,128)S(1)} %pad_add_fusion), channel_id=1, source_target_pairs={{0,1},{1,0},{2,3},{3,2},{4,5},{5,4},{6,7},{7,6},{8,9},{9,8},{10,11... | collective-permute-start | bytes 52232 | tf_op jit(solution)/shard_map/ppermute | solution.py:89
  15.7 7.8 %collective-permute-start.3 = (bf16[128,1024]{1,0:T(8,128)(2,1)S(1)}, bf16[128,1024]{1,0:T(8,128)(2,1)S(1)}, u32[]{:S(2)}, u32[]{:S(2)}) collective-permute-start(bf16[128,1024]{1,0:T(8,128)(2,1)S(1)} %pad_maximum_fusion.7), channel_id=1, source_target_pairs={{0,8},{1,9},{2,10},{3,11},{4,12},{5,13},{6,14},{7,15},{8,0},{9,1},... | collective-permute-start | bytes 786440 | tf_op jit(solution)/shard_map/ppermute | solution.py:89
  23.5 9.2 %collective-permute-start.4 = (bf16[256,1024]{1,0:T(8,128)(2,1)S(1)}, bf16[256,1024]{1,0:T(8,128)(2,1)S(1)}, u32[]{:S(2)}, u32[]{:S(2)}) collective-permute-start(bf16[256,1024]{1,0:T(8,128)(2,1)S(1)} %pad_maximum_fusion.5), channel_id=1, source_target_pairs={{0,4},{1,3},{2,6},{3,1},{4,0},{5,7},{6,2},{7,5},{8,12},{9,11},{10,... | collective-permute-start | bytes 1572872 | tf_op jit(solution)/shard_map/ppermute | solution.py:89
  33.8 15.0 %collective-permute-start.5 = (bf16[512,1024]{1,0:T(8,128)(2,1)}, bf16[512,1024]{1,0:T(8,128)(2,1)S(1)}, u32[]{:S(2)}, u32[]{:S(2)}) collective-permute-start(bf16[512,1024]{1,0:T(8,128)(2,1)} %get-tuple-element.74), channel_id=1, source_target_pairs={{0,2},{1,5},{2,0},{3,7},{4,6},{5,1},{6,4},{7,3},{8,10},{9,13},{10,... | collective-permute-start | bytes 3145736 | tf_op jit(solution)/shard_map/ppermute | solution.py:89
  54.6 5.7 %collective-permute-start.7 = (bf16[512,1024]{1,0:T(8,128)(2,1)S(1)}, bf16[512,1024]{1,0:T(8,128)(2,1)S(1)}, u32[]{:S(2)}, u32[]{:S(2)}) collective-permute-start(bf16[512,1024]{1,0:T(8,128)(2,1)S(1)} %fusion.9), channel_id=1, source_target_pairs={{0,1},{1,0},{2,3},{3,2},{4,5},{5,4},{6,7},{7,6},{8,9},{9,8},{10,11... | collective-permute-start | bytes 3145736 | tf_op jit(solution)/shard_map/ppermute | solution.py:89
  55.8 9.1 %collective-permute-start.8 = (bf16[256,1024]{1,0:T(8,128)(2,1)}, bf16[256,1024]{1,0:T(8,128)(2,1)S(1)}, u32[]{:S(2)}, u32[]{:S(2)}) collective-permute-start(bf16[256,1024]{1,0:T(8,128)(2,1)} %get-tuple-element.70), channel_id=1, source_target_pairs={{0,1},{1,0},{2,3},{3,2},{4,5},{5,4},{6,7},{7,6},{8,9},{9,8},{10,11... | collective-permute-start | bytes 1572872 | tf_op jit(solution)/shard_map/ppermute | solution.py:89
  69.5 4.0 %collective-permute-start.9 = (f32[8,1024]{1,0:T(8,128)S(1)}, f32[8,1024]{1,0:T(8,128)S(1)}, u32[]{:S(2)}, u32[]{:S(2)}) collective-permute-start(f32[8,1024]{1,0:T(8,128)S(1)} %stack.104), channel_id=1, source_target_pairs={{0,8},{1,9},{2,10},{3,11},{4,12},{5,13},{6,14},{7,15},{8,0},{9,1},... | collective-permute-start | bytes 98312 | tf_op jit(solution)/shard_map/ppermute | solution.py:89
  73.7 4.9 %collective-permute-start.10 = (f32[8,1024]{1,0:T(8,128)S(1)}, f32[8,1024]{1,0:T(8,128)S(1)}, u32[]{:S(2)}, u32[]{:S(2)}) collective-permute-start(f32[8,1024]{1,0:T(8,128)S(1)} %stack.105), channel_id=1, source_target_pairs={{0,16},{1,17},{2,18},{3,19},{4,20},{5,21},{6,22},{7,23},{8,24},{9,... | collective-permute-start | bytes 98312 | tf_op jit(solution)/shard_map/ppermute | solution.py:89
  78.7 4.1 %collective-permute-start.11 = (f32[8,1024]{1,0:T(8,128)S(1)}, f32[8,1024]{1,0:T(8,128)S(1)}, u32[]{:S(2)}, u32[]{:S(2)}) collective-permute-start(f32[8,1024]{1,0:T(8,128)S(1)} %stack.106), channel_id=1, source_target_pairs={{0,2},{1,5},{2,0},{3,7},{4,6},{5,1},{6,4},{7,3},{8,10},{9,13},{10,... | collective-permute-start | bytes 98312 | tf_op jit(solution)/shard_map/ppermute | solution.py:89
  83.0 5.7 %collective-permute-start.12 = (f32[8,1024]{1,0:T(8,128)S(1)}, f32[8,1024]{1,0:T(8,128)S(1)}, u32[]{:S(2)}, u32[]{:S(2)}) collective-permute-start(f32[8,1024]{1,0:T(8,128)S(1)} %stack.107), channel_id=1, source_target_pairs={{0,4},{1,3},{2,6},{3,1},{4,0},{5,7},{6,2},{7,5},{8,12},{9,11},{10,... | collective-permute-start | bytes 98312 | tf_op jit(solution)/shard_map/ppermute | solution.py:89
  87.2 20.4 %collective-permute-start.22 = (bf16[512,1024]{1,0:T(8,128)(2,1)S(1)}, bf16[512,1024]{1,0:T(8,128)(2,1)S(1)}, u32[]{:S(2)}, u32[]{:S(2)}) collective-permute-start(bf16[512,1024]{1,0:T(8,128)(2,1)S(1)} %get-tuple-element.63), channel_id=1, source_target_pairs={{0,2},{1,5},{2,0},{3,7},{4,6},{5,1},{6,4},{7,3},{8,10},{9,13},{10,... | collective-permute-start | bytes 3145736 | tf_op jit(solution)/shard_map/ppermute | solution.py:89
  92.5 15.2 %collective-permute-start.21 = (bf16[512,512]{1,0:T(8,128)(2,1)S(1)}, bf16[512,512]{1,0:T(8,128)(2,1)S(1)}, u32[]{:S(2)}, u32[]{:S(2)}) collective-permute-start(bf16[512,512]{1,0:T(8,128)(2,1)S(1)} %get-tuple-element.65), channel_id=1, source_target_pairs={{0,2},{1,5},{2,0},{3,7},{4,6},{5,1},{6,4},{7,3},{8,10},{9,13},{10,... | collective-permute-start | bytes 1572872 | tf_op jit(solution)/shard_map/ppermute | solution.py:89
  93.1 35.9 %collective-permute-start.20 = (bf16[512,1024]{1,0:T(8,128)(2,1)}, bf16[512,1024]{1,0:T(8,128)(2,1)}, u32[]{:S(2)}, u32[]{:S(2)}) collective-permute-start(bf16[512,1024]{1,0:T(8,128)(2,1)} %get-tuple-element.62), channel_id=1, source_target_pairs={{0,2},{1,5},{2,0},{3,7},{4,6},{5,1},{6,4},{7,3},{8,10},{9,13},{10,... | collective-permute-start | bytes 3145736 | tf_op jit(solution)/shard_map/ppermute | solution.py:89
  109.9 19.1 %collective-permute-start.23 = (bf16[1024,512]{1,0:T(8,128)(2,1)}, bf16[1024,512]{1,0:T(8,128)(2,1)}, u32[]{:S(2)}, u32[]{:S(2)}) collective-permute-start(bf16[1024,512]{1,0:T(8,128)(2,1)} %fusion.18), channel_id=1, source_target_pairs={{0,4},{1,3},{2,6},{3,1},{4,0},{5,7},{6,2},{7,5},{8,12},{9,11},{10,... | collective-permute-start | bytes 3145736 | tf_op jit(solution)/shard_map/ppermute | solution.py:89
  133.1 14.7 %collective-permute-start.24 = (bf16[512,512]{1,0:T(8,128)(2,1)S(1)}, bf16[512,512]{1,0:T(8,128)(2,1)S(1)}, u32[]{:S(2)}, u32[]{:S(2)}) collective-permute-start(bf16[512,512]{1,0:T(8,128)(2,1)S(1)} %constant_dynamic-slice_fusion.1), channel_id=1, source_target_pairs={{0,8},{1,9},{2,10},{3,11},{4,12},{5,13},{6,14},{7,15},{8,0},{9,1},... | collective-permute-start | bytes 1572872 | tf_op jit(solution)/shard_map/ppermute | solution.py:89
  149.1 15.5 %collective-permute-start.25 = (bf16[256,512]{1,0:T(8,128)(2,1)S(1)}, bf16[256,512]{1,0:T(8,128)(2,1)S(1)}, u32[]{:S(2)}, u32[]{:S(2)}) collective-permute-start(bf16[256,512]{1,0:T(8,128)(2,1)S(1)} %constant_dynamic-slice_fusion), channel_id=1, source_target_pairs={{0,16},{1,17},{2,18},{3,19},{4,20},{5,21},{6,22},{7,23},{8,24},{9,... | collective-permute-start | bytes 786440 | tf_op jit(solution)/shard_map/ppermute | solution.py:89
  164.7 14.1 %collective-permute-start.26 = (bf16[256,512]{1,0:T(8,128)(2,1)S(1)}, bf16[256,512]{1,0:T(8,128)(2,1)S(1)}, u32[]{:S(2)}, u32[]{:S(2)}) collective-permute-start(bf16[256,512]{1,0:T(8,128)(2,1)S(1)} %add_convert_fusion.5), channel_id=1, source_target_pairs={{0,16},{1,17},{2,18},{3,19},{4,20},{5,21},{6,22},{7,23},{8,24},{9,... | collective-permute-start | bytes 786440 | tf_op jit(solution)/shard_map/ppermute | solution.py:89
  180.3 12.5 %collective-permute-start.27 = (bf16[512,512]{1,0:T(8,128)(2,1)}, bf16[512,512]{1,0:T(8,128)(2,1)}, u32[]{:S(2)}, u32[]{:S(2)}) collective-permute-start(bf16[512,512]{1,0:T(8,128)(2,1)} %pad_maximum_fusion.6), channel_id=1, source_target_pairs={{0,8},{1,9},{2,10},{3,11},{4,12},{5,13},{6,14},{7,15},{8,0},{9,1},... | collective-permute-start | bytes 1572872 | tf_op jit(solution)/shard_map/ppermute | solution.py:89
  195.0 22.6 %collective-permute-start.28 = (bf16[1024,512]{1,0:T(8,128)(2,1)}, bf16[1024,512]{1,0:T(8,128)(2,1)}, u32[]{:S(2)}, u32[]{:S(2)}) collective-permute-start(bf16[1024,512]{1,0:T(8,128)(2,1)} %pad_maximum_fusion.2), channel_id=1, source_target_pairs={{0,4},{1,3},{2,6},{3,1},{4,0},{5,7},{6,2},{7,5},{8,12},{9,11},{10,... | collective-permute-start | bytes 3145736 | tf_op jit(solution)/shard_map/ppermute | solution.py:89
  202.7 19.9 %collective-permute-start.15 = (bf16[512,1024]{1,0:T(8,128)(2,1)}, bf16[512,1024]{1,0:T(8,128)(2,1)}, u32[]{:S(2)}, u32[]{:S(2)}) collective-permute-start(bf16[512,1024]{1,0:T(8,128)(2,1)} %convolution_convert_fusion.2), channel_id=1, source_target_pairs={{0,2},{1,5},{2,0},{3,7},{4,6},{5,1},{6,4},{7,3},{8,10},{9,13},{10,... | collective-permute-start | bytes 3145736 | tf_op jit(solution)/shard_map/ppermute | solution.py:89
  220.5 32.0 %collective-permute-start.29 = (bf16[2048,512]{1,0:T(8,128)(2,1)}, bf16[2048,512]{1,0:T(8,128)(2,1)}, u32[]{:S(2)}, u32[]{:S(2)}) collective-permute-start(bf16[2048,512]{1,0:T(8,128)(2,1)} %pad_maximum_fusion.piece), channel_id=1, source_target_pairs={{0,2},{1,5},{2,0},{3,7},{4,6},{5,1},{6,4},{7,3},{8,10},{9,13},{10,... | collective-permute-start | bytes 6291464 | tf_op jit(solution)/shard_map/ppermute | solution.py:89
  221.1 18.9 %collective-permute-start.32 = (f32[3,1024]{1,0:T(4,128)S(1)}, f32[3,1024]{1,0:T(4,128)S(1)}, u32[]{:S(2)}, u32[]{:S(2)}) collective-permute-start(f32[3,1024]{1,0:T(4,128)S(1)} %pad_maximum_fusion.9), channel_id=1, source_target_pairs={{0,1},{1,0},{2,3},{3,2},{4,5},{5,4},{6,7},{7,6},{8,9},{9,8},{10,11... | collective-permute-start | bytes 36872 | tf_op jit(solution)/shard_map/ppermute | solution.py:89
  224.7 14.9 %collective-permute-start.16 = (bf16[256,1024]{1,0:T(8,128)(2,1)S(1)}, bf16[256,1024]{1,0:T(8,128)(2,1)S(1)}, u32[]{:S(2)}, u32[]{:S(2)}) collective-permute-start(bf16[256,1024]{1,0:T(8,128)(2,1)S(1)} %slice.702), channel_id=1, source_target_pairs={{0,4},{1,3},{2,6},{3,1},{4,0},{5,7},{6,2},{7,5},{8,12},{9,11},{10,... | collective-permute-start | bytes 1572872 | tf_op jit(solution)/shard_map/ppermute | solution.py:89
  226.7 36.5 %collective-permute-start.14 = (bf16[256,1024]{1,0:T(8,128)(2,1)S(1)}, bf16[256,1024]{1,0:T(8,128)(2,1)S(1)}, u32[]{:S(2)}, u32[]{:S(2)}) collective-permute-start(bf16[256,1024]{1,0:T(8,128)(2,1)S(1)} %get-tuple-element.67), channel_id=1, source_target_pairs={{0,1},{1,0},{2,3},{3,2},{4,5},{5,4},{6,7},{7,6},{8,9},{9,8},{10,11... | collective-permute-start | bytes 1572872 | tf_op jit(solution)/shard_map/ppermute | solution.py:89
  239.8 12.6 %collective-permute-start.17 = (bf16[128,1024]{1,0:T(8,128)(2,1)S(1)}, bf16[128,1024]{1,0:T(8,128)(2,1)S(1)}, u32[]{:S(2)}, u32[]{:S(2)}) collective-permute-start(bf16[128,1024]{1,0:T(8,128)(2,1)S(1)} %slice.703), channel_id=1, source_target_pairs={{0,8},{1,9},{2,10},{3,11},{4,12},{5,13},{6,14},{7,15},{8,0},{9,1},... | collective-permute-start | bytes 786440 | tf_op jit(solution)/shard_map/ppermute | solution.py:89
  240.0 21.8 %collective-permute-start.13 = (bf16[256,1024]{1,0:T(8,128)(2,1)S(1)}, bf16[256,1024]{1,0:T(8,128)(2,1)S(1)}, u32[]{:S(2)}, u32[]{:S(2)}) collective-permute-start(bf16[256,1024]{1,0:T(8,128)(2,1)S(1)} %get-tuple-element.69), channel_id=1, source_target_pairs={{0,1},{1,0},{2,3},{3,2},{4,5},{5,4},{6,7},{7,6},{8,9},{9,8},{10,11... | collective-permute-start | bytes 1572872 | tf_op jit(solution)/shard_map/ppermute | solution.py:89
  240.1 38.2 %collective-permute-start.31 = (bf16[2048,512]{1,0:T(8,128)(2,1)}, bf16[2048,512]{1,0:T(8,128)(2,1)}, u32[]{:S(2)}, u32[]{:S(2)}) collective-permute-start(bf16[2048,512]{1,0:T(8,128)(2,1)} %pad_maximum_fusion.piece), channel_id=1, source_target_pairs={{0,1},{1,0},{2,3},{3,2},{4,5},{5,4},{6,7},{7,6},{8,9},{9,8},{10,11... | collective-permute-start | bytes 6291464 | tf_op jit(solution)/shard_map/ppermute | solution.py:89
  252.4 39.2 %collective-permute-start.30 = (bf16[2048,512]{1,0:T(8,128)(2,1)}, bf16[2048,512]{1,0:T(8,128)(2,1)}, u32[]{:S(2)}, u32[]{:S(2)}) collective-permute-start(bf16[2048,512]{1,0:T(8,128)(2,1)} %collective-permute-done.29.piece), channel_id=1, source_target_pairs={{0,1},{1,0},{2,3},{3,2},{4,5},{5,4},{6,7},{7,6},{8,9},{9,8},{10,11... | collective-permute-start | bytes 6291464 | tf_op jit(solution)/shard_map/ppermute | solution.py:89
  252.5 9.1 %collective-permute-start.18 = (bf16[64,1024]{1,0:T(8,128)(2,1)S(1)}, bf16[64,1024]{1,0:T(8,128)(2,1)S(1)}, u32[]{:S(2)}, u32[]{:S(2)}) collective-permute-start(bf16[64,1024]{1,0:T(8,128)(2,1)S(1)} %slice.704), channel_id=1, source_target_pairs={{0,16},{1,17},{2,18},{3,19},{4,20},{5,21},{6,22},{7,23},{8,24},{9,... | collective-permute-start | bytes 393224 | tf_op jit(solution)/shard_map/ppermute | solution.py:89
  261.7 1.5 collective-permute-start.19
  (31 other events, 277.2 us)

commit v2 on v0

v2 whole, which is shorter than its diff:
```python
import functools

import jax
import jax.numpy as jnp
from jax import lax
from jax.experimental import pallas as pl
from jax.experimental.pallas import tpu as pltpu
from jax.sharding import PartitionSpec as P

BF = jnp.bfloat16
F32 = jnp.float32
MIB = 1 << 20
HALO_WAYS = ((512, "z1 z0 s f"), (512, "z1 z0 s f"))
BACK_WAY = "s f z0 z1"
TILES = 2

FREE = pl.CostEstimate(flops=0, bytes_accessed=0, transcendentals=0)
SMALL = pl.CostEstimate(flops=0, bytes_accessed=2 * MIB, transcendentals=0)
HBM = pl.BlockSpec(memory_space=pltpu.HBM)
SMEM = pl.BlockSpec(memory_space=pltpu.SMEM)
VMEM = pl.BlockSpec(memory_space=pltpu.VMEM)
BY_ROWS = (((0,), (0,)), ((), ()))


def shape_of(shape, dtype):
    return jax.ShapeDtypeStruct(shape, dtype)


def far_shape(shape, dtype):
    return pltpu.HBM(shape, dtype)


def call(body, out_shape, name, vmem=24, cost=FREE, **rest):
    kernel = pl.pallas_call(
        body,
        out_shape=out_shape,
        compiler_params=pltpu.CompilerParams(vmem_limit_bytes=vmem * MIB),
        cost_estimate=cost,
        name=name,
        **rest,
    )
    specs = rest.get("in_specs")

    def run(*operands):
        if specs is None:
            return kernel(*operands)
        return kernel(
            *[
                pltpu.with_memory_space_constraint(x, pltpu.HBM) if spec is HBM else x
                for x, spec in zip(operands, specs)
            ]
        )

    return run


def scalars(*x):
    return jnp.stack([jnp.int32(v) for v in x])


def mxu(a, b):
    return jnp.dot(a, b, preferred_element_type=F32)


def by_rows(a, b):
    return lax.dot_general(a, b, BY_ROWS, preferred_element_type=F32)


def copy_all(copies):
    for c in copies:
        c.start()
    for c in copies:
        c.wait()


def outgoing_kernel(where, rows, features, away, *keep):
    nodes, width = features.shape
    half = width // 2
    hot = (rows[...] == lax.broadcasted_iota(jnp.int32, (rows.shape[0], nodes), 1)).astype(BF)
    there = features[:, pl.ds(pl.multiple_of((1 - where[0]) * half, half), half)]
    away[...] = mxu(hot, there).astype(BF)
    here = mxu(hot, features[:, pl.ds(pl.multiple_of(where[0] * half, half), half)]).astype(BF)
    at = 0
    for out in keep:
        out[...] = here[:, at : at + out.shape[1]]
        at += out.shape[1]


def outgoing_rows(core, rows, features, widths):
    sends, half = rows.shape[0], features.shape[1] // 2
    return call(
        outgoing_kernel,
        tuple(shape_of((sends, w), BF) for w in (half,) + widths),
        "outgoing",
        in_specs=[SMEM, VMEM, VMEM],
    )(scalars(core), rows, features)


def stack_kernel(n, received, *refs):
    own, outs = refs[:n], refs[n:]
    at = 0
    for x, out in zip(own, outs):
        rows, w = x.shape
        out[:rows, :] = x[...]
        out[rows:, :] = received[:, at : at + w]
        at += w


def stack(own, received):
    return call(
        functools.partial(stack_kernel, len(own)),
        tuple(shape_of((2 * x.shape[0], x.shape[1]), BF) for x in own),
        "stack",
    )(received, *own)


def interleave_kernel(outer, own, received, out):
    step = own.shape[0] // outer
    for a in range(outer):
        out[2 * a * step : (2 * a + 1) * step, :] = own[a * step : (a + 1) * step, :]
        out[(2 * a + 1) * step : (2 * a + 2) * step, :] = received[a * step : (a + 1) * step, :]


def interleave(own, received, outer):
    rows, w = own.shape
    return call(
        functools.partial(interleave_kernel, outer), shape_of((2 * rows, w), own.dtype), "interleave"
    )(own, received)


def counts_kernel(packed, label, halo_count, own_count, factors):
    nodes, columns = packed.shape
    slots = columns - 1

    def count(labels):
        total = jnp.zeros((nodes, labels.shape[1]), F32)
        for e in range(slots):
            total = total + jnp.where(packed[:, e : e + 1] == labels, 1.0, 0.0)
        return total

    halo_count[...] = count(label[...]).astype(BF)
    local = lax.broadcasted_iota(jnp.int32, (nodes, nodes), 1)
    row = lax.broadcasted_iota(jnp.int32, (nodes, nodes), 0)
    own_count[...] = (count(local) + jnp.where(row == local, 2.0, 0.0)).astype(BF)
    degree = jnp.zeros((nodes, 1), F32)
    for e in range(slots):
        degree = degree + jnp.where(packed[:, e : e + 1] >= 0, 1.0, 0.0)
    lane = lax.broadcasted_iota(jnp.int32, factors.shape, 1)
    factors[...] = jnp.where(lane == 0, packed[:, slots:].astype(F32), 1.0 / (degree + 1.0))


def counts(packed, label):
    nodes = packed.shape[0]
    return call(
        counts_kernel,
        (
            shape_of((nodes, label.shape[1]), BF),
            shape_of((nodes, nodes), BF),
            shape_of((nodes, 128), F32),
        ),
        "counts",
    )(packed, label)


def split_kernel(where, features, cotangent, feature_out, cotangent_out, sem):
    half = features.shape[1] // 2
    away = pl.ds(pl.multiple_of((1 - where[0]) * half, half), half)
    copy_all(
        [
            pltpu.make_async_copy(features.at[:, away], feature_out, sem.at[0]),
            pltpu.make_async_copy(cotangent.at[:, away], cotangent_out, sem.at[1]),
        ]
    )


def split(core, features, cotangent):
    rows, width = features.shape
    out = shape_of((rows, width // 2), BF)
    return call(
        split_kernel,
        (out, out),
        "split",
        in_specs=[SMEM, HBM, HBM],
        out_specs=(VMEM, VMEM),
        scratch_shapes=[pltpu.SemaphoreType.DMA((2,))],
    )(scalars(core), features, cotangent)


def aggregate_kernel(n, where, features, feature_in, *refs):
    own, sibling, halos = refs[:3], refs[3:6], refs[6 : 6 + n]
    first, second, near_own, sem = refs[6 + n :]
    nodes, half = near_own.shape
    core = where[0]
    here = pl.ds(pl.multiple_of(core * half, half), half)
    copy = pltpu.make_async_copy(features.at[:, here], near_own, sem)
    copy.start()

    def means(side, table):
        halo_count, own_count, factors = side
        start = 0
        parts = []
        for halo in halos:
            part = slice(start, start + halo.shape[1])
            total = mxu(halo_count[...], halo[...]) + mxu(own_count[...], table[:, part])
            parts.append((part, (total * factors[:, 1:2]).astype(BF)))
            start += halo.shape[1]
        return parts

    for k, (side, table) in enumerate(((sibling, feature_in), (own, near_own))):
        if k == 1:
            copy.wait()
        parts = means(side, table)
        for part, value in parts:
            for flag, out in ((k == 1, first), (k == 0, second)):

                @pl.when((core == 0) == flag)
                def _():
                    out[:, part] = value


def aggregate(core, features, feature_in, own, sibling, halos):
    rows, half = feature_in.shape
    out = shape_of((rows, half), BF)
    return call(
        functools.partial(aggregate_kernel, len(halos)),
        (out, out),
        "aggregate",
        in_specs=[SMEM, HBM] + [VMEM] * (7 + len(halos)),
        scratch_shapes=[pltpu.VMEM((rows, half), BF), pltpu.SemaphoreType.DMA],
    )(scalars(core), features, feature_in, *own, *sibling, *halos)


def grad_loads(core, cotangent, cotangent_in, near_g, column, sems):
    rows, half = cotangent_in.shape
    start, size = column
    whole = pl.ds(pl.multiple_of(core * half + start, 256), size)
    part = pl.ds(pl.multiple_of(start, 256), size)
    own = pl.ds(pl.multiple_of(core * rows, rows), rows)
    far = pl.ds(pl.multiple_of((1 - core) * rows, rows), rows)
    return [
        pltpu.make_async_copy(cotangent.at[:, whole], near_g.at[own, part], sems.at[0]),
        pltpu.make_async_copy(cotangent_in.at[:, part], near_g.at[far, part], sems.at[1]),
    ]


def forward_kernel(
    where, first_mine, second_mine, first_other, second_other, bias, own_factors, other_factors,
    weight, cotangent, cotangent_in,
    z_out, stats_ref, near_mine, near_other, near_g, z_ref, sem, out_sem,
):
    core = where[0]
    block = 256
    half = z_ref.shape[1]
    nodes = first_mine.shape[0]
    own = pl.ds(pl.multiple_of(core * half, half), half)
    far = pl.ds(pl.multiple_of((1 - core) * half, half), half)

    def loads(k, start, size):
        whole = pl.ds(pl.multiple_of(core * half + start, 256), size)
        part = slice(start, start + size)
        return [
            pltpu.make_async_copy(weight.at[own, whole], near_mine.at[:, part], sem.at[0, k]),
            pltpu.make_async_copy(weight.at[far, whole], near_other.at[:, part], sem.at[1, k]),
        ]

    ranges = ((0, block), (block, half - block))
    copies = [loads(k, *r) for k, r in enumerate(ranges)]
    grads = grad_loads(core, cotangent, cotangent_in, near_g, (0, half), sem.at[2])
    for c in copies[0] + grads + copies[1]:
        c.start()

    def store(j):
        part = slice(2 * j * block, 2 * (j + 1) * block)
        return pltpu.make_async_copy(z_ref.at[:, part], z_out.at[:, part], out_sem.at[j])

    valids = [
        jnp.where(core == k, own_factors[:, 0:1], other_factors[:, 0:1]) for k in range(2)
    ]
    valid = jnp.concatenate(valids, 0)
    for j in range(half // block):
        at = slice(j * block, (j + 1) * block)
        if j < 2:
            for c in copies[j]:
                c.wait()
        for k, (a, b) in enumerate(((first_mine, first_other), (second_mine, second_other))):
            z = mxu(a[...], near_mine[:, at]) + mxu(b[...], near_other[:, at])
            z_ref[k * nodes : (k + 1) * nodes, at] = z + bias[:, at]
        if j == 0:
            for c in grads:
                c.wait()
        if j % 2 == 1:
            store(j // 2).start()
        z = z_ref[:, at]
        sigma = 1.0 / (1.0 + jnp.exp(-z))
        y = z * sigma
        slope = (sigma + y * (1.0 - sigma)) * valid
        g = near_g[:, at].astype(F32) * valid

        def column(x):
            return jnp.sum(x, axis=0, keepdims=True)

        count = jnp.broadcast_to(column(valid), (1, block))
        y_sum = column(y * valid)
        centred = (y - y_sum / jnp.maximum(count, 1.0)) * valid
        stats_ref[0:1, at] = count
        stats_ref[1:2, at] = y_sum
        stats_ref[2:3, at] = column(centred * centred)
        stats_ref[3:4, at] = column(g)
        stats_ref[4:5, at] = column(g * centred)
        stats_ref[5:6, at] = column(slope * g)
        stats_ref[6:7, at] = column(slope)
        stats_ref[7:8, at] = column(slope * centred)
    for j in range(half // block // 2):
        store(j).wait()


def forward(core, mine, other, weight, bias, cotangent, cotangent_in, own, sibling):
    rows, half = cotangent_in.shape
    return call(
        forward_kernel,
        (far_shape((2 * rows, half), F32), shape_of((8, half), F32)),
        "forward",
        in_specs=[SMEM] + [VMEM] * 7 + [HBM] * 3,
        out_specs=(HBM, VMEM),
        scratch_shapes=[
            pltpu.VMEM((half, half), BF),
            pltpu.VMEM((half, half), BF),
            pltpu.VMEM((2 * rows, half), BF),
            pltpu.VMEM((2 * rows, half), F32),
            pltpu.SemaphoreType.DMA((3, 2)),
            pltpu.SemaphoreType.DMA((half // 512,)),
        ],
    )(
        scalars(core), *mine, *other, bias[None, :], own, sibling, weight, cotangent, cotangent_in
    )


def merge_kernel(where, own, received, out):
    upper = where[0] == 1
    a, b = own[...], received[...]
    a, b = jnp.where(upper, b, a), jnp.where(upper, a, b)

    def row(x, k):
        return x[k : k + 1, :]

    na, nb = row(a, 0), row(b, 0)
    n = na + nb
    mean = (row(a, 1) + row(b, 1)) / jnp.maximum(n, 1.0)
    da = row(a, 1) / jnp.maximum(na, 1.0) - mean
    db = row(b, 1) / jnp.maximum(nb, 1.0) - mean
    out[...] = a + b
    out[2:3, :] = (row(a, 2) + na * da * da) + (row(b, 2) + nb * db * db)
    out[4:5, :] = (row(a, 4) + da * row(a, 3)) + (row(b, 4) + db * row(b, 3))
    out[7:8, :] = (row(a, 7) + da * row(a, 6)) + (row(b, 7) + db * row(b, 6))


def merge(own, received, v):
    return call(
        merge_kernel, shape_of(own.shape, F32), "merge", in_specs=[SMEM, VMEM, VMEM]
    )(scalars(v), own, received)


def backward_kernel(
    where, stats_ref, gamma_ref, beta_ref, own_factors, other_factors, z_ref, cotangent, cotangent_in,
    dz_send, dz_keep, dz_scaled, act_first, act_second, vectors, near_z, near_g, sem,
):
    first, core = where[0], where[1]
    rows, half = z_ref.shape
    block = 256
    some = half // block // 2
    nodes = act_first.shape[0]

    def loads(i):
        start = (1 - first if i == 0 else first) * some * block
        part = pl.ds(pl.multiple_of(start, some * block), some * block)
        copy = pltpu.make_async_copy(z_ref.at[:, part], near_z.at[:, part], sem.at[i, 2])
        return [copy] + grad_loads(
            core, cotangent, cotangent_in, near_g, (start, some * block), sem.at[i]
        )

    copies = [loads(i) for i in range(2)]
    for c in copies[0] + copies[1]:
        c.start()
    valids, inverses = (
        jnp.concatenate(
            [
                jnp.where(core == k, own_factors[:, lane : lane + 1], other_factors[:, lane : lane + 1])
                for k in range(2)
            ],
            0,
        )
        for lane in range(2)
    )

    def columns(i, k, out):
        base = ((1 - first if i == 0 else first) * some + k) * block
        at = pl.ds(pl.multiple_of(base, block), block)
        vector = pl.ds(pl.multiple_of(core * half + base, block), block)
        z = near_z[:, at]
        valid = valids
        stats = stats_ref[:, at]
        gamma, beta = gamma_ref[:, vector], beta_ref[:, vector]
        n = stats[0:1, :]
        mean = stats[1:2, :] / n
        deviation = lax.rsqrt(stats[2:3, :] / n + 1e-05)
        shift = stats[3:4, :]
        scale = deviation * stats[4:5, :]
        gain = gamma * deviation
        vectors[0:1, at] = gain * (
            stats[5:6, :] - shift / n * stats[6:7, :] - deviation * scale / n * stats[7:8, :]
        )
        vectors[1:2, at] = scale
        vectors[2:3, at] = shift
        vectors[3:8, at] = jnp.zeros((5, block), F32)
        sigma = 1.0 / (1.0 + jnp.exp(-z))
        y = z * sigma
        slope = (sigma + y * (1.0 - sigma)) * valid
        g = near_g[:, at].astype(F32) * valid
        normalized = (y - mean) * deviation
        act = (valid * (gamma * normalized + beta)).astype(BF)
        act_first[:, at] = act[:nodes]
        act_second[:, at] = act[nodes:]
        dz = gain * (g - shift / n - normalized * (scale / n)) * slope
        dz_scaled[:, at] = (dz * inverses).astype(BF)
        out[:, k * block : (k + 1) * block] = dz.astype(BF)

    for i, out in enumerate((dz_send, dz_keep)):
        for c in copies[i]:
            c.wait()
        for k in range(some):
            columns(i, k, out)


def backward(core, first, z, stats, gamma, beta, cotangent, cotangent_in, own, sibling):
    rows, half = z.shape
    return call(
        backward_kernel,
        (
            shape_of((rows, half // 2), BF),
            shape_of((rows, half // 2), BF),
            shape_of((rows, half), BF),
            shape_of((rows // 2, half), BF),
            shape_of((rows // 2, half), BF),
            shape_of((8, half), F32),
        ),
        "backward",
        in_specs=[SMEM] + [VMEM] * 5 + [HBM] * 3,
        scratch_shapes=[
            pltpu.VMEM((rows, half), F32),
            pltpu.VMEM((rows, half), BF),
            pltpu.SemaphoreType.DMA((2, 3)),
        ],
    )(
        scalars(first, core), stats, gamma[None, :], beta[None, :], own, sibling, z, cotangent, cotangent_in
    )


def weight_part_kernel(t, where, *refs):
    aggs, (dz, dz_pair, out, near, sem) = refs[:8], refs[8:]
    nodes = aggs[0].shape[0]
    columns = slice(t * out.shape[0], (t + 1) * out.shape[0])

    def copy(k, pair):
        return pltpu.make_async_copy(aggs[2 * pair + k % 2 + 4 * (k // 2)].at[:, columns], near.at[k], sem.at[k])

    for flag, pair in ((1, 0), (0, 1)):

        @pl.when(where[0] == flag)
        def _():
            for k in range(4):
                copy(k, pair).start()

    total = 0.0
    for k in range(4):
        copy(k, 0).wait()
        rows = slice(k % 2 * nodes, (k % 2 + 1) * nodes)
        total = total + by_rows(near[k], (dz, dz_pair)[k // 2][rows, :])
    out[...] = total.astype(BF)


def weight_part(flag, aggs, dz, dz_pair, t):
    nodes, half = aggs[0].shape
    tall = half // TILES
    return call(
        functools.partial(weight_part_kernel, t),
        shape_of((tall, dz.shape[1]), BF),
        "weight_part",
        in_specs=[SMEM] + [HBM] * 8 + [VMEM] * 2,
        scratch_shapes=[pltpu.VMEM((4, nodes, tall), BF), pltpu.SemaphoreType.DMA((4,))],
    )(scalars(flag), *aggs, dz, dz_pair)


def fold_kernel(where, own, received, away, keep):
    rows = keep.shape[0]
    for side, out in ((1 - where[0], away), (where[0], keep)):
        part = pl.ds(pl.multiple_of(side * rows, rows), rows)
        out[...] = (own[part, :].astype(F32) + received[part, :].astype(F32)).astype(BF)


def fold(own, received, v):
    rows, w = own.shape
    out = shape_of((rows // 2, w), BF)
    return call(fold_kernel, (out, out), "fold", in_specs=[SMEM, VMEM, VMEM])(
        scalars(v), own, received
    )


def total_kernel(own, received, out):
    out[...] = (own[...].astype(F32) + received[...].astype(F32)).astype(BF)


def total_of(own, received):
    return call(total_kernel, shape_of(own.shape, BF), "total")(own, received)


def join_kernel(where, own, received, out):
    rows = own.shape[0]
    for side, x in ((where[0], own), (1 - where[0], received)):
        out[pl.ds(pl.multiple_of(side * rows, rows), rows), :] = x[...]


def join(own, received, v):
    rows, w = own.shape
    return call(join_kernel, shape_of((2 * rows, w), BF), "join", in_specs=[SMEM, VMEM, VMEM])(
        scalars(v), own, received
    )


def place_kernel(n, where, *refs):
    pieces, (out, wide, put) = refs[:n], refs[-3:]

    def write(i):
        rows, w = pieces[i].shape
        row = pl.multiple_of(where[2 * i], 256)
        column = pl.multiple_of(where[2 * i + 1], 128)
        return pltpu.make_async_copy(
            wide.at[i], out.at[pl.ds(row, rows), pl.ds(column, w)], put.at[i]
        )

    for i in range(n):
        step = 128

        @pl.loop(0, pieces[i].shape[0] // step)
        def _(k):
            part = pl.ds(pl.multiple_of(k * step, step), step)
            wide[i, part, :] = pieces[i][part, :].astype(F32)

        write(i).start()
    for i in range(n):
        write(i).wait()


def place(total, pieces, shape, cost=FREE):
    n = len(pieces)
    rows, w = pieces[0][0].shape
    operands = [scalars(*[x for p in pieces for x in p[1:]])] + [p[0] for p in pieces]
    specs = [SMEM] + [VMEM] * n
    aliases = {}
    if total is not None:
        aliases = {len(operands): 0}
        operands.append(total)
        specs.append(HBM)
    return call(
        functools.partial(place_kernel, n),
        far_shape(shape, F32),
        "place",
        in_specs=specs,
        out_specs=HBM,
        cost=cost,
        scratch_shapes=[pltpu.VMEM((n, rows, w), F32), pltpu.SemaphoreType.DMA((n,))],
        input_output_aliases=aliases,
    )(*operands)


def back_part_kernel(columns, where, own, sibling, dz, out):
    nodes = own.shape[0]
    total = 0.0
    for side, count in ((where[0], own), (1 - where[0], sibling)):
        rows = pl.ds(pl.multiple_of(side * nodes, nodes), nodes)
        total = total + by_rows(count[:, columns], dz[rows, :])
    out[...] = total.astype(BF)


def back_part(core, own, sibling, dz, k, parts):
    rows = own.shape[1] // parts
    return call(
        functools.partial(back_part_kernel, slice(k * rows, (k + 1) * rows)),
        shape_of((rows, dz.shape[1]), BF),
        "back_part",
        in_specs=[SMEM] + [VMEM] * 3,
    )(scalars(core), own, sibling, dz)


def halve_kernel(own, received, away, keep):
    rows = keep.shape[0]
    keep[...] = (own[:rows].astype(F32) + received[:rows].astype(F32)).astype(BF)
    away[...] = (own[rows:].astype(F32) + received[rows:].astype(F32)).astype(BF)


def halve(own, received):
    rows, w = own.shape
    out = shape_of((rows // 2, w), BF)
    return call(halve_kernel, (out, out), "halve")(own, received)


def own_back_body(where, own, sibling, dz, act_first, act_second, keep, away, act_keep, act_away):
    nodes = keep.shape[0]
    core = where[0]
    for side, count, out in ((core, own, keep), (1 - core, sibling, away)):
        part = pl.ds(pl.multiple_of(side * nodes, nodes), nodes)
        out[...] = by_rows(count[...], dz[part, :]).astype(BF)
    act_keep[...] = jnp.where(core == 0, act_first[...], act_second[...])
    act_away[...] = jnp.where(core == 0, act_second[...], act_first[...])


def own_back(core, own, sibling, dz, act_first, act_second):
    nodes, half = act_first.shape
    out, far = shape_of((nodes, half), BF), shape_of((nodes, half), BF)
    return call(own_back_body, (far, out, far, out), "own_back", in_specs=[SMEM] + [VMEM] * 5)(
        scalars(core), own, sibling, dz, act_first, act_second
    )


def finish_kernel(
    where, rows, back, back_in, vec, vec_in, own, own_in, act, act_in, weight,
    grad, activations, vectors, near_weight, near_own, table, weight_sem, own_sem, act_sem,
):
    core = where[0]
    nodes, half = own.shape
    sends = rows.shape[0]
    block = 256
    blocks = weight.shape[0] // block

    def side_of(k):
        return pl.ds(pl.multiple_of((core if k == 0 else 1 - core) * half, half), half)

    owns = [
        pltpu.make_async_copy(x, near_own.at[k], own_sem.at[k]) for k, x in enumerate((own, own_in))
    ]
    acts = [
        pltpu.make_async_copy(x, activations.at[:, side_of(k)], act_sem.at[k])
        for k, x in enumerate((act, act_in))
    ]
    weights = [
        pltpu.make_async_copy(
            weight.at[k * block : (k + 1) * block, :],
            near_weight.at[k * block : (k + 1) * block, :],
            weight_sem.at[k],
        )
        for k in range(blocks)
    ]
    for c in owns + weights + acts:
        c.start()
    hot = (rows[...] == lax.broadcasted_iota(jnp.int32, (sends, nodes), 1)).astype(BF)
    for k, (back_part, vector) in enumerate(((back[:sends], vec), (back_in[...], vec_in))):
        vectors[:, side_of(k)] = vector[...]
        owns[k].wait()
        part = near_own[k].astype(F32) + by_rows(hot, back_part)
        table[:, side_of(k)] = part.astype(BF)
    for k in range(blocks):
        weights[k].wait()
        part = slice(k * block, (k + 1) * block)
        grad[:, part] = lax.dot_general(
            table[...], near_weight[part, :], (((1,), (1,)), ((), ())), preferred_element_type=F32
        ).astype(BF)
    for c in acts:
        c.wait()


def finish(core, rows, back, back_in, own, own_in, act, act_in, vec, vec_in, weight):
    nodes, half = own.shape
    width = 2 * half
    return call(
        finish_kernel,
        (
            shape_of((nodes, width), BF),
            shape_of((nodes, width), BF),
            shape_of((8, width), F32),
        ),
        "finish",
        in_specs=[SMEM] + [VMEM] * 5 + [HBM] * 5,
        out_specs=(VMEM, VMEM, VMEM),
        scratch_shapes=[
            pltpu.VMEM(weight.shape, BF),
            pltpu.VMEM((2, nodes, half), BF),
            pltpu.VMEM((nodes, width), BF),
            pltpu.SemaphoreType.DMA((width // 256,)),
            pltpu.SemaphoreType.DMA((2,)),
            pltpu.SemaphoreType.DMA((2,)),
        ],
    )(scalars(core), rows, back, back_in, vec, vec_in, own, own_in, act, act_in, weight)


def on_device(
    size,
    features,
    weight,
    bias,
    gamma,
    beta,
    neighbours,
    edge_mask,
    node_mask,
    send_rows,
    send_mask,
    cotangent,
):
    nodes, width = features.shape
    sends = send_rows.shape[0]
    half = width // 2
    quarter = width // 4
    rest = list(range(3, size.bit_length() - 1))
    levels = len(rest)
    cut = (levels + 1) // 2
    ways = {"f": ["f"], "s": ["s"], "z0": rest[:cut], "z1": rest[cut:]}

    me = lax.axis_index("dom")
    core = me & 1
    is0 = core == 0
    b1, b2 = (me >> 1) & 1, (me >> 2) & 1
    first = jnp.where(is0, b1, b2)
    second = jnp.where(is0, b2, b1)
    first_weight = jnp.where(is0, 2, 4)
    second_weight = 6 - first_weight

    def bit(b):
        return first if b == "f" else second if b == "s" else (me >> b) & 1

    def weight_of(b):
        return first_weight if b == "f" else second_weight if b == "s" else 1 << b

    def peer(i, b):
        if b == "f":
            return i ^ (4 if i & 1 else 2)
        if b == "s":
            return i ^ (2 if i & 1 else 4)
        return i ^ (1 << b)

    def along(x, b):
        return lax.ppermute(x, "dom", [(i, peer(i, b)) for i in range(size)])

    def swap(x):
        return lax.ppermute(x, "dom", [(i, i ^ 1) for i in range(size)])

    token = [jnp.zeros((8, 128), F32)]

    def arrive(*x):
        *x, token[0] = lax.optimization_barrier((*x, token[0]))
        return x[0] if len(x) == 1 else x

    def start(generators):
        running = dict(generators)
        for k in running:
            next(running[k])
        done = {}

        def advance(k):
            try:
                next(running[k])
            except StopIteration as stop:
                done[k] = stop.value

        return advance, done

    def bits_of(way):
        return [b for name in way.split() for b in ways[name]]

    live_row = jnp.where(send_mask > 0, send_rows, -1)[:, None]
    out_away, *out_keep = outgoing_rows(
        core, live_row, features, tuple(w for w, _ in HALO_WAYS)
    )
    outgoing = stack(out_keep, arrive(swap(out_away)))
    axes = bits_of(BACK_WAY)
    halo_rows = sends * size
    chip_rows = 2 * sends

    def gather_halo(x, way):
        got = []
        for b in bits_of(way):
            received = along(x, b)
            yield
            outer = 1 << len([g for g in got if axes.index(g) < axes.index(b)])
            x = interleave(x, arrive(received), outer)
            got.append(b)
        return x

    generators = {
        k: gather_halo(x, way) for k, (x, (_, way)) in enumerate(zip(outgoing, HALO_WAYS))
    }
    advance, halo = start(generators)

    def hop():
        for k in generators:
            advance(k)

    live_neighbour = jnp.where(edge_mask > 0, neighbours, -1)
    packed = jnp.concatenate([live_neighbour, node_mask[:, None]], 1)
    place_of = jnp.arange(halo_rows)
    chip, row = place_of // chip_rows, place_of % chip_rows
    relative = 0
    for k, b in enumerate(axes):
        relative = relative + ((chip >> (len(axes) - 1 - k)) & 1) * weight_of(b)
    owner = (me ^ relative) ^ (row // sends)
    label = (nodes + owner * sends + row % sends)[None, :]
    packed, label = arrive(packed, label)
    sibling_packed = arrive(swap(packed))
    hop()
    feature_out, cotangent_out = arrive(*split(core, *arrive(features, cotangent)))
    feature_in, cotangent_in = swap(feature_out), swap(cotangent_out)
    packed = arrive(packed)
    own = arrive(*counts(packed, label))
    hop()
    feature_in, cotangent_in, sibling_packed = arrive(feature_in, cotangent_in, sibling_packed)
    sibling = arrive(*counts(sibling_packed, label))
    hop()
    for _ in range(levels - 1):
        hop()

    agg_mine = aggregate(
        core, features, feature_in, own, sibling, [halo[k] for k in generators]
    )
    agg_other = [swap(x) for x in agg_mine]
    mine_pair = [along(x, "f") for x in agg_mine]
    agg_other = [arrive(x) for x in agg_other]
    other_pair = [along(x, "f") for x in agg_other]
    own_bias = lax.dynamic_slice_in_dim(bias, core * half, half, 0)
    z, stats = forward(
        core, agg_mine, agg_other, weight, own_bias, cotangent, cotangent_in, own[2], sibling[2]
    )

    same = (second == core).astype(jnp.int32)
    for k, b in enumerate(bits_of("z1 z0 s f")):
        received = along(stats, b)
        if k == 0:
            mine_pair = [arrive(x) for x in mine_pair]
        if b == "s":
            other_pair = [arrive(x) for x in other_pair]
        stats = merge(stats, arrive(received), bit(b))
    dz_send, dz_keep, dz_scaled, act_first, act_second, vectors = backward(
        core, first, z, stats, gamma, beta, cotangent, cotangent_in, own[2], sibling[2]
    )

    dz_pair = along(dz_send, "f")
    dz_keep, dz_scaled = arrive(dz_keep, dz_scaled)
    aggs = [*agg_mine, *agg_other, *mine_pair, *other_pair]
    dz_pair = arrive(dz_pair)

    def weight_gradient(t):
        received = along(weight_part(1 - same, aggs, dz_keep, dz_pair, t), "s")
        part = weight_part(same, aggs, dz_keep, dz_pair, t)
        yield
        part = arrive(part)
        if t == 0:
            yield
        received = arrive(received)
        for b in rest:
            out, part = fold(part, received, bit(b))
            received = along(out, b)
            yield
            received = arrive(received)
        part = total_of(part, received)
        for b in reversed(rest):
            received = along(part, b)
            yield
            part = join(part, arrive(received), bit(b))
        return part

    def reduce_halo():
        received, part = along(back_send, axes[0]), back_keep
        for b in axes[1:]:
            yield
            out, part = halve(part, arrive(received))
            received = along(out, b)
        yield
        return total_of(part, arrive(received))

    advance, weight_parts = start({t: weight_gradient(t) for t in range(TILES)})

    def step():
        for t in range(TILES):
            advance(t)

    for t in range(TILES):
        advance(t)
    back_send, back_keep = (
        back_part(core, own[0], sibling[0], dz_scaled, k, 2) for k in (1, 0)
    )
    kept_back, away_back, act, act_away = own_back(
        core, own[1], sibling[1], dz_scaled, act_first, act_second
    )
    back_send, back_keep, kept_back, away_back, act, act_away = arrive(
        back_send, back_keep, kept_back, away_back, act, act_away
    )
    own_in, act_in, vectors_in = swap(away_back), swap(act_away), swap(vectors)
    advance(0)
    back_send = arrive(back_send)
    advance_halo, halo_part = start({"h": reduce_halo()})
    own_in, act_in, vectors_in = arrive(own_in, act_in, vectors_in)
    for k in range(levels):
        step()
        if k < 2:
            advance_halo("h")
    for k in range(levels):
        step()
    for _ in ways["z0"]:
        advance_halo("h")

    tall = half // TILES
    tiles = range(TILES)
    part = [weight_parts[t] for t in tiles]
    across = [along(x, "s") for x in part]
    pair = [along(x, "f") for x in part]
    here = [swap(x) for x in part]
    here_at, there_at = core * half, (1 - core) * half
    shape = (width, width)

    def pieces(own, sibling, row, sibling_row, column, sibling_column):
        return [(x, row * half + t * tall, here_at + column * quarter) for t, x in own.items()] + [
            (x, sibling_row * half + t * tall, there_at + sibling_column * quarter)
            for t, x in sibling.items()
        ]

    def numbered(x):
        return dict(enumerate(x))

    pair_across, here_across, here_pair = [], [], []
    for t in tiles:
        across[t] = arrive(across[t])
        pair_across.append(along(across[t], "f"))
        here_across.append(swap(across[t]))
        pair[t] = arrive(pair[t])
        here_pair.append(swap(pair[t]))
        if t == 0:
            here = [arrive(x) for x in here]
            total = place(
                None, pieces(numbered(part), numbered(here), second, first, first, second), shape, SMALL
            )
            total = arrive(total)
    while "h" not in halo_part:
        advance_halo("h")
    back = halo_part["h"]
    back_in = arrive(swap(back[sends:]))
    grad_features, activations, vectors = finish(
        core, live_row, back, back_in, kept_back, own_in, act, act_in, vectors, vectors_in, weight
    )
    grad_features, activations, vectors = arrive(grad_features, activations, vectors)
    here_across = [arrive(x) for x in here_across]
    here_pair = [arrive(x) for x in here_pair]
    total = place(
        total,
        pieces(numbered(across), numbered(here_across), 1 - second, 1 - first, first, second)
        + pieces(numbered(pair), numbered(here_pair), second, first, 1 - first, 1 - second),
        shape,
    )
    total = arrive(total)
    for t in tiles:
        pair_across[t] = arrive(pair_across[t])
        here_pair_across = swap(pair_across[t])
        total = place(
            total,
            pieces(
                {t: pair_across[t]},
                {t: here_pair_across},
                1 - second,
                1 - first,
                1 - first,
                1 - second,
            ),
            shape,
            SMALL,
        )
        if t == 0:
            total = arrive(total)
            vectors = vectors + token[0][0, 0]
    return activations, grad_features, total, vectors[0], vectors[1], vectors[2]


def solution(mesh):
    size = mesh.shape["dom"]
    return jax.shard_map(
        functools.partial(on_device, size),
        mesh=mesh,
        in_specs=(
            P("dom", None),
            P(),
            P(),
            P(),
            P(),
            P("dom", None),
            P("dom", None),
            P("dom"),
            P("dom"),
            P("dom"),
            P("dom", None),
        ),
        out_specs=(P("dom", None), P("dom", None), P(), P(), P(), P()),
        check_vma=False,
    )
```

time: 791 us -> 229 us (0.29)
  waiting for transfers between devices: 428 us -> 97.6 us
  blocking collectives: 163 us -> 0 us
  other arithmetic: 97.8 us -> 3.02 us
  Pallas kernels: 0 us -> 59.4 us
  starting transfers between devices: 0.12 us -> 54.8 us
  local copies, waits for them, and re-layouts: 57.6 us -> 12.1 us
  matrix products: 29.2 us -> 0 us
  between operations: 14 us -> 1.43 us
    psum x1 -> x0, waiting for transfers between devices: 273 us -> none  [on_device(): grad_weight, grad_bias = lax.psum((weight_part, bias_part), 'dom')]
    psum x4 -> x0, blocking collectives: 163 us -> none  [the longest x1 42.7 us: on_device(): grad_weight, grad_bias = lax.psum((weight_part, bias_part), 'dom')]
    ppermute x0 -> x55, waiting for transfers between devices: none -> 97.6 us  [the longest x37 94.1 us: along(): return lax.ppermute(x, 'dom', [(i, peer(i, b)) for i in range(size)])]
    reduce_scatter x1 -> x0, waiting for transfers between devices: 93.4 us -> none  [on_device(): lax.psum_scatter(halo_part, 'dom', scatter_dimension=0, tiled=True)]
    all_gather x1 -> x0, waiting for transfers between devices: 61.6 us -> none  [on_device(): halo = lax.all_gather(outgoing, 'dom', axis=0, tiled=True)]
    scatter-add x2 -> x0, other arithmetic: 61 us -> none  [the longest x1 56.6 us: on_device(): jnp.zeros((table.shape[0], width), jnp.float32).at[neighbours.reshape(-1)]]
    pallas_call x0 -> x46, Pallas kernels: none -> 59.4 us  [the longest x29 52.8 us: run(): kernel(*[pltpu.with_memory_space_constraint(x, pltpu.HBM) if spec is HBM...]
    ppermute x0 -> x55, starting transfers between devices: none -> 54.8 us  [the longest x37 50.2 us: along(): return lax.ppermute(x, 'dom', [(i, peer(i, b)) for i in range(size)])]
  transfers between devices with their start and end apart: 3 -> 55, of which waited for: 3 -> 30; matrix products, arithmetic and copies ran while one was open for 3% -> 2% of each run, Pallas kernels for 0% -> 20%
where the time goes in v2:
time: 229 us; the launch traced here: 228 us
  waiting for transfers between devices  97.6 us (43%)
  Pallas kernels  59.4 us (26%)
  starting transfers between devices  54.8 us (24%)
  local copies, waits for them, and re-layouts  12.1 us (5%)
  other arithmetic  3.02 us (1%)
    ppermute x37, waiting for transfers between devices, along(): return lax.ppermute(x, 'dom', [(i, peer(i, b)) for i in range(size)])  94.1 us
    pallas_call x29, Pallas kernels, run(): kernel(*[pltpu.with_memory_space_constraint(x, pltpu.HBM) if spec is HBM...  52.8 us
    ppermute x37, starting transfers between devices, along(): return lax.ppermute(x, 'dom', [(i, peer(i, b)) for i in range(size)])  50.2 us
    unnamed x58, local copies, waits for them, and re-layouts  10.4 us
    pallas_call x17, Pallas kernels, run(): return kernel(*operands)  6.61 us
  transfers between devices with their start and end apart: 55, of which 30 were waited for; matrix products, arithmetic and copies ran while one was open for 2% of the time, Pallas kernels for 20%

profile of v2, /device:TPU:0, one launch (start us, length us, event | category | flops | bytes accessed | tf_op | source)
XLA Modules:
  0.0 228.3 jit_solution(15624688541971008206)
XLA Ops:
  4.9 3.7 %collective-permute-start.2 = (bf16[64,512]{1,0:T(8,128)(2,1)S(1)}, bf16[64,512]{1,0:T(8,128)(2,1)S(1)}, u32[]{:S(2)}, u32[]{:S(2)}) collective-permute-start(bf16[64,512]{1,0:T(8,128)(2,1)S(1)} %get-tuple-element.205.own), channel_id=1, source_target_pairs={{0,16},{1,17},{2,18},{3,19},{4,20},{5,21},{6,22},{7,23},{8,24},{9,... | collective-permute-start | bytes 196616 | tf_op jit(solution)/shard_map/ppermute | solution.py:740
  10.2 2.7 %collective-permute-done.2.received = bf16[64,512]{1,0:T(8,128)(2,1)S(1)} collective-permute-done((bf16[64,512]{1,0:T(8,128)(2,1)S(1)}, bf16[64,512]{1,0:T(8,128)(2,1)S(1)}, u32[]{:S(2)}, u32[]{:S(2)}) %collective-permute-start.2) | collective-permute-done | bytes 65568 | tf_op jit(solution)/shard_map/ppermute | solution.py:740
  12.9 2.6 %collective-permute-done.1.received = bf16[64,512]{1,0:T(8,128)(2,1)S(1)} collective-permute-done((bf16[64,512]{1,0:T(8,128)(2,1)S(1)}, bf16[64,512]{1,0:T(8,128)(2,1)S(1)}, u32[]{:S(2)}, u32[]{:S(2)}) %collective-permute-start.1) | collective-permute-done | bytes 65568 | tf_op jit(solution)/shard_map/ppermute | solution.py:740
  19.6 2.6 %counts.2 = (bf16[256,1024]{1,0:T(8,128)(2,1)S(1)}, bf16[256,256]{1,0:T(8,128)(2,1)S(1)}, f32[256,128]{1,0:T(8,128)S(1)}) custom-call(s32[256,17]{1,0:T(8,128)S(1)} %copy.33.packed, s32[1,1024]{1,0:T(1,128)S(1)} %fusion.label), custom_call_target="tpu_custom_call" | custom-call | tf_op jit(solution)/shard_map/counts/pallas_call | solution.py:46
  27.3 2.6 %counts.3 = (bf16[256,1024]{1,0:T(8,128)(2,1)S(1)}, bf16[256,256]{1,0:T(8,128)(2,1)S(1)}, f32[256,128]{1,0:T(8,128)S(1)}) custom-call(s32[256,17]{1,0:T(8,128)S(1)} %collective-permute-done.3.packed, s32[1,1024]{1,0:T(1,128)S(1)} %fusion.label), custom_call_target="tpu_custom_call" | custom-call | tf_op jit(solution)/shard_map/counts/pallas_call | solution.py:46
  31.9 2.5 %collective-permute-done.10.received = bf16[256,512]{1,0:T(8,128)(2,1)S(1)} collective-permute-done((bf16[256,512]{1,0:T(8,128)(2,1)S(1)}, bf16[256,512]{1,0:T(8,128)(2,1)S(1)}, u32[]{:S(2)}, u32[]{:S(2)}) %collective-permute-start.10) | collective-permute-done | bytes 262176 | tf_op jit(solution)/shard_map/ppermute | solution.py:740
  34.4 2.7 %collective-permute-start.11 = (bf16[512,512]{1,0:T(8,128)(2,1)S(1)}, bf16[512,512]{1,0:T(8,128)(2,1)S(1)}, u32[]{:S(2)}, u32[]{:S(2)}) collective-permute-start(bf16[512,512]{1,0:T(8,128)(2,1)S(1)} %interleave.14.own), channel_id=1, source_target_pairs={{0,2},{1,5},{2,0},{3,7},{4,6},{5,1},{6,4},{7,3},{8,10},{9,13},{10,... | collective-permute-start | bytes 1572872 | tf_op jit(solution)/shard_map/ppermute | solution.py:740
  39.5 5.6 %collective-permute-done.11.received = bf16[512,512]{1,0:T(8,128)(2,1)S(1)} collective-permute-done((bf16[512,512]{1,0:T(8,128)(2,1)S(1)}, bf16[512,512]{1,0:T(8,128)(2,1)S(1)}, u32[]{:S(2)}, u32[]{:S(2)}) %collective-permute-start.11) | collective-permute-done | bytes 524320 | tf_op jit(solution)/shard_map/ppermute | solution.py:740
  52.2 6.5 %forward.1 = (f32[512,1024]{1,0:T(8,128)}, f32[8,1024]{1,0:T(8,128)S(1)}) custom-call(s32[1]{0:T(128)} %bitcast.where, bf16[256,1024]{1,0:T(8,128)(2,1)S(1)} %get-tuple-element.252.first_mine.refs_0_, bf16[256,1024]{1,0:T(8,128)(2,1)S(1)} %get-tuple-element.253.second_mine.refs_1_, bf16[256,1024]{1,0:T(8,128)(2,1)S(1)} %collective-permute-done.12.first_other.refs_2_, ...), custom_call_target="tpu_custom_call" | custom-call | tf_op jit(solution)/shard_map/forward/pallas_call | solution.py:47
  64.9 2.7 %collective-permute-done.17.received = f32[8,1024]{1,0:T(8,128)S(1)} collective-permute-done((f32[8,1024]{1,0:T(8,128)S(1)}, f32[8,1024]{1,0:T(8,128)S(1)}, u32[]{:S(2)}, u32[]{:S(2)}) %collective-permute-start.17) | collective-permute-done | bytes 32800 | tf_op jit(solution)/shard_map/ppermute | solution.py:740
  69.3 5.2 %collective-permute-done.19.refs_7_ = bf16[256,1024]{1,0:T(8,128)(2,1)} collective-permute-done((bf16[256,1024]{1,0:T(8,128)(2,1)S(1)}, bf16[256,1024]{1,0:T(8,128)(2,1)}, u32[]{:S(2)}, u32[]{:S(2)}) %collective-permute-start.19) | collective-permute-done | bytes 524320 | tf_op jit(solution)/shard_map/ppermute | solution.py:740
  80.0 4.1 %backward.1 = (bf16[512,512]{1,0:T(8,128)(2,1)}, bf16[512,512]{1,0:T(8,128)(2,1)S(1)}, bf16[512,1024]{1,0:T(8,128)(2,1)S(1)}, bf16[256,1024]{1,0:T(8,128)(2,1)S(...) custom-call(s32[2]{0:T(128)S(1)} %pad_add_fusion.1.where, f32[8,1024]{1,0:T(8,128)S(1)} %merge.7.stats_ref, ...), custom_call_target="tpu_custom_call" | custom-call | tf_op jit(solution)/shard_map/backward/pallas_call | solution.py:47
  88.7 7.9 %collective-permute-done.22.refs_9_ = bf16[512,512]{1,0:T(8,128)(2,1)} collective-permute-done((bf16[512,512]{1,0:T(8,128)(2,1)}, bf16[512,512]{1,0:T(8,128)(2,1)}, u32[]{:S(2)}, u32[]{:S(2)}) %collective-permute-start.22) | collective-permute-done | bytes 524320 | tf_op jit(solution)/shard_map/ppermute | solution.py:740
  97.7 3.1 %weight_part.4 = bf16[512,512]{1,0:T(8,128)(2,1)S(1)} custom-call(s32[1]{0:T(128)} %bitcast.10.where, bf16[256,1024]{1,0:T(8,128)(2,1)} %copy-done, bf16[256,1024]{1,0:T(8,128)(2,1)} %copy-done.1, bf16[256,1024]{1,0:T(8,128)(2,1)} %copy-done.2, bf16[256,1024]{1,0:T(8,128)(2,1)} %copy-done.3, bf16[256,1024]{1,0:T(8,128)(2,1)} %copy-done.25, ...), custom_call_target="tpu_custom_call" | custom-call | tf_op jit(solution)/shard_map/weight_part/pallas_call | solution.py:47
  102.5 3.0 %weight_part.7 = bf16[512,512]{1,0:T(8,128)(2,1)S(1)} custom-call(s32[1]{0:T(128)} %bitcast.10.where, bf16[256,1024]{1,0:T(8,128)(2,1)} %copy-done, bf16[256,1024]{1,0:T(8,128)(2,1)} %copy-done.1, bf16[256,1024]{1,0:T(8,128)(2,1)} %copy-done.2, bf16[256,1024]{1,0:T(8,128)(2,1)} %copy-done.3, bf16[256,1024]{1,0:T(8,128)(2,1)} %copy-done.25, ...), custom_call_target="tpu_custom_call" | custom-call | tf_op jit(solution)/shard_map/weight_part/pallas_call | solution.py:47
  111.8 3.2 %weight_part.6.own = bf16[512,512]{1,0:T(8,128)(2,1)S(1)} custom-call(s32[1]{0:T(128)} %bitcast.11.where, bf16[256,1024]{1,0:T(8,128)(2,1)} %copy-done, bf16[256,1024]{1,0:T(8,128)(2,1)} %copy-done.1, bf16[256,1024]{1,0:T(8,128)(2,1)} %copy-done.2, bf16[256,1024]{1,0:T(8,128)(2,1)} %copy-done.3, bf16[256,1024]{1,0:T(8,128)(2,1)} %copy-done.25, ...), custom_call_target="tpu_custom_call" | custom-call | tf_op jit(solution)/shard_map/weight_part/pallas_call | solution.py:47
  115.1 3.0 %weight_part.5.own = bf16[512,512]{1,0:T(8,128)(2,1)S(1)} custom-call(s32[1]{0:T(128)} %bitcast.11.where, bf16[256,1024]{1,0:T(8,128)(2,1)} %copy-done, bf16[256,1024]{1,0:T(8,128)(2,1)} %copy-done.1, bf16[256,1024]{1,0:T(8,128)(2,1)} %copy-done.2, bf16[256,1024]{1,0:T(8,128)(2,1)} %copy-done.3, bf16[256,1024]{1,0:T(8,128)(2,1)} %copy-done.25, ...), custom_call_target="tpu_custom_call" | custom-call | tf_op jit(solution)/shard_map/weight_part/pallas_call | solution.py:47
  123.1 6.4 %collective-permute-done.27.received = bf16[256,512]{1,0:T(8,128)(2,1)S(1)} collective-permute-done((bf16[256,512]{1,0:T(8,128)(2,1)S(1)}, bf16[256,512]{1,0:T(8,128)(2,1)S(1)}, u32[]{:S(2)}, u32[]{:S(2)}) %collective-permute-start.27) | collective-permute-done | bytes 262176 | tf_op jit(solution)/shard_map/ppermute | solution.py:740
  129.5 5.2 %collective-permute-done.26.received = bf16[256,512]{1,0:T(8,128)(2,1)S(1)} collective-permute-done((bf16[256,512]{1,0:T(8,128)(2,1)S(1)}, bf16[256,512]{1,0:T(8,128)(2,1)S(1)}, u32[]{:S(2)}, u32[]{:S(2)}) %collective-permute-start.26) | collective-permute-done | bytes 262176 | tf_op jit(solution)/shard_map/ppermute | solution.py:740
  139.8 8.5 %collective-permute-done.33.received = bf16[128,512]{1,0:T(8,128)(2,1)S(1)} collective-permute-done((bf16[128,512]{1,0:T(8,128)(2,1)S(1)}, bf16[128,512]{1,0:T(8,128)(2,1)S(1)}, u32[]{:S(2)}, u32[]{:S(2)}) %collective-permute-start.33) | collective-permute-done | bytes 131104 | tf_op jit(solution)/shard_map/ppermute | solution.py:740
  148.4 2.7 %collective-permute-done.32.received = bf16[128,512]{1,0:T(8,128)(2,1)S(1)} collective-permute-done((bf16[128,512]{1,0:T(8,128)(2,1)S(1)}, bf16[128,512]{1,0:T(8,128)(2,1)S(1)}, u32[]{:S(2)}, u32[]{:S(2)}) %collective-permute-start.32) | collective-permute-done | bytes 131104 | tf_op jit(solution)/shard_map/ppermute | solution.py:740
  151.1 6.0 %collective-permute-done.36.received = bf16[128,512]{1,0:T(8,128)(2,1)S(1)} collective-permute-done((bf16[128,512]{1,0:T(8,128)(2,1)S(1)}, bf16[128,512]{1,0:T(8,128)(2,1)S(1)}, u32[]{:S(2)}, u32[]{:S(2)}) %collective-permute-start.36) | collective-permute-done | bytes 131104 | tf_op jit(solution)/shard_map/ppermute | solution.py:740
  157.2 2.5 %collective-permute-start.35 = (bf16[128,512]{1,0:T(8,128)(2,1)S(1)}, bf16[128,512]{1,0:T(8,128)(2,1)S(1)}, u32[]{:S(2)}, u32[]{:S(2)}) collective-permute-start(bf16[128,512]{1,0:T(8,128)(2,1)S(1)} %total.3.own), channel_id=1, source_target_pairs={{0,16},{1,17},{2,18},{3,19},{4,20},{5,21},{6,22},{7,23},{8,24},{9,... | collective-permute-start | bytes 393224 | tf_op jit(solution)/shard_map/ppermute | solution.py:740
  159.7 4.7 %collective-permute-done.35.received = bf16[128,512]{1,0:T(8,128)(2,1)S(1)} collective-permute-done((bf16[128,512]{1,0:T(8,128)(2,1)S(1)}, bf16[128,512]{1,0:T(8,128)(2,1)S(1)}, u32[]{:S(2)}, u32[]{:S(2)}) %collective-permute-start.35) | collective-permute-done | bytes 131104 | tf_op jit(solution)/shard_map/ppermute | solution.py:740
  167.1 3.4 %collective-permute-start.37 = (bf16[256,512]{1,0:T(8,128)(2,1)S(1)}, bf16[256,512]{1,0:T(8,128)(2,1)S(1)}, u32[]{:S(2)}, u32[]{:S(2)}) collective-permute-start(bf16[256,512]{1,0:T(8,128)(2,1)S(1)} %join.4.own), channel_id=1, source_target_pairs={{0,8},{1,9},{2,10},{3,11},{4,12},{5,13},{6,14},{7,15},{8,0},{9,1},... | collective-permute-start | bytes 786440 | tf_op jit(solution)/shard_map/ppermute | solution.py:740
  172.4 5.4 %collective-permute-done.37.received = bf16[256,512]{1,0:T(8,128)(2,1)S(1)} collective-permute-done((bf16[256,512]{1,0:T(8,128)(2,1)S(1)}, bf16[256,512]{1,0:T(8,128)(2,1)S(1)}, u32[]{:S(2)}, u32[]{:S(2)}) %collective-permute-start.37) | collective-permute-done | bytes 262176 | tf_op jit(solution)/shard_map/ppermute | solution.py:740
  177.9 3.9 %collective-permute-done.34.received = bf16[128,1024]{1,0:T(8,128)(2,1)S(1)} collective-permute-done((bf16[128,1024]{1,0:T(8,128)(2,1)S(1)}, bf16[128,1024]{1,0:T(8,128)(2,1)S(1)}, u32[]{:S(2)}, u32[]{:S(2)}) %collective-permute-start.34) | collective-permute-done | bytes 262176 | tf_op jit(solution)/shard_map/ppermute | solution.py:740
  186.1 3.3 %place.4.refs_8_ = f32[2048,2048]{1,0:T(8,128)} custom-call(s32[8]{0:T(128)S(1)} %stack.126.where, bf16[512,512]{1,0:T(8,128)(2,1)S(1)} %join.7.refs_0_, bf16[512,512]{1,0:T(8,128)(2,1)S(1)} %join.6.refs_1_, bf16[512,512]{1,0:T(8,128)(2,1)} %collective-permute-done.42.refs_2_, bf16[512,512]{1,0:T(8,128)(2,1)} %collective-permute-done.45.refs_3_), custom_call_target="tpu_custom_call" | custom-call | bytes 2097152 | tf_op jit(solution)/shard_map/place/pallas_call | solution.py:47
  189.5 6.2 %collective-permute-done.41.refs_1_ = bf16[512,512]{1,0:T(8,128)(2,1)S(1)} collective-permute-done((bf16[512,512]{1,0:T(8,128)(2,1)S(1)}, bf16[512,512]{1,0:T(8,128)(2,1)S(1)}, u32[]{:S(2)}, u32[]{:S(2)}) %collective-permute-start.41) | collective-permute-done | bytes 524320 | tf_op jit(solution)/shard_map/ppermute | solution.py:740
  198.1 11.0 %finish.1 = (bf16[256,2048]{1,0:T(8,128)(2,1)}, bf16[256,2048]{1,0:T(8,128)(2,1)}, f32[8,2048]{1,0:T(8,128)S(1)}) custom-call(s32[1]{0:T(128)} %bitcast.where, s32[32,1]{1,0:T(8,128)S(1)} %copy.34.rows, bf16[64,1024]{1,0:T(8,128)(2,1)S(1)} %total.5.back, bf16[32,1024]{1,0:T(8,128)(2,1)S(1)} %collective-permute-done.46.back_in, f32[8,1024]{1,0:T(8,128)S(1)} %copy-done.22, ...), custom_call_target="tpu_custom_call" | custom-call | tf_op jit(solution)/shard_map/finish/pallas_call | solution.py:47
  209.1 5.0 %place.5.refs_2_ = f32[2048,2048]{1,0:T(8,128)} custom-call(s32[16]{0:T(128)S(1)} %stack.135.where, bf16[512,512]{1,0:T(8,128)(2,1)S(1)} %collective-permute-done.44.refs_0_, bf16[512,512]{1,0:T(8,128)(2,1)S(1)} %collective-permute-done.41.refs_1_, bf16[512,512]{1,0:T(8,128)(2,1)} %collective-permute-done.49.refs_2_, ...), custom_call_target="tpu_custom_call", output_to_operand_aliasing={{}: (9, {})} | custom-call | tf_op jit(solution)/shard_map/place/pallas_call | solution.py:47
  219.0 5.2 %collective-permute-done.47.refs_0_ = bf16[512,512]{1,0:T(8,128)(2,1)S(1)} collective-permute-done((bf16[512,512]{1,0:T(8,128)(2,1)S(1)}, bf16[512,512]{1,0:T(8,128)(2,1)S(1)}, u32[]{:S(2)}, u32[]{:S(2)}) %collective-permute-start.47) | collective-permute-done | bytes 524320 | tf_op jit(solution)/shard_map/ppermute | solution.py:740
  (200 shorter events, 83.7 us)
Async XLA Ops:
  16.7 10.6 %collective-permute-start.4 = (bf16[256,1024]{1,0:T(8,128)(2,1)S(1)}, bf16[256,1024]{1,0:T(8,128)(2,1)S(1)}, u32[]{:S(2)}, u32[]{:S(2)}) collective-permute-start(bf16[256,1024]{1,0:T(8,128)(2,1)S(1)} %get-tuple-element.223), channel_id=1, source_target_pairs={{0,1},{1,0},{2,3},{3,2},{4,5},{5,4},{6,7},{7,6},{8,9},{9,8},{10,11... | collective-permute-start | bytes 1572872 | tf_op jit(solution)/shard_map/ppermute | solution.py:743
  16.8 10.5 %collective-permute-start.5 = (bf16[256,1024]{1,0:T(8,128)(2,1)S(1)}, bf16[256,1024]{1,0:T(8,128)(2,1)}, u32[]{:S(2)}, u32[]{:S(2)}) collective-permute-start(bf16[256,1024]{1,0:T(8,128)(2,1)S(1)} %get-tuple-element.224), channel_id=1, source_target_pairs={{0,1},{1,0},{2,3},{3,2},{4,5},{5,4},{6,7},{7,6},{8,9},{9,8},{10,11... | collective-permute-start | bytes 1572872 | tf_op jit(solution)/shard_map/ppermute | solution.py:743
  30.2 9.2 %collective-permute-start.9 = (bf16[512,512]{1,0:T(8,128)(2,1)S(1)}, bf16[512,512]{1,0:T(8,128)(2,1)S(1)}, u32[]{:S(2)}, u32[]{:S(2)}) collective-permute-start(bf16[512,512]{1,0:T(8,128)(2,1)S(1)} %interleave.11.own), channel_id=1, source_target_pairs={{0,2},{1,5},{2,0},{3,7},{4,6},{5,1},{6,4},{7,3},{8,10},{9,13},{10,... | collective-permute-start | bytes 1572872 | tf_op jit(solution)/shard_map/ppermute | solution.py:740
  34.4 10.7 %collective-permute-start.11 = (bf16[512,512]{1,0:T(8,128)(2,1)S(1)}, bf16[512,512]{1,0:T(8,128)(2,1)S(1)}, u32[]{:S(2)}, u32[]{:S(2)}) collective-permute-start(bf16[512,512]{1,0:T(8,128)(2,1)S(1)} %interleave.14.own), channel_id=1, source_target_pairs={{0,2},{1,5},{2,0},{3,7},{4,6},{5,1},{6,4},{7,3},{8,10},{9,13},{10,... | collective-permute-start | bytes 1572872 | tf_op jit(solution)/shard_map/ppermute | solution.py:740
  48.0 12.8 %collective-permute-start.16 = (bf16[256,1024]{1,0:T(8,128)(2,1)S(1)}, bf16[256,1024]{1,0:T(8,128)(2,1)S(1)}, u32[]{:S(2)}, u32[]{:S(2)}) collective-permute-start(bf16[256,1024]{1,0:T(8,128)(2,1)S(1)} %get-tuple-element.252.first_mine.refs_0_), channel_id=1, source_target_pairs={{0,2},{1,5},{2,0},{3,7},{4,6},{5,1},{6,4},{7,3},{8,10},{9,13},{10,... | collective-permute-start | bytes 1572872 | tf_op jit(solution)/shard_map/ppermute | solution.py:740
  49.6 13.4 %collective-permute-start.15 = (bf16[256,1024]{1,0:T(8,128)(2,1)S(1)}, bf16[256,1024]{1,0:T(8,128)(2,1)}, u32[]{:S(2)}, u32[]{:S(2)}) collective-permute-start(bf16[256,1024]{1,0:T(8,128)(2,1)S(1)} %get-tuple-element.253.second_mine.refs_1_), channel_id=1, source_target_pairs={{0,2},{1,5},{2,0},{3,7},{4,6},{5,1},{6,4},{7,3},{8,10},{9,13},{10,... | collective-permute-start | bytes 1572872 | tf_op jit(solution)/shard_map/ppermute | solution.py:740
  50.1 19.3 %collective-permute-start.20 = (bf16[256,1024]{1,0:T(8,128)(2,1)S(1)}, bf16[256,1024]{1,0:T(8,128)(2,1)}, u32[]{:S(2)}, u32[]{:S(2)}) collective-permute-start(bf16[256,1024]{1,0:T(8,128)(2,1)S(1)} %collective-permute-done.12.first_other.refs_2_), channel_id=1, source_target_pairs={{0,2},{1,5},{2,0},{3,7},{4,6},{5,1},{6,4},{7,3},{8,10},{9,13},{10,... | collective-permute-start | bytes 1572872 | tf_op jit(solution)/shard_map/ppermute | solution.py:740
  51.6 22.9 %collective-permute-start.19 = (bf16[256,1024]{1,0:T(8,128)(2,1)S(1)}, bf16[256,1024]{1,0:T(8,128)(2,1)}, u32[]{:S(2)}, u32[]{:S(2)}) collective-permute-start(bf16[256,1024]{1,0:T(8,128)(2,1)S(1)} %collective-permute-done.13.second_other.refs_3_), channel_id=1, source_target_pairs={{0,2},{1,5},{2,0},{3,7},{4,6},{5,1},{6,4},{7,3},{8,10},{9,13},{10,... | collective-permute-start | bytes 1572872 | tf_op jit(solution)/shard_map/ppermute | solution.py:740
  87.1 9.5 %collective-permute-start.22 = (bf16[512,512]{1,0:T(8,128)(2,1)}, bf16[512,512]{1,0:T(8,128)(2,1)}, u32[]{:S(2)}, u32[]{:S(2)}) collective-permute-start(bf16[512,512]{1,0:T(8,128)(2,1)} %get-tuple-element.288), channel_id=1, source_target_pairs={{0,2},{1,5},{2,0},{3,7},{4,6},{5,1},{6,4},{7,3},{8,10},{9,13},{10,... | collective-permute-start | bytes 1572872 | tf_op jit(solution)/shard_map/ppermute | solution.py:740
  100.8 17.2 %collective-permute-start.23 = (bf16[512,512]{1,0:T(8,128)(2,1)S(1)}, bf16[512,512]{1,0:T(8,128)(2,1)S(1)}, u32[]{:S(2)}, u32[]{:S(2)}) collective-permute-start(bf16[512,512]{1,0:T(8,128)(2,1)S(1)} %weight_part.4), channel_id=1, source_target_pairs={{0,4},{1,3},{2,6},{3,1},{4,0},{5,7},{6,2},{7,5},{8,12},{9,11},{10,... | collective-permute-start | bytes 1572872 | tf_op jit(solution)/shard_map/ppermute | solution.py:740
  105.5 12.6 %collective-permute-start.24 = (bf16[512,512]{1,0:T(8,128)(2,1)S(1)}, bf16[512,512]{1,0:T(8,128)(2,1)S(1)}, u32[]{:S(2)}, u32[]{:S(2)}) collective-permute-start(bf16[512,512]{1,0:T(8,128)(2,1)S(1)} %weight_part.7), channel_id=1, source_target_pairs={{0,4},{1,3},{2,6},{3,1},{4,0},{5,7},{6,2},{7,5},{8,12},{9,11},{10,... | collective-permute-start | bytes 1572872 | tf_op jit(solution)/shard_map/ppermute | solution.py:740
  118.1 16.7 %collective-permute-start.25 = (bf16[512,1024]{1,0:T(8,128)(2,1)S(1)}, bf16[512,1024]{1,0:T(8,128)(2,1)S(1)}, u32[]{:S(2)}, u32[]{:S(2)}) collective-permute-start(bf16[512,1024]{1,0:T(8,128)(2,1)S(1)} %back_part.2), channel_id=1, source_target_pairs={{0,4},{1,3},{2,6},{3,1},{4,0},{5,7},{6,2},{7,5},{8,12},{9,11},{10,... | collective-permute-start | bytes 3145736 | tf_op jit(solution)/shard_map/ppermute | solution.py:740
  120.3 9.2 %collective-permute-start.27 = (bf16[256,512]{1,0:T(8,128)(2,1)S(1)}, bf16[256,512]{1,0:T(8,128)(2,1)S(1)}, u32[]{:S(2)}, u32[]{:S(2)}) collective-permute-start(bf16[256,512]{1,0:T(8,128)(2,1)S(1)} %get-tuple-element.305), channel_id=1, source_target_pairs={{0,8},{1,9},{2,10},{3,11},{4,12},{5,13},{6,14},{7,15},{8,0},{9,1},... | collective-permute-start | bytes 786440 | tf_op jit(solution)/shard_map/ppermute | solution.py:740
  122.4 12.3 %collective-permute-start.26 = (bf16[256,512]{1,0:T(8,128)(2,1)S(1)}, bf16[256,512]{1,0:T(8,128)(2,1)S(1)}, u32[]{:S(2)}, u32[]{:S(2)}) collective-permute-start(bf16[256,512]{1,0:T(8,128)(2,1)S(1)} %get-tuple-element.302), channel_id=1, source_target_pairs={{0,8},{1,9},{2,10},{3,11},{4,12},{5,13},{6,14},{7,15},{8,0},{9,1},... | collective-permute-start | bytes 786440 | tf_op jit(solution)/shard_map/ppermute | solution.py:740
  135.0 16.1 %collective-permute-start.31 = (bf16[256,1024]{1,0:T(8,128)(2,1)S(1)}, bf16[256,1024]{1,0:T(8,128)(2,1)S(1)}, u32[]{:S(2)}, u32[]{:S(2)}) collective-permute-start(bf16[256,1024]{1,0:T(8,128)(2,1)S(1)} %get-tuple-element.315), channel_id=1, source_target_pairs={{0,2},{1,5},{2,0},{3,7},{4,6},{5,1},{6,4},{7,3},{8,10},{9,13},{10,... | collective-permute-start | bytes 1572872 | tf_op jit(solution)/shard_map/ppermute | solution.py:740
  136.6 11.6 %collective-permute-start.33 = (bf16[128,512]{1,0:T(8,128)(2,1)S(1)}, bf16[128,512]{1,0:T(8,128)(2,1)S(1)}, u32[]{:S(2)}, u32[]{:S(2)}) collective-permute-start(bf16[128,512]{1,0:T(8,128)(2,1)S(1)} %get-tuple-element.321), channel_id=1, source_target_pairs={{0,16},{1,17},{2,18},{3,19},{4,20},{5,21},{6,22},{7,23},{8,24},{9,... | collective-permute-start | bytes 393224 | tf_op jit(solution)/shard_map/ppermute | solution.py:740
  139.1 12.0 %collective-permute-start.32 = (bf16[128,512]{1,0:T(8,128)(2,1)S(1)}, bf16[128,512]{1,0:T(8,128)(2,1)S(1)}, u32[]{:S(2)}, u32[]{:S(2)}) collective-permute-start(bf16[128,512]{1,0:T(8,128)(2,1)S(1)} %get-tuple-element.318), channel_id=1, source_target_pairs={{0,16},{1,17},{2,18},{3,19},{4,20},{5,21},{6,22},{7,23},{8,24},{9,... | collective-permute-start | bytes 393224 | tf_op jit(solution)/shard_map/ppermute | solution.py:740
  148.3 8.8 %collective-permute-start.36 = (bf16[128,512]{1,0:T(8,128)(2,1)S(1)}, bf16[128,512]{1,0:T(8,128)(2,1)S(1)}, u32[]{:S(2)}, u32[]{:S(2)}) collective-permute-start(bf16[128,512]{1,0:T(8,128)(2,1)S(1)} %total.4.own), channel_id=1, source_target_pairs={{0,16},{1,17},{2,18},{3,19},{4,20},{5,21},{6,22},{7,23},{8,24},{9,... | collective-permute-start | bytes 393224 | tf_op jit(solution)/shard_map/ppermute | solution.py:740
  165.5 17.9 %collective-permute-start.44 = (bf16[512,512]{1,0:T(8,128)(2,1)S(1)}, bf16[512,512]{1,0:T(8,128)(2,1)S(1)}, u32[]{:S(2)}, u32[]{:S(2)}) collective-permute-start(bf16[512,512]{1,0:T(8,128)(2,1)S(1)} %join.7.refs_0_), channel_id=1, source_target_pairs={{0,4},{1,3},{2,6},{3,1},{4,0},{5,7},{6,2},{7,5},{8,12},{9,11},{10,... | collective-permute-start | bytes 1572872 | tf_op jit(solution)/shard_map/ppermute | solution.py:740
  167.1 10.7 %collective-permute-start.37 = (bf16[256,512]{1,0:T(8,128)(2,1)S(1)}, bf16[256,512]{1,0:T(8,128)(2,1)S(1)}, u32[]{:S(2)}, u32[]{:S(2)}) collective-permute-start(bf16[256,512]{1,0:T(8,128)(2,1)S(1)} %join.4.own), channel_id=1, source_target_pairs={{0,8},{1,9},{2,10},{3,11},{4,12},{5,13},{6,14},{7,15},{8,0},{9,1},... | collective-permute-start | bytes 786440 | tf_op jit(solution)/shard_map/ppermute | solution.py:740
  170.7 11.2 %collective-permute-start.34 = (bf16[128,1024]{1,0:T(8,128)(2,1)S(1)}, bf16[128,1024]{1,0:T(8,128)(2,1)S(1)}, u32[]{:S(2)}, u32[]{:S(2)}) collective-permute-start(bf16[128,1024]{1,0:T(8,128)(2,1)S(1)} %get-tuple-element.327), channel_id=1, source_target_pairs={{0,8},{1,9},{2,10},{3,11},{4,12},{5,13},{6,14},{7,15},{8,0},{9,1},... | collective-permute-start | bytes 786440 | tf_op jit(solution)/shard_map/ppermute | solution.py:740
  170.8 13.8 %collective-permute-start.43 = (bf16[512,512]{1,0:T(8,128)(2,1)S(1)}, bf16[512,512]{1,0:T(8,128)(2,1)S(1)}, u32[]{:S(2)}, u32[]{:S(2)}) collective-permute-start(bf16[512,512]{1,0:T(8,128)(2,1)S(1)} %join.7.refs_0_), channel_id=1, source_target_pairs={{0,2},{1,5},{2,0},{3,7},{4,6},{5,1},{6,4},{7,3},{8,10},{9,13},{10,... | collective-permute-start | bytes 1572872 | tf_op jit(solution)/shard_map/ppermute | solution.py:740
  172.4 13.7 %collective-permute-start.42 = (bf16[512,512]{1,0:T(8,128)(2,1)S(1)}, bf16[512,512]{1,0:T(8,128)(2,1)}, u32[]{:S(2)}, u32[]{:S(2)}) collective-permute-start(bf16[512,512]{1,0:T(8,128)(2,1)S(1)} %join.7.refs_0_), channel_id=1, source_target_pairs={{0,1},{1,0},{2,3},{3,2},{4,5},{5,4},{6,7},{7,6},{8,9},{9,8},{10,11... | collective-permute-start | bytes 1572872 | tf_op jit(solution)/shard_map/ppermute | solution.py:743
  181.9 13.8 %collective-permute-start.41 = (bf16[512,512]{1,0:T(8,128)(2,1)S(1)}, bf16[512,512]{1,0:T(8,128)(2,1)S(1)}, u32[]{:S(2)}, u32[]{:S(2)}) collective-permute-start(bf16[512,512]{1,0:T(8,128)(2,1)S(1)} %join.6.refs_1_), channel_id=1, source_target_pairs={{0,4},{1,3},{2,6},{3,1},{4,0},{5,7},{6,2},{7,5},{8,12},{9,11},{10,... | collective-permute-start | bytes 1572872 | tf_op jit(solution)/shard_map/ppermute | solution.py:740
  183.5 12.2 %collective-permute-start.40 = (bf16[512,512]{1,0:T(8,128)(2,1)S(1)}, bf16[512,512]{1,0:T(8,128)(2,1)S(1)}, u32[]{:S(2)}, u32[]{:S(2)}) collective-permute-start(bf16[512,512]{1,0:T(8,128)(2,1)S(1)} %join.6.refs_1_), channel_id=1, source_target_pairs={{0,2},{1,5},{2,0},{3,7},{4,6},{5,1},{6,4},{7,3},{8,10},{9,13},{10,... | collective-permute-start | bytes 1572872 | tf_op jit(solution)/shard_map/ppermute | solution.py:740
  184.6 11.1 %collective-permute-start.39 = (bf16[64,1024]{1,0:T(8,128)(2,1)}, bf16[64,1024]{1,0:T(8,128)(2,1)S(1)}, u32[]{:S(2)}, u32[]{:S(2)}) collective-permute-start(bf16[64,1024]{1,0:T(8,128)(2,1)} %get-tuple-element.341), channel_id=1, source_target_pairs={{0,16},{1,17},{2,18},{3,19},{4,20},{5,21},{6,22},{7,23},{8,24},{9,... | collective-permute-start | bytes 393224 | tf_op jit(solution)/shard_map/ppermute | solution.py:740
  195.8 13.2 %collective-permute-start.49 = (bf16[512,512]{1,0:T(8,128)(2,1)S(1)}, bf16[512,512]{1,0:T(8,128)(2,1)}, u32[]{:S(2)}, u32[]{:S(2)}) collective-permute-start(bf16[512,512]{1,0:T(8,128)(2,1)S(1)} %collective-permute-done.44.refs_0_), channel_id=1, source_target_pairs={{0,1},{1,0},{2,3},{3,2},{4,5},{5,4},{6,7},{7,6},{8,9},{9,8},{10,11... | collective-permute-start | bytes 1572872 | tf_op jit(solution)/shard_map/ppermute | solution.py:743
  196.3 12.8 %collective-permute-start.50 = (bf16[512,512]{1,0:T(8,128)(2,1)S(1)}, bf16[512,512]{1,0:T(8,128)(2,1)}, u32[]{:S(2)}, u32[]{:S(2)}) collective-permute-start(bf16[512,512]{1,0:T(8,128)(2,1)S(1)} %collective-permute-done.41.refs_1_), channel_id=1, source_target_pairs={{0,1},{1,0},{2,3},{3,2},{4,5},{5,4},{6,7},{7,6},{8,9},{9,8},{10,11... | collective-permute-start | bytes 1572872 | tf_op jit(solution)/shard_map/ppermute | solution.py:743
  196.4 12.7 %collective-permute-start.51 = (bf16[512,512]{1,0:T(8,128)(2,1)S(1)}, bf16[512,512]{1,0:T(8,128)(2,1)}, u32[]{:S(2)}, u32[]{:S(2)}) collective-permute-start(bf16[512,512]{1,0:T(8,128)(2,1)S(1)} %collective-permute-done.43.refs_4_), channel_id=1, source_target_pairs={{0,1},{1,0},{2,3},{3,2},{4,5},{5,4},{6,7},{7,6},{8,9},{9,8},{10,11... | collective-permute-start | bytes 1572872 | tf_op jit(solution)/shard_map/ppermute | solution.py:743
  196.8 12.3 %collective-permute-start.52 = (bf16[512,512]{1,0:T(8,128)(2,1)S(1)}, bf16[512,512]{1,0:T(8,128)(2,1)}, u32[]{:S(2)}, u32[]{:S(2)}) collective-permute-start(bf16[512,512]{1,0:T(8,128)(2,1)S(1)} %collective-permute-done.40.refs_5_), channel_id=1, source_target_pairs={{0,1},{1,0},{2,3},{3,2},{4,5},{5,4},{6,7},{7,6},{8,9},{9,8},{10,11... | collective-permute-start | bytes 1572872 | tf_op jit(solution)/shard_map/ppermute | solution.py:743
  197.1 17.0 %collective-permute-start.48 = (bf16[512,512]{1,0:T(8,128)(2,1)S(1)}, bf16[512,512]{1,0:T(8,128)(2,1)S(1)}, u32[]{:S(2)}, u32[]{:S(2)}) collective-permute-start(bf16[512,512]{1,0:T(8,128)(2,1)S(1)} %collective-permute-done.44.refs_0_), channel_id=1, source_target_pairs={{0,2},{1,5},{2,0},{3,7},{4,6},{5,1},{6,4},{7,3},{8,10},{9,13},{10,... | collective-permute-start | bytes 1572872 | tf_op jit(solution)/shard_map/ppermute | solution.py:740
  215.0 9.2 %collective-permute-start.47 = (bf16[512,512]{1,0:T(8,128)(2,1)S(1)}, bf16[512,512]{1,0:T(8,128)(2,1)S(1)}, u32[]{:S(2)}, u32[]{:S(2)}) collective-permute-start(bf16[512,512]{1,0:T(8,128)(2,1)S(1)} %collective-permute-done.41.refs_1_), channel_id=1, source_target_pairs={{0,2},{1,5},{2,0},{3,7},{4,6},{5,1},{6,4},{7,3},{8,10},{9,13},{10,... | collective-permute-start | bytes 1572872 | tf_op jit(solution)/shard_map/ppermute | solution.py:740
  (52 other events, 673.2 us)

commit v3 on v2

v3 whole, which is shorter than its diff:
```python
import functools

import jax
import jax.numpy as jnp
from jax import lax
from jax.experimental import pallas as pl
from jax.experimental.pallas import tpu as pltpu
from jax.sharding import PartitionSpec as P

BF = jnp.bfloat16
F32 = jnp.float32
MIB = 1 << 20
HALO_WIDTHS = (512, 512)
TILES = 2
LAST = ("q", "p")
ORDER = "K O d0 d1 G d0 d1 H B d0 d1 t h d0 d1 b t h d0 d1 t h e t h x0 x1 p0 p1 t R F P"

FREE = pl.CostEstimate(flops=0, bytes_accessed=0, transcendentals=0)
LARGE = pl.CostEstimate(flops=5_000_000_000, bytes_accessed=0, transcendentals=0)
SMALL = pl.CostEstimate(flops=0, bytes_accessed=0, transcendentals=0)
HBM = pl.BlockSpec(memory_space=pltpu.HBM)
SMEM = pl.BlockSpec(memory_space=pltpu.SMEM)
VMEM = pl.BlockSpec(memory_space=pltpu.VMEM)
BY_ROWS = (((0,), (0,)), ((), ()))


def shape_of(shape, dtype):
    return jax.ShapeDtypeStruct(shape, dtype)


def far_shape(shape, dtype):
    return pltpu.HBM(shape, dtype)


def call(body, out_shape, name, vmem=24, cost=FREE, **rest):
    kernel = pl.pallas_call(
        body,
        out_shape=out_shape,
        compiler_params=pltpu.CompilerParams(vmem_limit_bytes=vmem * MIB),
        cost_estimate=cost,
        name=name,
        **rest,
    )
    specs = rest.get("in_specs")

    def run(*operands):
        if specs is None:
            return kernel(*operands)
        return kernel(
            *[
                pltpu.with_memory_space_constraint(x, pltpu.HBM) if spec is HBM else x
                for x, spec in zip(operands, specs)
            ]
        )

    return run


def scalars(*x):
    return jnp.stack([jnp.int32(v) for v in x])


def mxu(a, b):
    return jnp.dot(a, b, preferred_element_type=F32)


def by_rows(a, b):
    return lax.dot_general(a, b, BY_ROWS, preferred_element_type=F32)


def copy_all(copies):
    for c in copies:
        c.start()
    for c in copies:
        c.wait()


def tick_kernel(x, out):
    out[...] = x[...]


def tick_of(x):
    return call(tick_kernel, shape_of(x.shape, x.dtype), "tick", cost=LARGE)(x)


def outgoing_kernel(where, rows, features, away, *keep):
    nodes, width = features.shape
    half = width // 2
    hot = (rows[...] == lax.broadcasted_iota(jnp.int32, (rows.shape[0], nodes), 1)).astype(BF)
    there = features[:, pl.ds(pl.multiple_of((1 - where[0]) * half, half), half)]
    away[...] = mxu(hot, there).astype(BF)
    here = mxu(hot, features[:, pl.ds(pl.multiple_of(where[0] * half, half), half)]).astype(BF)
    at = 0
    for out in keep:
        out[...] = here[:, at : at + out.shape[1]]
        at += out.shape[1]


def outgoing_rows(core, rows, features, widths):
    sends, half = rows.shape[0], features.shape[1] // 2
    return call(
        outgoing_kernel,
        tuple(shape_of((sends, w), BF) for w in (half,) + widths),
        "outgoing",
        in_specs=[SMEM, VMEM, VMEM],
    )(scalars(core), rows, features)


def stack_kernel(n, received, *refs):
    own, outs = refs[:n], refs[n:]
    at = 0
    for x, out in zip(own, outs):
        rows, w = x.shape
        out[:rows, :] = x[...]
        out[rows:, :] = received[:, at : at + w]
        at += w


def stack(own, received):
    return call(
        functools.partial(stack_kernel, len(own)),
        tuple(shape_of((2 * x.shape[0], x.shape[1]), BF) for x in own),
        "stack",
    )(received, *own)


def stack_rows_kernel(own, received, out):
    rows = own.shape[0]
    out[:rows, :] = own[...]
    out[rows:, :] = received[...]


def stack_rows(own, received, cost=FREE):
    rows, w = own.shape
    return call(stack_rows_kernel, shape_of((2 * rows, w), own.dtype), "stack_rows", cost=cost)(
        own, received
    )


def counts_kernel(packed, label, halo_count, own_count, factors):
    nodes, columns = packed.shape
    slots = columns - 1

    def count(labels):
        total = jnp.zeros((nodes, labels.shape[1]), F32)
        for e in range(slots):
            total = total + jnp.where(packed[:, e : e + 1] == labels, 1.0, 0.0)
        return total

    halo_count[...] = count(label[...]).astype(BF)
    local = lax.broadcasted_iota(jnp.int32, (nodes, nodes), 1)
    row = lax.broadcasted_iota(jnp.int32, (nodes, nodes), 0)
    own_count[...] = (count(local) + jnp.where(row == local, 2.0, 0.0)).astype(BF)
    degree = jnp.zeros((nodes, 1), F32)
    for e in range(slots):
        degree = degree + jnp.where(packed[:, e : e + 1] >= 0, 1.0, 0.0)
    lane = lax.broadcasted_iota(jnp.int32, factors.shape, 1)
    factors[...] = jnp.where(lane == 0, packed[:, slots:].astype(F32), 1.0 / (degree + 1.0))


def counts(packed, label):
    nodes = packed.shape[0]
    return call(
        counts_kernel,
        (
            shape_of((nodes, label.shape[1]), BF),
            shape_of((nodes, nodes), BF),
            shape_of((nodes, 128), F32),
        ),
        "counts",
    )(packed, label)


def aggregate_kernel(n, where, features, features_in, *refs):
    own, sibling, halos = refs[:3], refs[3:6], refs[6 : 6 + n]
    out, near, sem = refs[6 + n :]
    _, nodes, half = near.shape
    core = where[0]
    here = pl.ds(pl.multiple_of(core * half, half), half)
    copies = [
        pltpu.make_async_copy(x.at[:, here], near.at[k], sem.at[k])
        for k, x in enumerate((features, features_in))
    ]
    for c in copies:
        c.start()
    for k, (halo_count, own_count, factors) in enumerate((own, sibling)):
        rows = pl.ds(pl.multiple_of((core if k == 0 else 1 - core) * nodes, nodes), nodes)
        start = 0
        for i, halo in enumerate(halos):
            part = slice(start, start + halo.shape[1])
            total = mxu(halo_count[...], halo[...])
            if i == 0:
                copies[k].wait()
            total = total + mxu(own_count[...], near[k][:, part])
            out[rows, part] = (total * factors[:, 1:2]).astype(BF)
            start += halo.shape[1]


def aggregate(core, features, features_in, own, sibling, halos):
    rows, width = features.shape
    half = width // 2
    return call(
        functools.partial(aggregate_kernel, len(halos)),
        shape_of((2 * rows, half), BF),
        "aggregate",
        in_specs=[SMEM, HBM, HBM] + [VMEM] * (6 + len(halos)),
        scratch_shapes=[pltpu.VMEM((2, rows, half), BF), pltpu.SemaphoreType.DMA((2,))],
    )(scalars(core), features, features_in, *own, *sibling, *halos)


def grad_loads(core, cotangent, cotangent_in, near_g, column, sems):
    rows, width = cotangent.shape
    start, size = column
    whole = pl.ds(pl.multiple_of(core * (width // 2) + start, 256), size)
    own = pl.ds(pl.multiple_of(core * rows, rows), rows)
    far = pl.ds(pl.multiple_of((1 - core) * rows, rows), rows)
    return [
        pltpu.make_async_copy(cotangent.at[:, whole], near_g.at[own, :], sems.at[0]),
        pltpu.make_async_copy(cotangent_in.at[:, whole], near_g.at[far, :], sems.at[1]),
    ]


def factor(core, own, other, lane):
    return jnp.concatenate(
        [jnp.where(core == k, own[:, lane : lane + 1], other[:, lane : lane + 1]) for k in range(2)], 0
    )


def forward_kernel(
    where, mine, other, constants, own_factors, other_factors,
    weight, cotangent, cotangent_in,
    z_out, stats_ref, near_mine, near_other, near_g, z_ref, sem, out_sem,
):
    core = where[0]
    block = 256
    half = z_ref.shape[1]
    own = pl.ds(pl.multiple_of(core * half, half), half)
    far = pl.ds(pl.multiple_of((1 - core) * half, half), half)

    def loads(k, start, size):
        whole = pl.ds(pl.multiple_of(core * half + start, 256), size)
        part = slice(start, start + size)
        return [
            pltpu.make_async_copy(weight.at[own, whole], near_mine.at[:, part], sem.at[0, k]),
            pltpu.make_async_copy(weight.at[far, whole], near_other.at[:, part], sem.at[1, k]),
        ]

    ranges = ((0, block), (block, half - block))
    copies = [loads(k, *r) for k, r in enumerate(ranges)]
    grads = grad_loads(core, cotangent, cotangent_in, near_g, (0, half), sem.at[2])
    for c in copies[0] + grads + copies[1]:
        c.start()

    def store(j):
        part = slice(2 * j * block, 2 * (j + 1) * block)
        return pltpu.make_async_copy(z_ref.at[:, part], z_out.at[:, part], out_sem.at[j])

    valid = factor(core, own_factors, other_factors, 0)
    bias = constants[0:1, own]
    for j in range(half // block):
        at = slice(j * block, (j + 1) * block)
        if j < 2:
            for c in copies[j]:
                c.wait()
        z_ref[:, at] = (
            mxu(mine[...], near_mine[:, at]) + mxu(other[...], near_other[:, at]) + bias[:, at]
        )
        if j == 0:
            for c in grads:
                c.wait()
        if j % 2 == 1:
            store(j // 2).start()
        z = z_ref[:, at]
        sigma = 1.0 / (1.0 + jnp.exp(-z))
        y = z * sigma
        slope = (sigma + y * (1.0 - sigma)) * valid
        g = near_g[:, at].astype(F32) * valid

        def column(x):
            return jnp.sum(x, axis=0, keepdims=True)

        count = jnp.broadcast_to(column(valid), (1, block))
        y_sum = column(y * valid)
        centred = (y - y_sum / jnp.maximum(count, 1.0)) * valid
        stats_ref[0:1, at] = count
        stats_ref[1:2, at] = y_sum
        stats_ref[2:3, at] = column(centred * centred)
        stats_ref[3:4, at] = column(g)
        stats_ref[4:5, at] = column(g * centred)
        stats_ref[5:6, at] = column(slope * g)
        stats_ref[6:7, at] = column(slope)
        stats_ref[7:8, at] = column(slope * centred)
    for j in range(half // block // 2):
        store(j).wait()


def forward(core, mine, other, weight, constants, cotangent, cotangent_in, own, sibling):
    rows, half = cotangent.shape[0], mine.shape[1]
    return call(
        forward_kernel,
        (far_shape((2 * rows, half), F32), shape_of((8, half), F32)),
        "forward",
        in_specs=[SMEM] + [VMEM] * 5 + [HBM] * 3,
        out_specs=(HBM, VMEM),
        scratch_shapes=[
            pltpu.VMEM((half, half), BF),
            pltpu.VMEM((half, half), BF),
            pltpu.VMEM((2 * rows, half), BF),
            pltpu.VMEM((2 * rows, half), F32),
            pltpu.SemaphoreType.DMA((3, 2)),
            pltpu.SemaphoreType.DMA((half // 512,)),
        ],
    )(
        scalars(core), mine, other, constants, own, sibling, weight, cotangent, cotangent_in
    )


def merge_kernel(where, own, received, out):
    upper = where[0] == 1
    a, b = own[...], received[...]
    a, b = jnp.where(upper, b, a), jnp.where(upper, a, b)

    def row(x, k):
        return x[k : k + 1, :]

    na, nb = row(a, 0), row(b, 0)
    n = na + nb
    mean = (row(a, 1) + row(b, 1)) / jnp.maximum(n, 1.0)
    da = row(a, 1) / jnp.maximum(na, 1.0) - mean
    db = row(b, 1) / jnp.maximum(nb, 1.0) - mean
    out[...] = a + b
    out[2:3, :] = (row(a, 2) + na * da * da) + (row(b, 2) + nb * db * db)
    out[4:5, :] = (row(a, 4) + da * row(a, 3)) + (row(b, 4) + db * row(b, 3))
    out[7:8, :] = (row(a, 7) + da * row(a, 6)) + (row(b, 7) + db * row(b, 6))


def merge(own, received, v):
    return call(
        merge_kernel, shape_of(own.shape, F32), "merge", in_specs=[SMEM, VMEM, VMEM]
    )(scalars(v), own, received)


def gradient(where, at, stats_ref, constants, z, g_in, valid):
    core, half, start = where
    size = z.shape[1]
    vector = pl.ds(pl.multiple_of(core * half + start, size), size)
    stats = stats_ref[:, at]
    gamma, beta = constants[1:2, vector], constants[2:3, vector]
    n = stats[0:1, :]
    mean = stats[1:2, :] / n
    deviation = lax.rsqrt(stats[2:3, :] / n + 1e-05)
    shift = stats[3:4, :]
    scale = deviation * stats[4:5, :]
    gain = gamma * deviation
    vectors = (
        gain * (stats[5:6, :] - shift / n * stats[6:7, :] - deviation * scale / n * stats[7:8, :]),
        scale,
        shift,
    )
    sigma = 1.0 / (1.0 + jnp.exp(-z))
    y = z * sigma
    slope = (sigma + y * (1.0 - sigma)) * valid
    g = g_in.astype(F32) * valid
    normalized = (y - mean) * deviation
    dz = gain * (g - shift / n - normalized * (scale / n)) * slope
    return dz, valid * (gamma * normalized + beta), vectors


def dz_kernel(
    where, stats_ref, constants, own_factors, other_factors, z_ref, cotangent, cotangent_in,
    out, near_z, near_g, sem,
):
    side, core = where[0], where[1]
    half, size = z_ref.shape[1], out.shape[1]
    block = 256
    blocks = size // block

    def loads(k):
        start = side * size + k * block
        part = pl.ds(pl.multiple_of(start, block), block)
        here = slice(k * block, (k + 1) * block)
        copy = pltpu.make_async_copy(z_ref.at[:, part], near_z.at[:, here], sem.at[k, 2])
        return [copy] + grad_loads(
            core, cotangent, cotangent_in, near_g.at[:, here], (start, block), sem.at[k]
        )

    copies = [loads(k) for k in range(blocks)]
    for c in copies[0] + copies[1]:
        c.start()
    valid = factor(core, own_factors, other_factors, 0)
    for k in range(blocks):
        for c in copies[k]:
            c.wait()
        here = slice(k * block, (k + 1) * block)
        start = side * size + k * block
        at = pl.ds(pl.multiple_of(start, block), block)
        dz, _, _ = gradient(
            (core, half, start), at, stats_ref, constants, near_z[:, here], near_g[:, here], valid
        )
        out[:, here] = dz.astype(BF)


def dz_of(core, side, z, stats, constants, cotangent, cotangent_in, own, sibling):
    rows, half = z.shape
    return call(
        dz_kernel,
        shape_of((rows, half // 2), BF),
        "dz",
        in_specs=[SMEM] + [VMEM] * 4 + [HBM] * 3,
        scratch_shapes=[
            pltpu.VMEM((rows, half // 2), F32),
            pltpu.VMEM((rows, half // 2), BF),
            pltpu.SemaphoreType.DMA((2, 3)),
        ],
    )(scalars(side, core), stats, constants, own, sibling, z, cotangent, cotangent_in)


def outputs_kernel(
    where, stats_ref, constants, own_factors, other_factors, z_ref, cotangent, cotangent_in,
    dz_scaled, act_keep, act_away, vectors, near_z, near_g, sem,
):
    core = where[0]
    rows, half = z_ref.shape
    nodes = rows // 2
    block = 256
    copies = [pltpu.make_async_copy(z_ref, near_z, sem.at[2])]
    copies += grad_loads(core, cotangent, cotangent_in, near_g, (0, half), sem)
    for c in copies:
        c.start()
    valid, inverse = (factor(core, own_factors, other_factors, lane) for lane in range(2))
    for c in copies:
        c.wait()
    vectors[3:8, :] = jnp.zeros((5, half), F32)
    for k in range(half // block):
        at = slice(k * block, (k + 1) * block)
        dz, act, sums = gradient(
            (core, half, k * block), at, stats_ref, constants, near_z[:, at], near_g[:, at], valid
        )
        dz_scaled[:, at] = (dz * inverse).astype(BF)
        act = act.astype(BF)
        act_keep[:, at] = jnp.where(core == 0, act[:nodes], act[nodes:])
        act_away[:, at] = jnp.where(core == 0, act[nodes:], act[:nodes])
        for i, x in enumerate(sums):
            vectors[i : i + 1, at] = x


def outputs(core, z, stats, constants, cotangent, cotangent_in, own, sibling):
    rows, half = z.shape
    act = shape_of((rows // 2, half), BF)
    return call(
        outputs_kernel,
        (shape_of((rows, half), BF), act, act, shape_of((8, half), F32)),
        "outputs",
        in_specs=[SMEM] + [VMEM] * 4 + [HBM] * 3,
        scratch_shapes=[
            pltpu.VMEM((rows, half), F32),
            pltpu.VMEM((rows, half), BF),
            pltpu.SemaphoreType.DMA((3,)),
        ],
    )(scalars(core), stats, constants, own, sibling, z, cotangent, cotangent_in)


def fetch_kernel(where, mine, other, mine_pair, other_pair, out, out_pair, sem):
    for flag, pair in ((1, (mine, mine_pair)), (0, (other, other_pair))):

        @pl.when(where[0] == flag)
        def _():
            copy_all(
                [
                    pltpu.make_async_copy(x, o, sem.at[i])
                    for i, (x, o) in enumerate(zip(pair, (out, out_pair)))
                ]
            )


def fetch(flag, mine, other, mine_pair, other_pair):
    out = shape_of(mine.shape, mine.dtype)
    return call(
        fetch_kernel,
        (out, out),
        "fetch",
        in_specs=[SMEM] + [HBM] * 4,
        out_specs=(VMEM, VMEM),
        scratch_shapes=[pltpu.SemaphoreType.DMA((2,))],
    )(scalars(flag), mine, other, mine_pair, other_pair)


def weight_part_kernel(columns, agg, agg_pair, dz, dz_pair, out):
    out[...] = (
        by_rows(agg[:, columns], dz[...]) + by_rows(agg_pair[:, columns], dz_pair[...])
    ).astype(BF)


def weight_part(agg, agg_pair, dz, dz_pair, t):
    tall = agg.shape[1] // TILES
    return call(
        functools.partial(weight_part_kernel, slice(t * tall, (t + 1) * tall)),
        shape_of((tall, dz.shape[1]), BF),
        "weight_part",
    )(agg, agg_pair, dz, dz_pair)


def fold_kernel(where, own, received, away, keep):
    rows = keep.shape[0]
    for side, out in ((1 - where[0], away), (where[0], keep)):
        part = pl.ds(pl.multiple_of(side * rows, rows), rows)
        out[...] = (own[part, :].astype(F32) + received[part, :].astype(F32)).astype(BF)


def fold(own, received, v, cost=FREE):
    rows, w = own.shape
    out = shape_of((rows // 2, w), BF)
    return call(fold_kernel, (out, out), "fold", in_specs=[SMEM, VMEM, VMEM], cost=cost)(
        scalars(v), own, received
    )


def total_kernel(own, received, out):
    out[...] = (own[...].astype(F32) + received[...].astype(F32)).astype(BF)


def total_of(own, received, cost=FREE):
    return call(total_kernel, shape_of(own.shape, BF), "total", cost=cost)(own, received)


def join_kernel(where, own, received, out):
    rows = own.shape[0]
    for side, x in ((where[0], own), (1 - where[0], received)):
        out[pl.ds(pl.multiple_of(side * rows, rows), rows), :] = x[...]


def join(own, received, v, cost=FREE):
    rows, w = own.shape
    return call(
        join_kernel,
        shape_of((2 * rows, w), BF),
        "join",
        in_specs=[SMEM, VMEM, VMEM],
        cost=cost,
    )(scalars(v), own, received)


def place_kernel(n, where, *refs):
    pieces, (out, wide, put) = refs[:n], refs[-3:]

    def write(i, k):
        rows, w = pieces[i].shape
        row = pl.multiple_of(where[3 * i + k], 64)
        column = pl.multiple_of(where[3 * i + 2], 128)
        return pltpu.make_async_copy(
            wide.at[i, k * (rows // 2) : (k + 1) * (rows // 2), :],
            out.at[pl.ds(row, rows // 2), pl.ds(column, w)],
            put.at[i, k],
        )

    for i in range(n):
        step = 128
        half = pieces[i].shape[0] // 2
        for k in range(2):

            @pl.loop(0, half // step)
            def _(j):
                part = pl.ds(pl.multiple_of(k * half + j * step, step), step)
                wide[i, part, :] = pieces[i][part, :].astype(F32)

            write(i, k).start()
    for i in range(n):
        for k in range(2):
            write(i, k).wait()


def place(total, pieces, shape):
    n = len(pieces)
    rows, w = pieces[0][0].shape
    operands = [scalars(*[x for p in pieces for x in p[1:]])] + [p[0] for p in pieces]
    specs = [SMEM] + [VMEM] * n
    aliases = {}
    if total is not None:
        aliases = {len(operands): 0}
        operands.append(total)
        specs.append(HBM)
    return call(
        functools.partial(place_kernel, n),
        far_shape(shape, F32),
        "place",
        in_specs=specs,
        out_specs=HBM,
        scratch_shapes=[pltpu.VMEM((n, rows, w), F32), pltpu.SemaphoreType.DMA((n, 2))],
        input_output_aliases=aliases,
    )(*operands)


def back_part_kernel(columns, where, own, sibling, dz, out):
    nodes = own.shape[0]
    total = 0.0
    for side, count in ((where[0], own), (1 - where[0], sibling)):
        rows = pl.ds(pl.multiple_of(side * nodes, nodes), nodes)
        total = total + by_rows(count[:, columns], dz[rows, :])
    out[...] = total.astype(BF)


def back_part(core, own, sibling, dz, k, parts):
    rows = own.shape[1] // parts
    return call(
        functools.partial(back_part_kernel, slice(k * rows, (k + 1) * rows)),
        shape_of((rows, dz.shape[1]), BF),
        "back_part",
        in_specs=[SMEM] + [VMEM] * 3,
    )(scalars(core), own, sibling, dz)


def halve_kernel(own, received, away, keep):
    rows = keep.shape[0]
    keep[...] = (own[:rows].astype(F32) + received[:rows].astype(F32)).astype(BF)
    away[...] = (own[rows:].astype(F32) + received[rows:].astype(F32)).astype(BF)


def halve(own, received):
    rows, w = own.shape
    out = shape_of((rows // 2, w), BF)
    return call(halve_kernel, (out, out), "halve")(own, received)


def own_back_kernel(where, own, sibling, dz, keep, away):
    nodes = keep.shape[0]
    core = where[0]
    for side, count, out in ((core, own, keep), (1 - core, sibling, away)):
        part = pl.ds(pl.multiple_of(side * nodes, nodes), nodes)
        out[...] = by_rows(count[...], dz[part, :]).astype(BF)


def own_back(core, own, sibling, dz):
    rows, half = dz.shape
    out = shape_of((rows // 2, half), BF)
    return call(own_back_kernel, (out, out), "own_back", in_specs=[SMEM] + [VMEM] * 3)(
        scalars(core), own, sibling, dz
    )


def finish_kernel(
    where, rows, back, back_in, vec, vec_in, own, own_in, act, act_in, weight,
    grad, activations, vectors, near_weight, near_own, table, weight_sem, own_sem, act_sem,
):
    core = where[0]
    nodes, half = own.shape
    sends = rows.shape[0]
    block = 512
    blocks = weight.shape[0] // block

    def side_of(k):
        return pl.ds(pl.multiple_of((core if k == 0 else 1 - core) * half, half), half)

    owns = [
        pltpu.make_async_copy(x, near_own.at[k], own_sem.at[k]) for k, x in enumerate((own, own_in))
    ]
    acts = [
        pltpu.make_async_copy(x, activations.at[:, side_of(k)], act_sem.at[k])
        for k, x in enumerate((act, act_in))
    ]
    weights = [
        pltpu.make_async_copy(
            weight.at[k * block : (k + 1) * block, :],
            near_weight.at[k * block : (k + 1) * block, :],
            weight_sem.at[k],
        )
        for k in range(blocks)
    ]
    for c in owns + weights + acts:
        c.start()
    hot = (rows[...] == lax.broadcasted_iota(jnp.int32, (sends, nodes), 1)).astype(BF)
    for k, (back_part, vector) in enumerate(((back[:sends], vec), (back_in[...], vec_in))):
        vectors[:, side_of(k)] = vector[...]
        owns[k].wait()
        part = near_own[k].astype(F32) + by_rows(hot, back_part)
        table[:, side_of(k)] = part.astype(BF)
    for k in range(blocks):
        weights[k].wait()
        part = slice(k * block, (k + 1) * block)
        grad[:, part] = lax.dot_general(
            table[...], near_weight[part, :], (((1,), (1,)), ((), ())), preferred_element_type=F32
        ).astype(BF)
    for c in acts:
        c.wait()


def finish(core, rows, back, back_in, own, own_in, act, act_in, vec, vec_in, weight):
    nodes, half = own.shape
    width = 2 * half
    return call(
        finish_kernel,
        (
            shape_of((nodes, width), BF),
            shape_of((nodes, width), BF),
            shape_of((8, width), F32),
        ),
        "finish",
        in_specs=[SMEM] + [VMEM] * 5 + [HBM] * 5,
        out_specs=(VMEM, VMEM, VMEM),
        scratch_shapes=[
            pltpu.VMEM(weight.shape, BF),
            pltpu.VMEM((2, nodes, half), BF),
            pltpu.VMEM((nodes, width), BF),
            pltpu.SemaphoreType.DMA((width // 512,)),
            pltpu.SemaphoreType.DMA((2,)),
            pltpu.SemaphoreType.DMA((2,)),
        ],
    )(scalars(core), rows, back, back_in, vec, vec_in, own, own_in, act, act_in, weight)


def on_device(
    size,
    features,
    weight,
    bias,
    gamma,
    beta,
    neighbours,
    edge_mask,
    node_mask,
    send_rows,
    send_mask,
    cotangent,
):
    nodes, width = features.shape
    sends = send_rows.shape[0]
    half = width // 2
    quarter = width // 4
    levels = size.bit_length() - 5

    me = lax.axis_index("dom")
    core = me & 1
    is0 = core == 0
    bits = {"f": (1, 2), "p": (2, 3), "q": (3, 1), "s": (2, 1), "z": (3, 3)}
    others = list(range(4, levels + 4))
    for b in others:
        bits[b] = (b, b)
    axes = ["f", "p", "q"] + others

    def bit_of(b):
        return (me >> b) & 1

    def bit(b):
        return jnp.where(is0, bit_of(bits[b][0]), bit_of(bits[b][1]))

    def weight_of(b):
        return jnp.where(is0, 1 << bits[b][0], 1 << bits[b][1])

    def peer(i, b):
        return i ^ (1 << bits[b][i & 1])

    first, sibling_first = bit("f"), jnp.where(is0, bit_of(2), bit_of(1))
    high, sibling_high = bit("p"), jnp.where(is0, bit_of(3), bit_of(2))

    def along(x, b):
        return lax.ppermute(x, "dom", [(i, peer(i, b)) for i in range(size)])

    def swap(x):
        return lax.ppermute(x, "dom", [(i, i ^ 1) for i in range(size)])

    token = [jnp.zeros((8, 128), F32)]

    def arrive(*x):
        *x, token[0] = lax.optimization_barrier((*x, token[0]))
        return x[0] if len(x) == 1 else x

    def tick():
        token[0] = tick_of(token[0])

    def start(generators):
        running = dict(generators)
        for k in running:
            next(running[k])
        done = {}

        def advance(k):
            try:
                next(running[k])
            except StopIteration as stop:
                done[k] = stop.value

        return advance, done

    live_row = jnp.where(send_mask > 0, send_rows, -1)[:, None]
    out_away, *out_keep = outgoing_rows(
        core, live_row, features, HALO_WIDTHS
    )
    outgoing = stack(out_keep, arrive(swap(out_away)))
    halo_rows = sends * size
    chip_rows = 2 * sends

    def gather_halo(k, x):
        for b in reversed(axes):
            received = along(x, b)
            yield
            x = stack_rows(x, arrive(received), SMALL if k else FREE)
        return x

    generators = {k: gather_halo(k, x) for k, x in enumerate(outgoing)}
    advance, halo = start(generators)

    def hop():
        for k in generators:
            advance(k)

    live_neighbour = jnp.where(edge_mask > 0, neighbours, -1)
    packed = jnp.concatenate([live_neighbour, node_mask[:, None]], 1)
    place_of = jnp.arange(halo_rows)
    chip, row = place_of // chip_rows, place_of % chip_rows
    relative = 0
    for k, b in enumerate(axes):
        relative = relative + ((chip >> (len(axes) - 1 - k)) & 1) * weight_of(b)
    owner = (me ^ relative) ^ (row // sends)
    label = (nodes + owner * sends + row % sends)[None, :]
    packed, label = arrive(packed, label)
    sibling_packed = arrive(swap(packed))
    hop()
    features_in, cotangent_in = swap(features), swap(cotangent)
    constants = jnp.stack([bias, gamma, beta])
    packed = arrive(packed)
    own = arrive(*counts(packed, label))
    constants = arrive(constants)
    hop()
    features_in, cotangent_in, sibling_packed = arrive(features_in, cotangent_in, sibling_packed)
    sibling = arrive(*counts(sibling_packed, label))
    hop()
    for _ in range(levels):
        hop()

    agg_mine = aggregate(
        core, features, features_in, own, sibling, [halo[k] for k in generators]
    )
    agg_other = swap(agg_mine)
    mine_pair = along(agg_mine, "f")
    agg_other = arrive(agg_other)
    other_pair = along(agg_other, "f")
    z, stats = forward(
        core, agg_mine, agg_other, weight, constants, cotangent, cotangent_in, own[2], sibling[2]
    )

    same = (high == core).astype(jnp.int32)
    for k, b in enumerate(others + ["q", "p", "f"]):
        received = along(stats, b)
        if k == 0:
            mine_pair = arrive(mine_pair)
        if b == "f":
            other_pair = arrive(other_pair)
        stats = merge(stats, arrive(received), bit(b))
    nodes_args = (z, stats, constants, cotangent, cotangent_in, own[2], sibling[2])
    dz_send = dz_of(core, 1 - first, *nodes_args)

    dz_pair = along(dz_send, "f")
    aggs = (agg_mine, agg_other, mine_pair, other_pair)
    dz_send = arrive(dz_send)
    dz_keep = dz_of(core, first, *nodes_args)
    away = fetch(1 - same, *aggs)
    dz_keep, *away = arrive(dz_keep, *away)
    dz_pair = arrive(dz_pair)

    def weight_gradient(t):
        cost = SMALL if t else FREE
        received = along(weight_part(*away, dz_keep, dz_pair, t), "p")
        yield
        part = weight_part(*keep, dz_keep, dz_pair, t)
        part = arrive(part)
        yield
        received = arrive(received)
        for b in axes[2:]:
            out, part = fold(part, received, bit(b), cost)
            received = along(out, b)
            yield
            received = arrive(received)
        part = total_of(part, received, cost)
        for b in others[::-1] + [LAST[0]]:
            received = along(part, b)
            yield
            part = join(part, arrive(received), bit(b), cost)
        return part

    def reduce_halo():
        received, part = along(back_send, axes[0]), back_keep
        for b in axes[1:]:
            yield
            out, part = halve(part, arrive(received))
            received = along(out, b)
        yield
        return total_of(part, arrive(received))

    generators = {"d%d" % t: weight_gradient(t) for t in range(TILES)}
    advance, found = start(generators)
    groups = {k: [1, 1, len(others), len(others), 1] for k in generators}
    groups["h"] = [1, 1, 1, len(others)]
    tall = half // TILES
    tiles = range(TILES)
    shape = (width, width)
    if LAST[1] == "z":
        layers = bit_of(3), bit_of(3)
        steps = jnp.where(is0, half, tall // 2), jnp.where(is0, tall // 2, half)
        steps = steps, steps[::-1]
    else:
        layers = high, sibling_high
        steps = ((tall // 2, half),) * 2

    def pieces(own, sibling, away, other):
        placed = []
        for side, arrays in enumerate((own, sibling)):
            begin = core if side == 0 else 1 - core
            f = first if side == 0 else sibling_first
            inner, outer = steps[side]
            z = 1 - layers[side] if away else layers[side]
            for t, x in enumerate(arrays):
                row = t * tall + z * outer
                column = begin * half + (1 - f if other else f) * quarter
                placed.append((x, row, row + inner, column))
        return placed

    across, pair, here = [None] * TILES, [None] * TILES, [None] * TILES
    here_across, here_pair, pair_across = [None] * TILES, [None] * TILES, [None] * TILES
    for action in ORDER.split():
        if action == "K":
            keep = arrive(*fetch(same, *aggs))
            for k in generators:
                advance(k)
        elif action == "O":
            dz_scaled, act, act_away, vectors = arrive(*outputs(core, *nodes_args))
        elif action == "G":
            dz_scaled = arrive(dz_scaled)
            back_send, back_keep = arrive(
                *(back_part(core, own[0], sibling[0], dz_scaled, k, 2) for k in (1, 0))
            )
        elif action == "H":
            back_send = arrive(back_send)
            advance_halo, halo_part = start({"h": reduce_halo()})
        elif action == "B":
            dz_scaled = arrive(dz_scaled)
            kept_back, away_back = arrive(*own_back(core, own[1], sibling[1], dz_scaled))
            own_in, act_in, vectors_in = swap(away_back), swap(act_away), swap(vectors)
        elif action == "b":
            own_in, act_in, vectors_in = arrive(own_in, act_in, vectors_in)
        elif action == "t":
            tick()
        elif action in groups:
            step = advance_halo if action == "h" else advance
            for _ in range(groups[action].pop(0)):
                step(action)
            if action in found:
                t = list(generators).index(action)
                across[t], pair[t] = along(found[action], LAST[1]), along(found[action], "f")
                here[t] = swap(found[action])
        elif action == "e":
            here = [arrive(x) for x in here]
            part = [found[k] for k in generators]
            total = arrive(place(None, pieces(part, here, False, False), shape))
        elif action[0] == "x":
            t = int(action[1])
            across[t] = arrive(across[t])
            here_across[t], pair_across[t] = swap(across[t]), along(across[t], "f")
        elif action[0] == "p":
            t = int(action[1])
            pair[t] = arrive(pair[t])
            here_pair[t] = swap(pair[t])
        elif action == "R":
            back = halo_part["h"]
            back_in = arrive(swap(back[sends:]))
        elif action == "F":
            grad_features, activations, vectors = arrive(
                *finish(
                    core, live_row, back, back_in, kept_back, own_in, act, act_in, vectors, vectors_in, weight
                )
            )
        elif action == "P":
            here_across = [arrive(x) for x in here_across]
            here_pair = [arrive(x) for x in here_pair]
            total = place(
                total,
                pieces(across, here_across, True, False) + pieces(pair, here_pair, False, True),
                shape,
            )
            total = arrive(total)
    pair_across = [arrive(x) for x in pair_across]
    vectors = vectors + token[0][0, 0]
    here_pair_across = [swap(x) for x in pair_across]
    total = place(total, pieces(pair_across, here_pair_across, True, True), shape)
    return activations, grad_features, total, vectors[0], vectors[1], vectors[2]


def solution(mesh):
    size = mesh.shape["dom"]
    return jax.shard_map(
        functools.partial(on_device, size),
        mesh=mesh,
        in_specs=(
            P("dom", None),
            P(),
            P(),
            P(),
            P(),
            P("dom", None),
            P("dom", None),
            P("dom"),
            P("dom"),
            P("dom"),
            P("dom", None),
        ),
        out_specs=(P("dom", None), P("dom", None), P(), P(), P(), P()),
        check_vma=False,
    )
```

time: 229 us -> 193 us (0.84)
  waiting for transfers between devices: 97.6 us -> 76.7 us
  starting transfers between devices: 54.8 us -> 48.1 us
  Pallas kernels: 59.4 us -> 53.9 us
  local copies, waits for them, and re-layouts: 12.1 us -> 8.45 us
    ppermute x37 -> x35, waiting for transfers between devices: 94.1 us -> 73.4 us  [along(): return lax.ppermute(x, 'dom', [(i, peer(i, b)) for i in range(size)])]
    pallas_call x29 -> x27, Pallas kernels: 52.8 us -> 44.9 us  [run(): kernel(*[pltpu.with_memory_space_constraint(x, pltpu.HBM) if spec is HBM...]
    ppermute x37 -> x35, starting transfers between devices: 50.2 us -> 44.4 us  [along(): return lax.ppermute(x, 'dom', [(i, peer(i, b)) for i in range(size)])]
    unnamed x58 -> x40, local copies, waits for them, and re-layouts: 10.4 us -> 6.71 us
    pallas_call x17 -> x26, Pallas kernels: 6.61 us -> 9 us  [run(): return kernel(*operands)]
  transfers between devices with their start and end apart: 55 -> 52, of which waited for: 30 -> 28; matrix products, arithmetic and copies ran while one was open for 2% -> 3% of each run, Pallas kernels for 20% -> 23%
where the time goes in v3:
time: 193 us; the launch traced here: 192 us
  waiting for transfers between devices  76.7 us (40%)
  Pallas kernels  53.9 us (28%)
  starting transfers between devices  48.1 us (25%)
  local copies, waits for them, and re-layouts  8.45 us (4%)
  other arithmetic  3.69 us (2%)
    ppermute x35, waiting for transfers between devices, along(): return lax.ppermute(x, 'dom', [(i, peer(i, b)) for i in range(size)])  73.4 us
    pallas_call x27, Pallas kernels, run(): kernel(*[pltpu.with_memory_space_constraint(x, pltpu.HBM) if spec is HBM...  44.9 us
    ppermute x35, starting transfers between devices, along(): return lax.ppermute(x, 'dom', [(i, peer(i, b)) for i in range(size)])  44.4 us
    pallas_call x26, Pallas kernels, run(): return kernel(*operands)  9 us
    unnamed x40, local copies, waits for them, and re-layouts  6.71 us
  transfers between devices with their start and end apart: 52, of which 28 were waited for; matrix products, arithmetic and copies ran while one was open for 3% of the time, Pallas kernels for 23%

profile of v3, /device:TPU:0, one launch (start us, length us, event | category | flops | bytes accessed | tf_op | source)
XLA Modules:
  0.0 192.4 jit_solution(284139597548177891)
XLA Ops:
  5.4 3.7 %collective-permute-start.2 = (bf16[64,512]{1,0:T(8,128)(2,1)S(1)}, bf16[64,512]{1,0:T(8,128)(2,1)S(1)}, u32[]{:S(2)}, u32[]{:S(2)}) collective-permute-start(bf16[64,512]{1,0:T(8,128)(2,1)S(1)} %get-tuple-element.203.own), channel_id=1, source_target_pairs={{0,16},{1,17},{2,18},{3,19},{4,20},{5,21},{6,22},{7,23},{8,24},{9,... | collective-permute-start | bytes 196616 | tf_op jit(solution)/shard_map/ppermute | solution.py:755
  10.8 2.6 %collective-permute-done.2.received = bf16[64,512]{1,0:T(8,128)(2,1)S(1)} collective-permute-done((bf16[64,512]{1,0:T(8,128)(2,1)S(1)}, bf16[64,512]{1,0:T(8,128)(2,1)S(1)}, u32[]{:S(2)}, u32[]{:S(2)}) %collective-permute-start.2) | collective-permute-done | bytes 65568 | tf_op jit(solution)/shard_map/ppermute | solution.py:755
  13.4 2.6 %collective-permute-done.1.received = bf16[64,512]{1,0:T(8,128)(2,1)S(1)} collective-permute-done((bf16[64,512]{1,0:T(8,128)(2,1)S(1)}, bf16[64,512]{1,0:T(8,128)(2,1)S(1)}, u32[]{:S(2)}, u32[]{:S(2)}) %collective-permute-start.1) | collective-permute-done | bytes 65568 | tf_op jit(solution)/shard_map/ppermute | solution.py:755
  19.1 2.6 %counts.2 = (bf16[256,1024]{1,0:T(8,128)(2,1)S(1)}, bf16[256,256]{1,0:T(8,128)(2,1)S(1)}, f32[256,128]{1,0:T(8,128)S(1)}) custom-call(s32[256,17]{1,0:T(8,128)S(1)} %copy.32.packed, s32[1,1024]{1,0:T(1,128)S(1)} %fusion.label), custom_call_target="tpu_custom_call" | custom-call | tf_op jit(solution)/shard_map/counts/pallas_call | solution.py:48
  25.2 2.6 %counts.3 = (bf16[256,1024]{1,0:T(8,128)(2,1)S(1)}, bf16[256,256]{1,0:T(8,128)(2,1)S(1)}, f32[256,128]{1,0:T(8,128)S(1)}) custom-call(s32[256,17]{1,0:T(8,128)S(1)} %collective-permute-done.3.packed, s32[1,1024]{1,0:T(1,128)S(1)} %fusion.label), custom_call_target="tpu_custom_call" | custom-call | tf_op jit(solution)/shard_map/counts/pallas_call | solution.py:48
  29.9 2.8 %collective-permute-done.10.received = bf16[256,512]{1,0:T(8,128)(2,1)S(1)} collective-permute-done((bf16[256,512]{1,0:T(8,128)(2,1)S(1)}, bf16[256,512]{1,0:T(8,128)(2,1)S(1)}, u32[]{:S(2)}, u32[]{:S(2)}) %collective-permute-start.10) | collective-permute-done | bytes 262176 | tf_op jit(solution)/shard_map/ppermute | solution.py:755
  34.3 3.2 %collective-permute-done.9.received = bf16[512,512]{1,0:T(8,128)(2,1)S(1)} collective-permute-done((bf16[512,512]{1,0:T(8,128)(2,1)S(1)}, bf16[512,512]{1,0:T(8,128)(2,1)S(1)}, u32[]{:S(2)}, u32[]{:S(2)}) %collective-permute-start.9) | collective-permute-done | bytes 524320 | tf_op jit(solution)/shard_map/ppermute | solution.py:755
  37.5 5.6 %collective-permute-done.11.received = bf16[512,512]{1,0:T(8,128)(2,1)S(1)} collective-permute-done((bf16[512,512]{1,0:T(8,128)(2,1)S(1)}, bf16[512,512]{1,0:T(8,128)(2,1)S(1)}, u32[]{:S(2)}, u32[]{:S(2)}) %collective-permute-start.11) | collective-permute-done | bytes 524320 | tf_op jit(solution)/shard_map/ppermute | solution.py:755
  43.3 2.9 %aggregate.1.mine = bf16[512,1024]{1,0:T(8,128)(2,1)S(1)} custom-call(s32[1]{0:T(128)} %bitcast.where, bf16[256,2048]{1,0:T(8,128)(2,1)} %features.3, bf16[256,2048]{1,0:T(8,128)(2,1)} %copy-done.17, bf16[256,1024]{1,0:T(8,128)(2,1)S(1)} %get-tuple-element.214.refs_0_.own, bf16[256,256]{1,0:T(8,128)(2,1)S(1)} %get-tuple-element.229.refs_1_.own, ...), custom_call_target="tpu_custom_call" | custom-call | tf_op jit(solution)/shard_map/aggregate/pallas_call | solution.py:49
  50.5 7.5 %forward.1 = (f32[512,1024]{1,0:T(8,128)}, f32[8,1024]{1,0:T(8,128)S(1)}) custom-call(s32[1]{0:T(128)} %bitcast.where, bf16[512,1024]{1,0:T(8,128)(2,1)S(1)} %aggregate.1.mine, bf16[512,1024]{1,0:T(8,128)(2,1)S(1)} %collective-permute-done.12.other, f32[3,2048]{1,0:T(4,128)S(1)} %pad_maximum_fusion.constants, ...), custom_call_target="tpu_custom_call" | custom-call | tf_op jit(solution)/shard_map/forward/pallas_call | solution.py:49
  57.9 2.3 %collective-permute-start.13 = (f32[8,1024]{1,0:T(8,128)S(1)}, f32[8,1024]{1,0:T(8,128)S(1)}, u32[]{:S(2)}, u32[]{:S(2)}) collective-permute-start(f32[8,1024]{1,0:T(8,128)S(1)} %get-tuple-element.247.own), channel_id=1, source_target_pairs={{0,16},{1,17},{2,18},{3,19},{4,20},{5,21},{6,22},{7,23},{8,24},{9,... | collective-permute-start | bytes 98312 | tf_op jit(solution)/shard_map/ppermute | solution.py:755
  64.1 2.9 %collective-permute-done.15.received = f32[8,1024]{1,0:T(8,128)S(1)} collective-permute-done((f32[8,1024]{1,0:T(8,128)S(1)}, f32[8,1024]{1,0:T(8,128)S(1)}, u32[]{:S(2)}, u32[]{:S(2)}) %collective-permute-start.15) | collective-permute-done | bytes 32800 | tf_op jit(solution)/shard_map/ppermute | solution.py:755
  68.5 2.9 %collective-permute-done.16.received = f32[8,1024]{1,0:T(8,128)S(1)} collective-permute-done((f32[8,1024]{1,0:T(8,128)S(1)}, f32[8,1024]{1,0:T(8,128)S(1)}, u32[]{:S(2)}, u32[]{:S(2)}) %collective-permute-start.16) | collective-permute-done | bytes 32800 | tf_op jit(solution)/shard_map/ppermute | solution.py:755
  72.8 2.7 %collective-permute-done.17.received = f32[8,1024]{1,0:T(8,128)S(1)} collective-permute-done((f32[8,1024]{1,0:T(8,128)S(1)}, f32[8,1024]{1,0:T(8,128)S(1)}, u32[]{:S(2)}, u32[]{:S(2)}) %collective-permute-start.17) | collective-permute-done | bytes 32800 | tf_op jit(solution)/shard_map/ppermute | solution.py:755
  75.5 3.2 %dz.2 = bf16[512,512]{1,0:T(8,128)(2,1)} custom-call(s32[2]{0:T(128)S(1)} %pad_add_fusion.1.where, f32[8,1024]{1,0:T(8,128)S(1)} %merge.7.stats_ref, f32[3,2048]{1,0:T(4,128)S(1)} %pad_maximum_fusion.constants, f32[256,128]{1,0:T(8,128)S(1)} %get-tuple-element.230.refs_2_.own_factors, f32[256,128]{1,0:T(8,128)S(1)} %get-tuple-element.232.refs_5_.other_factors, ...), custom_call_target="tpu_custom_call" | custom-call | tf_op jit(solution)/shard_map/dz/pallas_call | solution.py:49
  79.5 2.4 %dz.3 = bf16[512,512]{1,0:T(8,128)(2,1)S(1)} custom-call(s32[2]{0:T(128)S(1)} %pad_add_fusion.2.where, f32[8,1024]{1,0:T(8,128)S(1)} %merge.7.stats_ref, f32[3,2048]{1,0:T(4,128)S(1)} %pad_maximum_fusion.constants, f32[256,128]{1,0:T(8,128)S(1)} %get-tuple-element.230.refs_2_.own_factors, f32[256,128]{1,0:T(8,128)S(1)} %get-tuple-element.232.refs_5_.other_factors, ...), custom_call_target="tpu_custom_call" | custom-call | tf_op jit(solution)/shard_map/dz/pallas_call | solution.py:49
  83.6 4.6 %collective-permute-done.19.dz_pair = bf16[512,512]{1,0:T(8,128)(2,1)S(1)} collective-permute-done((bf16[512,512]{1,0:T(8,128)(2,1)}, bf16[512,512]{1,0:T(8,128)(2,1)S(1)}, u32[]{:S(2)}, u32[]{:S(2)}) %collective-permute-start.19) | collective-permute-done | bytes 524320 | tf_op jit(solution)/shard_map/ppermute | solution.py:755
  91.9 3.7 %outputs.1 = (bf16[512,1024]{1,0:T(8,128)(2,1)S(1)}, bf16[256,1024]{1,0:T(8,128)(2,1)S(1)}, bf16[256,1024]{1,0:T(8,128)(2,1)S(1)}, f32[8,1024]{1,0:T(8,128)S(1)}) custom-call(s32[1]{0:T(128)} %bitcast.where, f32[8,1024]{1,0:T(8,128)S(1)} %merge.7.stats_ref, f32[3,2048]{1,0:T(4,128)S(1)} %pad_maximum_fusion.constants, ...), custom_call_target="tpu_custom_call" | custom-call | tf_op jit(solution)/shard_map/outputs/pallas_call | solution.py:49
  100.7 3.2 %collective-permute-done.20.received = bf16[512,512]{1,0:T(8,128)(2,1)S(1)} collective-permute-done((bf16[512,512]{1,0:T(8,128)(2,1)S(1)}, bf16[512,512]{1,0:T(8,128)(2,1)S(1)}, u32[]{:S(2)}, u32[]{:S(2)}) %collective-permute-start.20) | collective-permute-done | bytes 524320 | tf_op jit(solution)/shard_map/ppermute | solution.py:755
  106.6 5.1 %collective-permute-done.22.received = bf16[256,512]{1,0:T(8,128)(2,1)S(1)} collective-permute-done((bf16[256,512]{1,0:T(8,128)(2,1)S(1)}, bf16[256,512]{1,0:T(8,128)(2,1)S(1)}, u32[]{:S(2)}, u32[]{:S(2)}) %collective-permute-start.22) | collective-permute-done | bytes 262176 | tf_op jit(solution)/shard_map/ppermute | solution.py:755
  115.9 3.2 %collective-permute-done.26.received = bf16[128,512]{1,0:T(8,128)(2,1)S(1)} collective-permute-done((bf16[128,512]{1,0:T(8,128)(2,1)S(1)}, bf16[128,512]{1,0:T(8,128)(2,1)S(1)}, u32[]{:S(2)}, u32[]{:S(2)}) %collective-permute-start.26) | collective-permute-done | bytes 131104 | tf_op jit(solution)/shard_map/ppermute | solution.py:755
  119.8 6.0 %collective-permute-done.25.received = bf16[128,512]{1,0:T(8,128)(2,1)S(1)} collective-permute-done((bf16[128,512]{1,0:T(8,128)(2,1)S(1)}, bf16[128,512]{1,0:T(8,128)(2,1)S(1)}, u32[]{:S(2)}, u32[]{:S(2)}) %collective-permute-start.25) | collective-permute-done | bytes 131104 | tf_op jit(solution)/shard_map/ppermute | solution.py:755
  128.9 4.2 %collective-permute-done.31.received = bf16[128,512]{1,0:T(8,128)(2,1)S(1)} collective-permute-done((bf16[128,512]{1,0:T(8,128)(2,1)S(1)}, bf16[128,512]{1,0:T(8,128)(2,1)S(1)}, u32[]{:S(2)}, u32[]{:S(2)}) %collective-permute-start.31) | collective-permute-done | bytes 131104 | tf_op jit(solution)/shard_map/ppermute | solution.py:755
  136.0 3.5 %collective-permute-done.35.received = bf16[256,512]{1,0:T(8,128)(2,1)S(1)} collective-permute-done((bf16[256,512]{1,0:T(8,128)(2,1)S(1)}, bf16[256,512]{1,0:T(8,128)(2,1)S(1)}, u32[]{:S(2)}, u32[]{:S(2)}) %collective-permute-start.35) | collective-permute-done | bytes 262176 | tf_op jit(solution)/shard_map/ppermute | solution.py:755
  139.6 2.7 %collective-permute-done.34.received = bf16[256,512]{1,0:T(8,128)(2,1)S(1)} collective-permute-done((bf16[256,512]{1,0:T(8,128)(2,1)S(1)}, bf16[256,512]{1,0:T(8,128)(2,1)S(1)}, u32[]{:S(2)}, u32[]{:S(2)}) %collective-permute-start.34) | collective-permute-done | bytes 262176 | tf_op jit(solution)/shard_map/ppermute | solution.py:755
  147.9 7.2 %collective-permute-done.33.received = bf16[128,1024]{1,0:T(8,128)(2,1)S(1)} collective-permute-done((bf16[128,1024]{1,0:T(8,128)(2,1)S(1)}, bf16[128,1024]{1,0:T(8,128)(2,1)S(1)}, u32[]{:S(2)}, u32[]{:S(2)}) %collective-permute-start.33) | collective-permute-done | bytes 262176 | tf_op jit(solution)/shard_map/ppermute | solution.py:755
  158.0 2.8 %collective-permute-start.36 = (bf16[64,1024]{1,0:T(8,128)(2,1)S(1)}, bf16[64,1024]{1,0:T(8,128)(2,1)S(1)}, u32[]{:S(2)}, u32[]{:S(2)}) collective-permute-start(bf16[64,1024]{1,0:T(8,128)(2,1)S(1)} %get-tuple-element.338), channel_id=1, source_target_pairs={{0,16},{1,17},{2,18},{3,19},{4,20},{5,21},{6,22},{7,23},{8,24},{9,... | collective-permute-start | bytes 393224 | tf_op jit(solution)/shard_map/ppermute | solution.py:755
  161.9 3.4 %place.3.refs_8_ = f32[2048,2048]{1,0:T(8,128)} custom-call(s32[12]{0:T(128)S(1)} %stack.182.where, bf16[512,512]{1,0:T(8,128)(2,1)S(1)} %join.6.refs_0_, bf16[512,512]{1,0:T(8,128)(2,1)S(1)} %join.7.refs_1_, bf16[512,512]{1,0:T(8,128)(2,1)S(1)} %copy-done.8, bf16[512,512]{1,0:T(8,128)(2,1)} %collective-permute-done.38.refs_3_), custom_call_target="tpu_custom_call" | custom-call | tf_op jit(solution)/shard_map/place/pallas_call | solution.py:49
  167.6 2.3 %collective-permute-done.40.refs_5_ = bf16[512,512]{1,0:T(8,128)(2,1)S(1)} collective-permute-done((bf16[512,512]{1,0:T(8,128)(2,1)S(1)}, bf16[512,512]{1,0:T(8,128)(2,1)S(1)}, u32[]{:S(2)}, u32[]{:S(2)}) %collective-permute-start.40) | collective-permute-done | bytes 524320 | tf_op jit(solution)/shard_map/ppermute | solution.py:755
  173.0 7.8 %finish.1 = (bf16[256,2048]{1,0:T(8,128)(2,1)}, bf16[256,2048]{1,0:T(8,128)(2,1)}, f32[8,2048]{1,0:T(8,128)S(1)}) custom-call(s32[1]{0:T(128)} %bitcast.where, s32[32,1]{1,0:T(8,128)S(1)} %copy.33.rows, bf16[64,1024]{1,0:T(8,128)(2,1)S(1)} %total.5.back, bf16[32,1024]{1,0:T(8,128)(2,1)S(1)} %collective-permute-done.39.back_in, ...), custom_call_target="tpu_custom_call" | custom-call | tf_op jit(solution)/shard_map/finish/pallas_call | solution.py:49
  180.8 4.8 %place.4.refs_4_ = f32[2048,2048]{1,0:T(8,128)} custom-call(s32[24]{0:T(128)S(1)} %stack.194.where, bf16[512,512]{1,0:T(8,128)(2,1)S(1)} %collective-permute-done.43.refs_0_, bf16[512,512]{1,0:T(8,128)(2,1)S(1)} %collective-permute-done.42.refs_1_, bf16[512,512]{1,0:T(8,128)(2,1)S(1)} %copy-done.6, ...), custom_call_target="tpu_custom_call", output_to_operand_aliasing={{}: (9, {})} | custom-call | tf_op jit(solution)/shard_map/place/pallas_call | solution.py:49
  189.0 3.2 %place.5 = f32[2048,2048]{1,0:T(8,128)} custom-call(s32[12]{0:T(128)S(1)} %stack.193.where, bf16[512,512]{1,0:T(8,128)(2,1)S(1)} %collective-permute-done.44.refs_0_, bf16[512,512]{1,0:T(8,128)(2,1)} %collective-permute-done.49.refs_1_, bf16[512,512]{1,0:T(8,128)(2,1)S(1)} %collective-permute-done.50.refs_2_, ...), custom_call_target="tpu_custom_call", output_to_operand_aliasing={{}: (5, {})} | custom-call | tf_op jit(solution)/shard_map/place/pallas_call | solution.py:49
  (183 shorter events, 70.8 us)
Async XLA Ops:
  0.6 23.6 %collective-permute-start.4 = (bf16[256,2048]{1,0:T(8,128)(2,1)}, bf16[256,2048]{1,0:T(8,128)(2,1)S(1)}, u32[]{:S(2)}, u32[]{:S(2)}) collective-permute-start(bf16[256,2048]{1,0:T(8,128)(2,1)} %features.3), channel_id=1, source_target_pairs={{0,1},{1,0},{2,3},{3,2},{4,5},{5,4},{6,7},{7,6},{8,9},{9,8},{10,11... | collective-permute-start | bytes 3145736 | tf_op jit(solution)/shard_map/ppermute | solution.py:758
  1.1 24.0 %collective-permute-start.5 = (bf16[256,2048]{1,0:T(8,128)(2,1)}, bf16[256,2048]{1,0:T(8,128)(2,1)}, u32[]{:S(2)}, u32[]{:S(2)}) collective-permute-start(bf16[256,2048]{1,0:T(8,128)(2,1)} %cotangent.7), channel_id=1, source_target_pairs={{0,1},{1,0},{2,3},{3,2},{4,5},{5,4},{6,7},{7,6},{8,9},{9,8},{10,11... | collective-permute-start | bytes 3145736 | tf_op jit(solution)/shard_map/ppermute | solution.py:758
  5.4 8.0 %collective-permute-start.2 = (bf16[64,512]{1,0:T(8,128)(2,1)S(1)}, bf16[64,512]{1,0:T(8,128)(2,1)S(1)}, u32[]{:S(2)}, u32[]{:S(2)}) collective-permute-start(bf16[64,512]{1,0:T(8,128)(2,1)S(1)} %get-tuple-element.203.own), channel_id=1, source_target_pairs={{0,16},{1,17},{2,18},{3,19},{4,20},{5,21},{6,22},{7,23},{8,24},{9,... | collective-permute-start | bytes 196616 | tf_op jit(solution)/shard_map/ppermute | solution.py:755
  23.5 9.3 %collective-permute-start.10 = (bf16[256,512]{1,0:T(8,128)(2,1)S(1)}, bf16[256,512]{1,0:T(8,128)(2,1)S(1)}, u32[]{:S(2)}, u32[]{:S(2)}) collective-permute-start(bf16[256,512]{1,0:T(8,128)(2,1)S(1)} %stack_rows.12.own), channel_id=1, source_target_pairs={{0,4},{1,9},{2,6},{3,11},{4,0},{5,13},{6,2},{7,15},{8,12},{9,1},{1... | collective-permute-start | bytes 786440 | tf_op jit(solution)/shard_map/ppermute | solution.py:755
  28.3 9.2 %collective-permute-start.9 = (bf16[512,512]{1,0:T(8,128)(2,1)S(1)}, bf16[512,512]{1,0:T(8,128)(2,1)S(1)}, u32[]{:S(2)}, u32[]{:S(2)}) collective-permute-start(bf16[512,512]{1,0:T(8,128)(2,1)S(1)} %stack_rows.11.own), channel_id=1, source_target_pairs={{0,2},{1,5},{2,0},{3,7},{4,6},{5,1},{6,4},{7,3},{8,10},{9,13},{10,... | collective-permute-start | bytes 1572872 | tf_op jit(solution)/shard_map/ppermute | solution.py:755
  32.8 10.4 %collective-permute-start.11 = (bf16[512,512]{1,0:T(8,128)(2,1)S(1)}, bf16[512,512]{1,0:T(8,128)(2,1)S(1)}, u32[]{:S(2)}, u32[]{:S(2)}) collective-permute-start(bf16[512,512]{1,0:T(8,128)(2,1)S(1)} %stack_rows.14.own), channel_id=1, source_target_pairs={{0,2},{1,5},{2,0},{3,7},{4,6},{5,1},{6,4},{7,3},{8,10},{9,13},{10,... | collective-permute-start | bytes 1572872 | tf_op jit(solution)/shard_map/ppermute | solution.py:755
  46.3 15.0 %collective-permute-start.14 = (bf16[512,1024]{1,0:T(8,128)(2,1)S(1)}, bf16[512,1024]{1,0:T(8,128)(2,1)}, u32[]{:S(2)}, u32[]{:S(2)}) collective-permute-start(bf16[512,1024]{1,0:T(8,128)(2,1)S(1)} %aggregate.1.mine), channel_id=1, source_target_pairs={{0,2},{1,5},{2,0},{3,7},{4,6},{5,1},{6,4},{7,3},{8,10},{9,13},{10,... | collective-permute-start | bytes 3145736 | tf_op jit(solution)/shard_map/ppermute | solution.py:755
  48.9 23.9 %collective-permute-start.18 = (bf16[512,1024]{1,0:T(8,128)(2,1)S(1)}, bf16[512,1024]{1,0:T(8,128)(2,1)}, u32[]{:S(2)}, u32[]{:S(2)}) collective-permute-start(bf16[512,1024]{1,0:T(8,128)(2,1)S(1)} %collective-permute-done.12.other), channel_id=1, source_target_pairs={{0,2},{1,5},{2,0},{3,7},{4,6},{5,1},{6,4},{7,3},{8,10},{9,13},{10,... | collective-permute-start | bytes 3145736 | tf_op jit(solution)/shard_map/ppermute | solution.py:755
  78.8 9.5 %collective-permute-start.19 = (bf16[512,512]{1,0:T(8,128)(2,1)}, bf16[512,512]{1,0:T(8,128)(2,1)S(1)}, u32[]{:S(2)}, u32[]{:S(2)}) collective-permute-start(bf16[512,512]{1,0:T(8,128)(2,1)} %dz.2), channel_id=1, source_target_pairs={{0,2},{1,5},{2,0},{3,7},{4,6},{5,1},{6,4},{7,3},{8,10},{9,13},{10,... | collective-permute-start | bytes 1572872 | tf_op jit(solution)/shard_map/ppermute | solution.py:755
  89.0 10.5 %collective-permute-start.21 = (bf16[512,512]{1,0:T(8,128)(2,1)S(1)}, bf16[512,512]{1,0:T(8,128)(2,1)S(1)}, u32[]{:S(2)}, u32[]{:S(2)}) collective-permute-start(bf16[512,512]{1,0:T(8,128)(2,1)S(1)} %weight_part.7), channel_id=1, source_target_pairs={{0,4},{1,9},{2,6},{3,11},{4,0},{5,13},{6,2},{7,15},{8,12},{9,1},{1... | collective-permute-start | bytes 1572872 | tf_op jit(solution)/shard_map/ppermute | solution.py:755
  91.2 12.6 %collective-permute-start.20 = (bf16[512,512]{1,0:T(8,128)(2,1)S(1)}, bf16[512,512]{1,0:T(8,128)(2,1)S(1)}, u32[]{:S(2)}, u32[]{:S(2)}) collective-permute-start(bf16[512,512]{1,0:T(8,128)(2,1)S(1)} %weight_part.6), channel_id=1, source_target_pairs={{0,4},{1,9},{2,6},{3,11},{4,0},{5,13},{6,2},{7,15},{8,12},{9,1},{1... | collective-permute-start | bytes 1572872 | tf_op jit(solution)/shard_map/ppermute | solution.py:755
  104.0 7.7 %collective-permute-start.22 = (bf16[256,512]{1,0:T(8,128)(2,1)S(1)}, bf16[256,512]{1,0:T(8,128)(2,1)S(1)}, u32[]{:S(2)}, u32[]{:S(2)}) collective-permute-start(bf16[256,512]{1,0:T(8,128)(2,1)S(1)} %get-tuple-element.292), channel_id=1, source_target_pairs={{0,8},{1,3},{2,10},{3,1},{4,12},{5,7},{6,14},{7,5},{8,0},{9,11},{1... | collective-permute-start | bytes 786440 | tf_op jit(solution)/shard_map/ppermute | solution.py:755
  111.7 14.8 %collective-permute-start.24 = (bf16[512,1024]{1,0:T(8,128)(2,1)S(1)}, bf16[512,1024]{1,0:T(8,128)(2,1)S(1)}, u32[]{:S(2)}, u32[]{:S(2)}) collective-permute-start(bf16[512,1024]{1,0:T(8,128)(2,1)S(1)} %back_part.2), channel_id=1, source_target_pairs={{0,2},{1,5},{2,0},{3,7},{4,6},{5,1},{6,4},{7,3},{8,10},{9,13},{10,... | collective-permute-start | bytes 3145736 | tf_op jit(solution)/shard_map/ppermute | solution.py:755
  111.8 7.3 %collective-permute-start.26 = (bf16[128,512]{1,0:T(8,128)(2,1)S(1)}, bf16[128,512]{1,0:T(8,128)(2,1)S(1)}, u32[]{:S(2)}, u32[]{:S(2)}) collective-permute-start(bf16[128,512]{1,0:T(8,128)(2,1)S(1)} %get-tuple-element.305), channel_id=1, source_target_pairs={{0,16},{1,17},{2,18},{3,19},{4,20},{5,21},{6,22},{7,23},{8,24},{9,... | collective-permute-start | bytes 393224 | tf_op jit(solution)/shard_map/ppermute | solution.py:755
  113.8 12.0 %collective-permute-start.25 = (bf16[128,512]{1,0:T(8,128)(2,1)S(1)}, bf16[128,512]{1,0:T(8,128)(2,1)S(1)}, u32[]{:S(2)}, u32[]{:S(2)}) collective-permute-start(bf16[128,512]{1,0:T(8,128)(2,1)S(1)} %get-tuple-element.302), channel_id=1, source_target_pairs={{0,16},{1,17},{2,18},{3,19},{4,20},{5,21},{6,22},{7,23},{8,24},{9,... | collective-permute-start | bytes 393224 | tf_op jit(solution)/shard_map/ppermute | solution.py:755
  114.9 20.2 %collective-permute-start.29 = (bf16[256,1024]{1,0:T(8,128)(2,1)S(1)}, bf16[256,1024]{1,0:T(8,128)(2,1)S(1)}, u32[]{:S(2)}, u32[]{:S(2)}) collective-permute-start(bf16[256,1024]{1,0:T(8,128)(2,1)S(1)} %get-tuple-element.318), channel_id=1, source_target_pairs={{0,1},{1,0},{2,3},{3,2},{4,5},{5,4},{6,7},{7,6},{8,9},{9,8},{10,11... | collective-permute-start | bytes 1572872 | tf_op jit(solution)/shard_map/ppermute | solution.py:758
  115.4 19.8 %collective-permute-start.28 = (bf16[256,1024]{1,0:T(8,128)(2,1)S(1)}, bf16[256,1024]{1,0:T(8,128)(2,1)S(1)}, u32[]{:S(2)}, u32[]{:S(2)}) collective-permute-start(bf16[256,1024]{1,0:T(8,128)(2,1)S(1)} %get-tuple-element.317), channel_id=1, source_target_pairs={{0,1},{1,0},{2,3},{3,2},{4,5},{5,4},{6,7},{7,6},{8,9},{9,8},{10,11... | collective-permute-start | bytes 1572872 | tf_op jit(solution)/shard_map/ppermute | solution.py:758
  119.1 9.7 %collective-permute-start.32 = (bf16[128,512]{1,0:T(8,128)(2,1)S(1)}, bf16[128,512]{1,0:T(8,128)(2,1)S(1)}, u32[]{:S(2)}, u32[]{:S(2)}) collective-permute-start(bf16[128,512]{1,0:T(8,128)(2,1)S(1)} %total.4.own), channel_id=1, source_target_pairs={{0,16},{1,17},{2,18},{3,19},{4,20},{5,21},{6,22},{7,23},{8,24},{9,... | collective-permute-start | bytes 393224 | tf_op jit(solution)/shard_map/ppermute | solution.py:755
  126.7 9.3 %collective-permute-start.27 = (bf16[256,1024]{1,0:T(8,128)(2,1)S(1)}, bf16[256,1024]{1,0:T(8,128)(2,1)S(1)}, u32[]{:S(2)}, u32[]{:S(2)}) collective-permute-start(bf16[256,1024]{1,0:T(8,128)(2,1)S(1)} %get-tuple-element.316), channel_id=1, source_target_pairs={{0,4},{1,9},{2,6},{3,11},{4,0},{5,13},{6,2},{7,15},{8,12},{9,1},{1... | collective-permute-start | bytes 1572872 | tf_op jit(solution)/shard_map/ppermute | solution.py:755
  139.5 17.1 %collective-permute-start.37 = (bf16[512,512]{1,0:T(8,128)(2,1)S(1)}, bf16[512,512]{1,0:T(8,128)(2,1)S(1)}, u32[]{:S(2)}, u32[]{:S(2)}) collective-permute-start(bf16[512,512]{1,0:T(8,128)(2,1)S(1)} %join.6.refs_0_), channel_id=1, source_target_pairs={{0,1},{1,0},{2,3},{3,2},{4,5},{5,4},{6,7},{7,6},{8,9},{9,8},{10,11... | collective-permute-start | bytes 1572872 | tf_op jit(solution)/shard_map/ppermute | solution.py:758
  142.3 15.7 %collective-permute-start.38 = (bf16[512,512]{1,0:T(8,128)(2,1)S(1)}, bf16[512,512]{1,0:T(8,128)(2,1)}, u32[]{:S(2)}, u32[]{:S(2)}) collective-permute-start(bf16[512,512]{1,0:T(8,128)(2,1)S(1)} %join.7.refs_1_), channel_id=1, source_target_pairs={{0,1},{1,0},{2,3},{3,2},{4,5},{5,4},{6,7},{7,6},{8,9},{9,8},{10,11... | collective-permute-start | bytes 1572872 | tf_op jit(solution)/shard_map/ppermute | solution.py:758
  142.5 23.9 %collective-permute-start.43 = (bf16[512,512]{1,0:T(8,128)(2,1)S(1)}, bf16[512,512]{1,0:T(8,128)(2,1)S(1)}, u32[]{:S(2)}, u32[]{:S(2)}) collective-permute-start(bf16[512,512]{1,0:T(8,128)(2,1)S(1)} %join.6.refs_0_), channel_id=1, source_target_pairs={{0,4},{1,9},{2,6},{3,11},{4,0},{5,13},{6,2},{7,15},{8,12},{9,1},{1... | collective-permute-start | bytes 1572872 | tf_op jit(solution)/shard_map/ppermute | solution.py:755
  144.0 23.1 %collective-permute-start.42 = (bf16[512,512]{1,0:T(8,128)(2,1)S(1)}, bf16[512,512]{1,0:T(8,128)(2,1)S(1)}, u32[]{:S(2)}, u32[]{:S(2)}) collective-permute-start(bf16[512,512]{1,0:T(8,128)(2,1)S(1)} %join.7.refs_1_), channel_id=1, source_target_pairs={{0,4},{1,9},{2,6},{3,11},{4,0},{5,13},{6,2},{7,15},{8,12},{9,1},{1... | collective-permute-start | bytes 1572872 | tf_op jit(solution)/shard_map/ppermute | solution.py:755
  145.8 9.3 %collective-permute-start.33 = (bf16[128,1024]{1,0:T(8,128)(2,1)S(1)}, bf16[128,1024]{1,0:T(8,128)(2,1)S(1)}, u32[]{:S(2)}, u32[]{:S(2)}) collective-permute-start(bf16[128,1024]{1,0:T(8,128)(2,1)S(1)} %get-tuple-element.330), channel_id=1, source_target_pairs={{0,8},{1,3},{2,10},{3,1},{4,12},{5,7},{6,14},{7,5},{8,0},{9,11},{1... | collective-permute-start | bytes 786440 | tf_op jit(solution)/shard_map/ppermute | solution.py:755
  155.1 12.0 %collective-permute-start.41 = (bf16[512,512]{1,0:T(8,128)(2,1)S(1)}, bf16[512,512]{1,0:T(8,128)(2,1)S(1)}, u32[]{:S(2)}, u32[]{:S(2)}) collective-permute-start(bf16[512,512]{1,0:T(8,128)(2,1)S(1)} %join.6.refs_0_), channel_id=1, source_target_pairs={{0,2},{1,5},{2,0},{3,7},{4,6},{5,1},{6,4},{7,3},{8,10},{9,13},{10,... | collective-permute-start | bytes 1572872 | tf_op jit(solution)/shard_map/ppermute | solution.py:755
  157.5 12.5 %collective-permute-start.40 = (bf16[512,512]{1,0:T(8,128)(2,1)S(1)}, bf16[512,512]{1,0:T(8,128)(2,1)S(1)}, u32[]{:S(2)}, u32[]{:S(2)}) collective-permute-start(bf16[512,512]{1,0:T(8,128)(2,1)S(1)} %join.7.refs_1_), channel_id=1, source_target_pairs={{0,2},{1,5},{2,0},{3,7},{4,6},{5,1},{6,4},{7,3},{8,10},{9,13},{10,... | collective-permute-start | bytes 1572872 | tf_op jit(solution)/shard_map/ppermute | solution.py:755
  158.0 8.4 %collective-permute-start.36 = (bf16[64,1024]{1,0:T(8,128)(2,1)S(1)}, bf16[64,1024]{1,0:T(8,128)(2,1)S(1)}, u32[]{:S(2)}, u32[]{:S(2)}) collective-permute-start(bf16[64,1024]{1,0:T(8,128)(2,1)S(1)} %get-tuple-element.338), channel_id=1, source_target_pairs={{0,16},{1,17},{2,18},{3,19},{4,20},{5,21},{6,22},{7,23},{8,24},{9,... | collective-permute-start | bytes 393224 | tf_op jit(solution)/shard_map/ppermute | solution.py:755
  167.1 13.7 %collective-permute-start.46 = (bf16[512,512]{1,0:T(8,128)(2,1)S(1)}, bf16[512,512]{1,0:T(8,128)(2,1)}, u32[]{:S(2)}, u32[]{:S(2)}) collective-permute-start(bf16[512,512]{1,0:T(8,128)(2,1)S(1)} %collective-permute-done.42.refs_1_), channel_id=1, source_target_pairs={{0,1},{1,0},{2,3},{3,2},{4,5},{5,4},{6,7},{7,6},{8,9},{9,8},{10,11... | collective-permute-start | bytes 1572872 | tf_op jit(solution)/shard_map/ppermute | solution.py:758
  167.2 13.6 %collective-permute-start.47 = (bf16[512,512]{1,0:T(8,128)(2,1)S(1)}, bf16[512,512]{1,0:T(8,128)(2,1)}, u32[]{:S(2)}, u32[]{:S(2)}) collective-permute-start(bf16[512,512]{1,0:T(8,128)(2,1)S(1)} %collective-permute-done.41.refs_4_), channel_id=1, source_target_pairs={{0,1},{1,0},{2,3},{3,2},{4,5},{5,4},{6,7},{7,6},{8,9},{9,8},{10,11... | collective-permute-start | bytes 1572872 | tf_op jit(solution)/shard_map/ppermute | solution.py:758
  169.9 10.9 %collective-permute-start.48 = (bf16[512,512]{1,0:T(8,128)(2,1)S(1)}, bf16[512,512]{1,0:T(8,128)(2,1)}, u32[]{:S(2)}, u32[]{:S(2)}) collective-permute-start(bf16[512,512]{1,0:T(8,128)(2,1)S(1)} %collective-permute-done.40.refs_5_), channel_id=1, source_target_pairs={{0,1},{1,0},{2,3},{3,2},{4,5},{5,4},{6,7},{7,6},{8,9},{9,8},{10,11... | collective-permute-start | bytes 1572872 | tf_op jit(solution)/shard_map/ppermute | solution.py:758
  169.9 15.8 %collective-permute-start.44 = (bf16[512,512]{1,0:T(8,128)(2,1)S(1)}, bf16[512,512]{1,0:T(8,128)(2,1)S(1)}, u32[]{:S(2)}, u32[]{:S(2)}) collective-permute-start(bf16[512,512]{1,0:T(8,128)(2,1)S(1)} %collective-permute-done.43.refs_0_), channel_id=1, source_target_pairs={{0,2},{1,5},{2,0},{3,7},{4,6},{5,1},{6,4},{7,3},{8,10},{9,13},{10,... | collective-permute-start | bytes 1572872 | tf_op jit(solution)/shard_map/ppermute | solution.py:755
  172.2 13.5 %collective-permute-start.49 = (bf16[512,512]{1,0:T(8,128)(2,1)S(1)}, bf16[512,512]{1,0:T(8,128)(2,1)}, u32[]{:S(2)}, u32[]{:S(2)}) collective-permute-start(bf16[512,512]{1,0:T(8,128)(2,1)S(1)} %collective-permute-done.42.refs_1_), channel_id=1, source_target_pairs={{0,2},{1,5},{2,0},{3,7},{4,6},{5,1},{6,4},{7,3},{8,10},{9,13},{10,... | collective-permute-start | bytes 1572872 | tf_op jit(solution)/shard_map/ppermute | solution.py:755
  (40 other events, 374.7 us)

commit v4 on v3

--- a/solution.py
+++ b/solution.py
@@ -13,11 +13,13 @@
 HALO_WIDTHS = (512, 512)
 TILES = 2
 LAST = ("q", "p")
-ORDER = "K O d0 d1 G d0 d1 H B d0 d1 t h d0 d1 b t h d0 d1 t h e t h x0 x1 p0 p1 t R F P"
+ORDER = (
+    "K", "O", "d0", "d1", "G", "d0", "d1", "H", "B", "d0", "d1", "t", "h", "d0", "d1", "b", "t",
+    "h", "d0", "d1", "t", "h", "e", "x0", "t", "p0", "h", "x1", "p1", "t", "R", "t", "F", "P",
+)
 
 FREE = pl.CostEstimate(flops=0, bytes_accessed=0, transcendentals=0)
 LARGE = pl.CostEstimate(flops=5_000_000_000, bytes_accessed=0, transcendentals=0)
-SMALL = pl.CostEstimate(flops=0, bytes_accessed=0, transcendentals=0)
 HBM = pl.BlockSpec(memory_space=pltpu.HBM)
 SMEM = pl.BlockSpec(memory_space=pltpu.SMEM)
 VMEM = pl.BlockSpec(memory_space=pltpu.VMEM)
@@ -130,9 +132,9 @@
     out[rows:, :] = received[...]
 
 
-def stack_rows(own, received, cost=FREE):
+def stack_rows(own, received):
     rows, w = own.shape
-    return call(stack_rows_kernel, shape_of((2 * rows, w), own.dtype), "stack_rows", cost=cost)(
+    return call(stack_rows_kernel, shape_of((2 * rows, w), own.dtype), "stack_rows")(
         own, received
     )
 
@@ -507,10 +509,10 @@
         out[...] = (own[part, :].astype(F32) + received[part, :].astype(F32)).astype(BF)
 
 
-def fold(own, received, v, cost=FREE):
+def fold(own, received, v):
     rows, w = own.shape
     out = shape_of((rows // 2, w), BF)
-    return call(fold_kernel, (out, out), "fold", in_specs=[SMEM, VMEM, VMEM], cost=cost)(
+    return call(fold_kernel, (out, out), "fold", in_specs=[SMEM, VMEM, VMEM])(
         scalars(v), own, received
     )
 
@@ -519,8 +521,8 @@
     out[...] = (own[...].astype(F32) + received[...].astype(F32)).astype(BF)
 
 
-def total_of(own, received, cost=FREE):
-    return call(total_kernel, shape_of(own.shape, BF), "total", cost=cost)(own, received)
+def total_of(own, received):
+    return call(total_kernel, shape_of(own.shape, BF), "total")(own, received)
 
 
 def join_kernel(where, own, received, out):
@@ -529,14 +531,13 @@
         out[pl.ds(pl.multiple_of(side * rows, rows), rows), :] = x[...]
 
 
-def join(own, received, v, cost=FREE):
+def join(own, received, v):
     rows, w = own.shape
     return call(
         join_kernel,
         shape_of((2 * rows, w), BF),
         "join",
         in_specs=[SMEM, VMEM, VMEM],
-        cost=cost,
     )(scalars(v), own, received)
 
 
@@ -788,14 +789,14 @@
     halo_rows = sends * size
     chip_rows = 2 * sends
 
-    def gather_halo(k, x):
+    def gather_halo(x):
         for b in reversed(axes):
             received = along(x, b)
             yield
-            x = stack_rows(x, arrive(received), SMALL if k else FREE)
+            x = stack_rows(x, arrive(received))
         return x
 
-    generators = {k: gather_halo(k, x) for k, x in enumerate(outgoing)}
+    generators = {k: gather_halo(x) for k, x in enumerate(outgoing)}
     advance, halo = start(generators)
 
     def hop():
@@ -857,7 +858,6 @@
     dz_pair = arrive(dz_pair)
 
     def weight_gradient(t):
-        cost = SMALL if t else FREE
         received = along(weight_part(*away, dz_keep, dz_pair, t), "p")
         yield
         part = weight_part(*keep, dz_keep, dz_pair, t)
@@ -865,15 +865,15 @@
         yield
         received = arrive(received)
         for b in axes[2:]:
-            out, part = fold(part, received, bit(b), cost)
+            out, part = fold(part, received, bit(b))
             received = along(out, b)
             yield
             received = arrive(received)
-        part = total_of(part, received, cost)
+        part = total_of(part, received)
         for b in others[::-1] + [LAST[0]]:
             received = along(part, b)
             yield
-            part = join(part, arrive(received), bit(b), cost)
+            part = join(part, arrive(received), bit(b))
         return part
 
     def reduce_halo():
@@ -915,7 +915,7 @@
 
     across, pair, here = [None] * TILES, [None] * TILES, [None] * TILES
     here_across, here_pair, pair_across = [None] * TILES, [None] * TILES, [None] * TILES
-    for action in ORDER.split():
+    for action in ORDER:
         if action == "K":
             keep = arrive(*fetch(same, *aggs))
             for k in generators:

time: 193 us -> 189 us (0.979)
  waiting for transfers between devices: 76.7 us -> 71.4 us
  starting transfers between devices: 48.1 us -> 51.5 us
    ppermute x35, waiting for transfers between devices: 73.4 us -> 68.2 us  [along(): return lax.ppermute(x, 'dom', [(i, peer(i, b)) for i in range(size)])]
    ppermute x35, starting transfers between devices: 44.4 us -> 47 us  [along(): return lax.ppermute(x, 'dom', [(i, peer(i, b)) for i in range(size)])]
    unnamed x40 -> x36, local copies, waits for them, and re-layouts: 6.71 us -> 5.91 us
    pallas_call x26 -> x27, Pallas kernels: 9 us -> 9.01 us  [run(): return kernel(*operands)]
where the time goes in v4:
time: 189 us
  waiting for transfers between devices  71.4 us (38%)
  Pallas kernels  53.1 us (28%)
  starting transfers between devices  51.5 us (27%)
  local copies, waits for them, and re-layouts  7.65 us (4%)
  other arithmetic  3.69 us (2%)
    ppermute x35, waiting for transfers between devices, along(): return lax.ppermute(x, 'dom', [(i, peer(i, b)) for i in range(size)])  68.2 us
    ppermute x35, starting transfers between devices, along(): return lax.ppermute(x, 'dom', [(i, peer(i, b)) for i in range(size)])  47 us
    pallas_call x27, Pallas kernels, run(): kernel(*[pltpu.with_memory_space_constraint(x, pltpu.HBM) if spec is HBM...  44.1 us
    pallas_call x27, Pallas kernels, run(): return kernel(*operands)  9.01 us
    unnamed x36, local copies, waits for them, and re-layouts  5.91 us
    ppermute x17, starting transfers between devices, swap(): return lax.ppermute(x, 'dom', [(i, i ^ 1) for i in range(size)])  4.55 us
  transfers between devices with their start and end apart: 52, of which 28 were waited for; matrix products, arithmetic and copies ran while one was open for 3% of the time, Pallas kernels for 23%

profile of v4, /device:TPU:0, one launch (start us, length us, event | category | flops | bytes accessed | tf_op | source)
XLA Modules:
  0.0 188.8 jit_solution(2682839948252601803)
XLA Ops:
  5.4 3.7 %collective-permute-start.2 = (bf16[64,512]{1,0:T(8,128)(2,1)S(1)}, bf16[64,512]{1,0:T(8,128)(2,1)S(1)}, u32[]{:S(2)}, u32[]{:S(2)}) collective-permute-start(bf16[64,512]{1,0:T(8,128)(2,1)S(1)} %get-tuple-element.203.own), channel_id=1, source_target_pairs={{0,16},{1,17},{2,18},{3,19},{4,20},{5,21},{6,22},{7,23},{8,24},{9,... | collective-permute-start | bytes 196616 | tf_op jit(solution)/shard_map/ppermute | solution.py:756
  10.8 2.6 %collective-permute-done.2.received = bf16[64,512]{1,0:T(8,128)(2,1)S(1)} collective-permute-done((bf16[64,512]{1,0:T(8,128)(2,1)S(1)}, bf16[64,512]{1,0:T(8,128)(2,1)S(1)}, u32[]{:S(2)}, u32[]{:S(2)}) %collective-permute-start.2) | collective-permute-done | bytes 65568 | tf_op jit(solution)/shard_map/ppermute | solution.py:756
  13.4 2.6 %collective-permute-done.1.received = bf16[64,512]{1,0:T(8,128)(2,1)S(1)} collective-permute-done((bf16[64,512]{1,0:T(8,128)(2,1)S(1)}, bf16[64,512]{1,0:T(8,128)(2,1)S(1)}, u32[]{:S(2)}, u32[]{:S(2)}) %collective-permute-start.1) | collective-permute-done | bytes 65568 | tf_op jit(solution)/shard_map/ppermute | solution.py:756
  19.1 2.6 %counts.2 = (bf16[256,1024]{1,0:T(8,128)(2,1)S(1)}, bf16[256,256]{1,0:T(8,128)(2,1)S(1)}, f32[256,128]{1,0:T(8,128)S(1)}) custom-call(s32[256,17]{1,0:T(8,128)S(1)} %copy.32.packed, s32[1,1024]{1,0:T(1,128)S(1)} %fusion.label), custom_call_target="tpu_custom_call" | custom-call | tf_op jit(solution)/shard_map/counts/pallas_call | solution.py:50
  25.2 2.6 %counts.3 = (bf16[256,1024]{1,0:T(8,128)(2,1)S(1)}, bf16[256,256]{1,0:T(8,128)(2,1)S(1)}, f32[256,128]{1,0:T(8,128)S(1)}) custom-call(s32[256,17]{1,0:T(8,128)S(1)} %collective-permute-done.3.packed, s32[1,1024]{1,0:T(1,128)S(1)} %fusion.label), custom_call_target="tpu_custom_call" | custom-call | tf_op jit(solution)/shard_map/counts/pallas_call | solution.py:50
  29.9 2.8 %collective-permute-done.10.received = bf16[256,512]{1,0:T(8,128)(2,1)S(1)} collective-permute-done((bf16[256,512]{1,0:T(8,128)(2,1)S(1)}, bf16[256,512]{1,0:T(8,128)(2,1)S(1)}, u32[]{:S(2)}, u32[]{:S(2)}) %collective-permute-start.10) | collective-permute-done | bytes 262176 | tf_op jit(solution)/shard_map/ppermute | solution.py:756
  34.3 3.2 %collective-permute-done.9.received = bf16[512,512]{1,0:T(8,128)(2,1)S(1)} collective-permute-done((bf16[512,512]{1,0:T(8,128)(2,1)S(1)}, bf16[512,512]{1,0:T(8,128)(2,1)S(1)}, u32[]{:S(2)}, u32[]{:S(2)}) %collective-permute-start.9) | collective-permute-done | bytes 524320 | tf_op jit(solution)/shard_map/ppermute | solution.py:756
  37.5 5.6 %collective-permute-done.11.received = bf16[512,512]{1,0:T(8,128)(2,1)S(1)} collective-permute-done((bf16[512,512]{1,0:T(8,128)(2,1)S(1)}, bf16[512,512]{1,0:T(8,128)(2,1)S(1)}, u32[]{:S(2)}, u32[]{:S(2)}) %collective-permute-start.11) | collective-permute-done | bytes 524320 | tf_op jit(solution)/shard_map/ppermute | solution.py:756
  43.3 2.9 %aggregate.1.mine = bf16[512,1024]{1,0:T(8,128)(2,1)S(1)} custom-call(s32[1]{0:T(128)} %bitcast.where, bf16[256,2048]{1,0:T(8,128)(2,1)} %features.3, bf16[256,2048]{1,0:T(8,128)(2,1)} %copy-done.15, bf16[256,1024]{1,0:T(8,128)(2,1)S(1)} %get-tuple-element.214.refs_0_.own, bf16[256,256]{1,0:T(8,128)(2,1)S(1)} %get-tuple-element.229.refs_1_.own, ...), custom_call_target="tpu_custom_call" | custom-call | tf_op jit(solution)/shard_map/aggregate/pallas_call | solution.py:51
  50.5 7.5 %forward.1 = (f32[512,1024]{1,0:T(8,128)}, f32[8,1024]{1,0:T(8,128)S(1)}) custom-call(s32[1]{0:T(128)} %bitcast.where, bf16[512,1024]{1,0:T(8,128)(2,1)S(1)} %aggregate.1.mine, bf16[512,1024]{1,0:T(8,128)(2,1)S(1)} %collective-permute-done.12.other, f32[3,2048]{1,0:T(4,128)S(1)} %pad_maximum_fusion.constants, ...), custom_call_target="tpu_custom_call" | custom-call | tf_op jit(solution)/shard_map/forward/pallas_call | solution.py:51
  57.9 2.3 %collective-permute-start.13 = (f32[8,1024]{1,0:T(8,128)S(1)}, f32[8,1024]{1,0:T(8,128)S(1)}, u32[]{:S(2)}, u32[]{:S(2)}) collective-permute-start(f32[8,1024]{1,0:T(8,128)S(1)} %get-tuple-element.247.own), channel_id=1, source_target_pairs={{0,16},{1,17},{2,18},{3,19},{4,20},{5,21},{6,22},{7,23},{8,24},{9,... | collective-permute-start | bytes 98312 | tf_op jit(solution)/shard_map/ppermute | solution.py:756
  64.1 2.9 %collective-permute-done.15.received = f32[8,1024]{1,0:T(8,128)S(1)} collective-permute-done((f32[8,1024]{1,0:T(8,128)S(1)}, f32[8,1024]{1,0:T(8,128)S(1)}, u32[]{:S(2)}, u32[]{:S(2)}) %collective-permute-start.15) | collective-permute-done | bytes 32800 | tf_op jit(solution)/shard_map/ppermute | solution.py:756
  68.5 2.9 %collective-permute-done.16.received = f32[8,1024]{1,0:T(8,128)S(1)} collective-permute-done((f32[8,1024]{1,0:T(8,128)S(1)}, f32[8,1024]{1,0:T(8,128)S(1)}, u32[]{:S(2)}, u32[]{:S(2)}) %collective-permute-start.16) | collective-permute-done | bytes 32800 | tf_op jit(solution)/shard_map/ppermute | solution.py:756
  72.8 2.7 %collective-permute-done.17.received = f32[8,1024]{1,0:T(8,128)S(1)} collective-permute-done((f32[8,1024]{1,0:T(8,128)S(1)}, f32[8,1024]{1,0:T(8,128)S(1)}, u32[]{:S(2)}, u32[]{:S(2)}) %collective-permute-start.17) | collective-permute-done | bytes 32800 | tf_op jit(solution)/shard_map/ppermute | solution.py:756
  75.5 3.2 %dz.2 = bf16[512,512]{1,0:T(8,128)(2,1)} custom-call(s32[2]{0:T(128)S(1)} %pad_add_fusion.1.where, f32[8,1024]{1,0:T(8,128)S(1)} %merge.7.stats_ref, f32[3,2048]{1,0:T(4,128)S(1)} %pad_maximum_fusion.constants, f32[256,128]{1,0:T(8,128)S(1)} %get-tuple-element.230.refs_2_.own_factors, f32[256,128]{1,0:T(8,128)S(1)} %get-tuple-element.232.refs_5_.other_factors, ...), custom_call_target="tpu_custom_call" | custom-call | tf_op jit(solution)/shard_map/dz/pallas_call | solution.py:51
  79.5 2.4 %dz.3 = bf16[512,512]{1,0:T(8,128)(2,1)S(1)} custom-call(s32[2]{0:T(128)S(1)} %pad_add_fusion.2.where, f32[8,1024]{1,0:T(8,128)S(1)} %merge.7.stats_ref, f32[3,2048]{1,0:T(4,128)S(1)} %pad_maximum_fusion.constants, f32[256,128]{1,0:T(8,128)S(1)} %get-tuple-element.230.refs_2_.own_factors, f32[256,128]{1,0:T(8,128)S(1)} %get-tuple-element.232.refs_5_.other_factors, ...), custom_call_target="tpu_custom_call" | custom-call | tf_op jit(solution)/shard_map/dz/pallas_call | solution.py:51
  83.6 4.6 %collective-permute-done.19.dz_pair = bf16[512,512]{1,0:T(8,128)(2,1)S(1)} collective-permute-done((bf16[512,512]{1,0:T(8,128)(2,1)}, bf16[512,512]{1,0:T(8,128)(2,1)S(1)}, u32[]{:S(2)}, u32[]{:S(2)}) %collective-permute-start.19) | collective-permute-done | bytes 524320 | tf_op jit(solution)/shard_map/ppermute | solution.py:756
  91.9 3.7 %outputs.1 = (bf16[512,1024]{1,0:T(8,128)(2,1)S(1)}, bf16[256,1024]{1,0:T(8,128)(2,1)S(1)}, bf16[256,1024]{1,0:T(8,128)(2,1)S(1)}, f32[8,1024]{1,0:T(8,128)S(1)}) custom-call(s32[1]{0:T(128)} %bitcast.where, f32[8,1024]{1,0:T(8,128)S(1)} %merge.7.stats_ref, f32[3,2048]{1,0:T(4,128)S(1)} %pad_maximum_fusion.constants, ...), custom_call_target="tpu_custom_call" | custom-call | tf_op jit(solution)/shard_map/outputs/pallas_call | solution.py:51
  100.7 3.2 %collective-permute-done.20.received = bf16[512,512]{1,0:T(8,128)(2,1)S(1)} collective-permute-done((bf16[512,512]{1,0:T(8,128)(2,1)S(1)}, bf16[512,512]{1,0:T(8,128)(2,1)S(1)}, u32[]{:S(2)}, u32[]{:S(2)}) %collective-permute-start.20) | collective-permute-done | bytes 524320 | tf_op jit(solution)/shard_map/ppermute | solution.py:756
  106.5 5.1 %collective-permute-done.22.received = bf16[256,512]{1,0:T(8,128)(2,1)S(1)} collective-permute-done((bf16[256,512]{1,0:T(8,128)(2,1)S(1)}, bf16[256,512]{1,0:T(8,128)(2,1)S(1)}, u32[]{:S(2)}, u32[]{:S(2)}) %collective-permute-start.22) | collective-permute-done | bytes 262176 | tf_op jit(solution)/shard_map/ppermute | solution.py:756
  115.9 3.2 %collective-permute-done.26.received = bf16[128,512]{1,0:T(8,128)(2,1)S(1)} collective-permute-done((bf16[128,512]{1,0:T(8,128)(2,1)S(1)}, bf16[128,512]{1,0:T(8,128)(2,1)S(1)}, u32[]{:S(2)}, u32[]{:S(2)}) %collective-permute-start.26) | collective-permute-done | bytes 131104 | tf_op jit(solution)/shard_map/ppermute | solution.py:756
  119.8 6.0 %collective-permute-done.25.received = bf16[128,512]{1,0:T(8,128)(2,1)S(1)} collective-permute-done((bf16[128,512]{1,0:T(8,128)(2,1)S(1)}, bf16[128,512]{1,0:T(8,128)(2,1)S(1)}, u32[]{:S(2)}, u32[]{:S(2)}) %collective-permute-start.25) | collective-permute-done | bytes 131104 | tf_op jit(solution)/shard_map/ppermute | solution.py:756
  126.7 2.1 %collective-permute-start.27 = (bf16[256,1024]{1,0:T(8,128)(2,1)S(1)}, bf16[256,1024]{1,0:T(8,128)(2,1)S(1)}, u32[]{:S(2)}, u32[]{:S(2)}) collective-permute-start(bf16[256,1024]{1,0:T(8,128)(2,1)S(1)} %get-tuple-element.316), channel_id=1, source_target_pairs={{0,4},{1,9},{2,6},{3,11},{4,0},{5,13},{6,2},{7,15},{8,12},{9,1},{1... | collective-permute-start | bytes 1572872 | tf_op jit(solution)/shard_map/ppermute | solution.py:756
  128.8 4.2 %collective-permute-done.31.received = bf16[128,512]{1,0:T(8,128)(2,1)S(1)} collective-permute-done((bf16[128,512]{1,0:T(8,128)(2,1)S(1)}, bf16[128,512]{1,0:T(8,128)(2,1)S(1)}, u32[]{:S(2)}, u32[]{:S(2)}) %collective-permute-start.31) | collective-permute-done | bytes 131104 | tf_op jit(solution)/shard_map/ppermute | solution.py:756
  136.0 3.5 %collective-permute-done.35.received = bf16[256,512]{1,0:T(8,128)(2,1)S(1)} collective-permute-done((bf16[256,512]{1,0:T(8,128)(2,1)S(1)}, bf16[256,512]{1,0:T(8,128)(2,1)S(1)}, u32[]{:S(2)}, u32[]{:S(2)}) %collective-permute-start.35) | collective-permute-done | bytes 262176 | tf_op jit(solution)/shard_map/ppermute | solution.py:756
  139.6 2.7 %collective-permute-done.34.received = bf16[256,512]{1,0:T(8,128)(2,1)S(1)} collective-permute-done((bf16[256,512]{1,0:T(8,128)(2,1)S(1)}, bf16[256,512]{1,0:T(8,128)(2,1)S(1)}, u32[]{:S(2)}, u32[]{:S(2)}) %collective-permute-start.34) | collective-permute-done | bytes 262176 | tf_op jit(solution)/shard_map/ppermute | solution.py:756
  149.3 4.9 %collective-permute-done.33.received = bf16[128,1024]{1,0:T(8,128)(2,1)S(1)} collective-permute-done((bf16[128,1024]{1,0:T(8,128)(2,1)S(1)}, bf16[128,1024]{1,0:T(8,128)(2,1)S(1)}, u32[]{:S(2)}, u32[]{:S(2)}) %collective-permute-start.33) | collective-permute-done | bytes 262176 | tf_op jit(solution)/shard_map/ppermute | solution.py:756
  158.0 2.8 %collective-permute-start.36 = (bf16[64,1024]{1,0:T(8,128)(2,1)S(1)}, bf16[64,1024]{1,0:T(8,128)(2,1)S(1)}, u32[]{:S(2)}, u32[]{:S(2)}) collective-permute-start(bf16[64,1024]{1,0:T(8,128)(2,1)S(1)} %get-tuple-element.338), channel_id=1, source_target_pairs={{0,16},{1,17},{2,18},{3,19},{4,20},{5,21},{6,22},{7,23},{8,24},{9,... | collective-permute-start | bytes 393224 | tf_op jit(solution)/shard_map/ppermute | solution.py:756
  161.9 3.4 %place.3.refs_8_ = f32[2048,2048]{1,0:T(8,128)} custom-call(s32[12]{0:T(128)S(1)} %stack.182.where, bf16[512,512]{1,0:T(8,128)(2,1)S(1)} %join.6.refs_0_, bf16[512,512]{1,0:T(8,128)(2,1)S(1)} %join.7.refs_1_, bf16[512,512]{1,0:T(8,128)(2,1)S(1)} %copy-done.6, bf16[512,512]{1,0:T(8,128)(2,1)} %collective-permute-done.40.refs_3_), custom_call_target="tpu_custom_call" | custom-call | tf_op jit(solution)/shard_map/place/pallas_call | solution.py:51
  170.3 7.8 %finish.1 = (bf16[256,2048]{1,0:T(8,128)(2,1)}, bf16[256,2048]{1,0:T(8,128)(2,1)}, f32[8,2048]{1,0:T(8,128)S(1)}) custom-call(s32[1]{0:T(128)} %bitcast.where, s32[32,1]{1,0:T(8,128)S(1)} %copy.33.rows, bf16[64,1024]{1,0:T(8,128)(2,1)S(1)} %total.5.back, bf16[32,1024]{1,0:T(8,128)(2,1)S(1)} %collective-permute-done.41.back_in, ...), custom_call_target="tpu_custom_call" | custom-call | tf_op jit(solution)/shard_map/finish/pallas_call | solution.py:51
  178.2 4.5 %place.4.refs_4_ = f32[2048,2048]{1,0:T(8,128)} custom-call(s32[24]{0:T(128)S(1)} %stack.194.where, bf16[512,512]{1,0:T(8,128)(2,1)S(1)} %collective-permute-done.38.refs_0_, bf16[512,512]{1,0:T(8,128)(2,1)S(1)} %collective-permute-done.43.refs_1_, bf16[512,512]{1,0:T(8,128)(2,1)} %collective-permute-done.45.refs_2_, ...), custom_call_target="tpu_custom_call", output_to_operand_aliasing={{}: (9, {})} | custom-call | tf_op jit(solution)/shard_map/place/pallas_call | solution.py:51
  186.0 2.6 %place.5 = f32[2048,2048]{1,0:T(8,128)} custom-call(s32[12]{0:T(128)S(1)} %stack.193.where, bf16[512,512]{1,0:T(8,128)(2,1)S(1)} %collective-permute-done.44.refs_0_, bf16[512,512]{1,0:T(8,128)(2,1)S(1)} %collective-permute-done.49.refs_1_, bf16[512,512]{1,0:T(8,128)(2,1)S(1)} %collective-permute-done.50.refs_2_, ...), custom_call_target="tpu_custom_call", output_to_operand_aliasing={{}: (5, {})} | custom-call | tf_op jit(solution)/shard_map/place/pallas_call | solution.py:51
  (180 shorter events, 70.6 us)
Async XLA Ops:
  0.6 23.6 %collective-permute-start.4 = (bf16[256,2048]{1,0:T(8,128)(2,1)}, bf16[256,2048]{1,0:T(8,128)(2,1)S(1)}, u32[]{:S(2)}, u32[]{:S(2)}) collective-permute-start(bf16[256,2048]{1,0:T(8,128)(2,1)} %features.3), channel_id=1, source_target_pairs={{0,1},{1,0},{2,3},{3,2},{4,5},{5,4},{6,7},{7,6},{8,9},{9,8},{10,11... | collective-permute-start | bytes 3145736 | tf_op jit(solution)/shard_map/ppermute | solution.py:759
  1.1 24.0 %collective-permute-start.5 = (bf16[256,2048]{1,0:T(8,128)(2,1)}, bf16[256,2048]{1,0:T(8,128)(2,1)}, u32[]{:S(2)}, u32[]{:S(2)}) collective-permute-start(bf16[256,2048]{1,0:T(8,128)(2,1)} %cotangent.7), channel_id=1, source_target_pairs={{0,1},{1,0},{2,3},{3,2},{4,5},{5,4},{6,7},{7,6},{8,9},{9,8},{10,11... | collective-permute-start | bytes 3145736 | tf_op jit(solution)/shard_map/ppermute | solution.py:759
  5.4 8.0 %collective-permute-start.2 = (bf16[64,512]{1,0:T(8,128)(2,1)S(1)}, bf16[64,512]{1,0:T(8,128)(2,1)S(1)}, u32[]{:S(2)}, u32[]{:S(2)}) collective-permute-start(bf16[64,512]{1,0:T(8,128)(2,1)S(1)} %get-tuple-element.203.own), channel_id=1, source_target_pairs={{0,16},{1,17},{2,18},{3,19},{4,20},{5,21},{6,22},{7,23},{8,24},{9,... | collective-permute-start | bytes 196616 | tf_op jit(solution)/shard_map/ppermute | solution.py:756
  23.5 9.3 %collective-permute-start.10 = (bf16[256,512]{1,0:T(8,128)(2,1)S(1)}, bf16[256,512]{1,0:T(8,128)(2,1)S(1)}, u32[]{:S(2)}, u32[]{:S(2)}) collective-permute-start(bf16[256,512]{1,0:T(8,128)(2,1)S(1)} %stack_rows.12.own), channel_id=1, source_target_pairs={{0,4},{1,9},{2,6},{3,11},{4,0},{5,13},{6,2},{7,15},{8,12},{9,1},{1... | collective-permute-start | bytes 786440 | tf_op jit(solution)/shard_map/ppermute | solution.py:756
  28.3 9.2 %collective-permute-start.9 = (bf16[512,512]{1,0:T(8,128)(2,1)S(1)}, bf16[512,512]{1,0:T(8,128)(2,1)S(1)}, u32[]{:S(2)}, u32[]{:S(2)}) collective-permute-start(bf16[512,512]{1,0:T(8,128)(2,1)S(1)} %stack_rows.11.own), channel_id=1, source_target_pairs={{0,2},{1,5},{2,0},{3,7},{4,6},{5,1},{6,4},{7,3},{8,10},{9,13},{10,... | collective-permute-start | bytes 1572872 | tf_op jit(solution)/shard_map/ppermute | solution.py:756
  32.8 10.4 %collective-permute-start.11 = (bf16[512,512]{1,0:T(8,128)(2,1)S(1)}, bf16[512,512]{1,0:T(8,128)(2,1)S(1)}, u32[]{:S(2)}, u32[]{:S(2)}) collective-permute-start(bf16[512,512]{1,0:T(8,128)(2,1)S(1)} %stack_rows.14.own), channel_id=1, source_target_pairs={{0,2},{1,5},{2,0},{3,7},{4,6},{5,1},{6,4},{7,3},{8,10},{9,13},{10,... | collective-permute-start | bytes 1572872 | tf_op jit(solution)/shard_map/ppermute | solution.py:756
  46.3 15.0 %collective-permute-start.14 = (bf16[512,1024]{1,0:T(8,128)(2,1)S(1)}, bf16[512,1024]{1,0:T(8,128)(2,1)}, u32[]{:S(2)}, u32[]{:S(2)}) collective-permute-start(bf16[512,1024]{1,0:T(8,128)(2,1)S(1)} %aggregate.1.mine), channel_id=1, source_target_pairs={{0,2},{1,5},{2,0},{3,7},{4,6},{5,1},{6,4},{7,3},{8,10},{9,13},{10,... | collective-permute-start | bytes 3145736 | tf_op jit(solution)/shard_map/ppermute | solution.py:756
  48.9 23.9 %collective-permute-start.18 = (bf16[512,1024]{1,0:T(8,128)(2,1)S(1)}, bf16[512,1024]{1,0:T(8,128)(2,1)}, u32[]{:S(2)}, u32[]{:S(2)}) collective-permute-start(bf16[512,1024]{1,0:T(8,128)(2,1)S(1)} %collective-permute-done.12.other), channel_id=1, source_target_pairs={{0,2},{1,5},{2,0},{3,7},{4,6},{5,1},{6,4},{7,3},{8,10},{9,13},{10,... | collective-permute-start | bytes 3145736 | tf_op jit(solution)/shard_map/ppermute | solution.py:756
  78.7 9.5 %collective-permute-start.19 = (bf16[512,512]{1,0:T(8,128)(2,1)}, bf16[512,512]{1,0:T(8,128)(2,1)S(1)}, u32[]{:S(2)}, u32[]{:S(2)}) collective-permute-start(bf16[512,512]{1,0:T(8,128)(2,1)} %dz.2), channel_id=1, source_target_pairs={{0,2},{1,5},{2,0},{3,7},{4,6},{5,1},{6,4},{7,3},{8,10},{9,13},{10,... | collective-permute-start | bytes 1572872 | tf_op jit(solution)/shard_map/ppermute | solution.py:756
  89.0 10.5 %collective-permute-start.21 = (bf16[512,512]{1,0:T(8,128)(2,1)S(1)}, bf16[512,512]{1,0:T(8,128)(2,1)S(1)}, u32[]{:S(2)}, u32[]{:S(2)}) collective-permute-start(bf16[512,512]{1,0:T(8,128)(2,1)S(1)} %weight_part.7), channel_id=1, source_target_pairs={{0,4},{1,9},{2,6},{3,11},{4,0},{5,13},{6,2},{7,15},{8,12},{9,1},{1... | collective-permute-start | bytes 1572872 | tf_op jit(solution)/shard_map/ppermute | solution.py:756
  91.2 12.6 %collective-permute-start.20 = (bf16[512,512]{1,0:T(8,128)(2,1)S(1)}, bf16[512,512]{1,0:T(8,128)(2,1)S(1)}, u32[]{:S(2)}, u32[]{:S(2)}) collective-permute-start(bf16[512,512]{1,0:T(8,128)(2,1)S(1)} %weight_part.6), channel_id=1, source_target_pairs={{0,4},{1,9},{2,6},{3,11},{4,0},{5,13},{6,2},{7,15},{8,12},{9,1},{1... | collective-permute-start | bytes 1572872 | tf_op jit(solution)/shard_map/ppermute | solution.py:756
  104.0 7.7 %collective-permute-start.22 = (bf16[256,512]{1,0:T(8,128)(2,1)S(1)}, bf16[256,512]{1,0:T(8,128)(2,1)S(1)}, u32[]{:S(2)}, u32[]{:S(2)}) collective-permute-start(bf16[256,512]{1,0:T(8,128)(2,1)S(1)} %get-tuple-element.292), channel_id=1, source_target_pairs={{0,8},{1,3},{2,10},{3,1},{4,12},{5,7},{6,14},{7,5},{8,0},{9,11},{1... | collective-permute-start | bytes 786440 | tf_op jit(solution)/shard_map/ppermute | solution.py:756
  111.7 14.8 %collective-permute-start.24 = (bf16[512,1024]{1,0:T(8,128)(2,1)S(1)}, bf16[512,1024]{1,0:T(8,128)(2,1)S(1)}, u32[]{:S(2)}, u32[]{:S(2)}) collective-permute-start(bf16[512,1024]{1,0:T(8,128)(2,1)S(1)} %back_part.2), channel_id=1, source_target_pairs={{0,2},{1,5},{2,0},{3,7},{4,6},{5,1},{6,4},{7,3},{8,10},{9,13},{10,... | collective-permute-start | bytes 3145736 | tf_op jit(solution)/shard_map/ppermute | solution.py:756
  111.7 7.3 %collective-permute-start.26 = (bf16[128,512]{1,0:T(8,128)(2,1)S(1)}, bf16[128,512]{1,0:T(8,128)(2,1)S(1)}, u32[]{:S(2)}, u32[]{:S(2)}) collective-permute-start(bf16[128,512]{1,0:T(8,128)(2,1)S(1)} %get-tuple-element.305), channel_id=1, source_target_pairs={{0,16},{1,17},{2,18},{3,19},{4,20},{5,21},{6,22},{7,23},{8,24},{9,... | collective-permute-start | bytes 393224 | tf_op jit(solution)/shard_map/ppermute | solution.py:756
  113.8 12.0 %collective-permute-start.25 = (bf16[128,512]{1,0:T(8,128)(2,1)S(1)}, bf16[128,512]{1,0:T(8,128)(2,1)S(1)}, u32[]{:S(2)}, u32[]{:S(2)}) collective-permute-start(bf16[128,512]{1,0:T(8,128)(2,1)S(1)} %get-tuple-element.302), channel_id=1, source_target_pairs={{0,16},{1,17},{2,18},{3,19},{4,20},{5,21},{6,22},{7,23},{8,24},{9,... | collective-permute-start | bytes 393224 | tf_op jit(solution)/shard_map/ppermute | solution.py:756
  114.9 20.2 %collective-permute-start.29 = (bf16[256,1024]{1,0:T(8,128)(2,1)S(1)}, bf16[256,1024]{1,0:T(8,128)(2,1)S(1)}, u32[]{:S(2)}, u32[]{:S(2)}) collective-permute-start(bf16[256,1024]{1,0:T(8,128)(2,1)S(1)} %get-tuple-element.318), channel_id=1, source_target_pairs={{0,1},{1,0},{2,3},{3,2},{4,5},{5,4},{6,7},{7,6},{8,9},{9,8},{10,11... | collective-permute-start | bytes 1572872 | tf_op jit(solution)/shard_map/ppermute | solution.py:759
  115.4 19.8 %collective-permute-start.28 = (bf16[256,1024]{1,0:T(8,128)(2,1)S(1)}, bf16[256,1024]{1,0:T(8,128)(2,1)S(1)}, u32[]{:S(2)}, u32[]{:S(2)}) collective-permute-start(bf16[256,1024]{1,0:T(8,128)(2,1)S(1)} %get-tuple-element.317), channel_id=1, source_target_pairs={{0,1},{1,0},{2,3},{3,2},{4,5},{5,4},{6,7},{7,6},{8,9},{9,8},{10,11... | collective-permute-start | bytes 1572872 | tf_op jit(solution)/shard_map/ppermute | solution.py:759
  119.1 9.7 %collective-permute-start.32 = (bf16[128,512]{1,0:T(8,128)(2,1)S(1)}, bf16[128,512]{1,0:T(8,128)(2,1)S(1)}, u32[]{:S(2)}, u32[]{:S(2)}) collective-permute-start(bf16[128,512]{1,0:T(8,128)(2,1)S(1)} %total.4.own), channel_id=1, source_target_pairs={{0,16},{1,17},{2,18},{3,19},{4,20},{5,21},{6,22},{7,23},{8,24},{9,... | collective-permute-start | bytes 393224 | tf_op jit(solution)/shard_map/ppermute | solution.py:756
  125.8 7.3 %collective-permute-start.31 = (bf16[128,512]{1,0:T(8,128)(2,1)S(1)}, bf16[128,512]{1,0:T(8,128)(2,1)S(1)}, u32[]{:S(2)}, u32[]{:S(2)}) collective-permute-start(bf16[128,512]{1,0:T(8,128)(2,1)S(1)} %total.3.own), channel_id=1, source_target_pairs={{0,16},{1,17},{2,18},{3,19},{4,20},{5,21},{6,22},{7,23},{8,24},{9,... | collective-permute-start | bytes 393224 | tf_op jit(solution)/shard_map/ppermute | solution.py:756
  126.7 9.3 %collective-permute-start.27 = (bf16[256,1024]{1,0:T(8,128)(2,1)S(1)}, bf16[256,1024]{1,0:T(8,128)(2,1)S(1)}, u32[]{:S(2)}, u32[]{:S(2)}) collective-permute-start(bf16[256,1024]{1,0:T(8,128)(2,1)S(1)} %get-tuple-element.316), channel_id=1, source_target_pairs={{0,4},{1,9},{2,6},{3,11},{4,0},{5,13},{6,2},{7,15},{8,12},{9,1},{1... | collective-permute-start | bytes 1572872 | tf_op jit(solution)/shard_map/ppermute | solution.py:756
  139.5 16.2 %collective-permute-start.39 = (bf16[512,512]{1,0:T(8,128)(2,1)S(1)}, bf16[512,512]{1,0:T(8,128)(2,1)S(1)}, u32[]{:S(2)}, u32[]{:S(2)}) collective-permute-start(bf16[512,512]{1,0:T(8,128)(2,1)S(1)} %join.6.refs_0_), channel_id=1, source_target_pairs={{0,1},{1,0},{2,3},{3,2},{4,5},{5,4},{6,7},{7,6},{8,9},{9,8},{10,11... | collective-permute-start | bytes 1572872 | tf_op jit(solution)/shard_map/ppermute | solution.py:759
  142.3 15.7 %collective-permute-start.40 = (bf16[512,512]{1,0:T(8,128)(2,1)S(1)}, bf16[512,512]{1,0:T(8,128)(2,1)}, u32[]{:S(2)}, u32[]{:S(2)}) collective-permute-start(bf16[512,512]{1,0:T(8,128)(2,1)S(1)} %join.7.refs_1_), channel_id=1, source_target_pairs={{0,1},{1,0},{2,3},{3,2},{4,5},{5,4},{6,7},{7,6},{8,9},{9,8},{10,11... | collective-permute-start | bytes 1572872 | tf_op jit(solution)/shard_map/ppermute | solution.py:759
  142.4 22.9 %collective-permute-start.38 = (bf16[512,512]{1,0:T(8,128)(2,1)S(1)}, bf16[512,512]{1,0:T(8,128)(2,1)S(1)}, u32[]{:S(2)}, u32[]{:S(2)}) collective-permute-start(bf16[512,512]{1,0:T(8,128)(2,1)S(1)} %join.6.refs_0_), channel_id=1, source_target_pairs={{0,4},{1,9},{2,6},{3,11},{4,0},{5,13},{6,2},{7,15},{8,12},{9,1},{1... | collective-permute-start | bytes 1572872 | tf_op jit(solution)/shard_map/ppermute | solution.py:756
  144.0 21.4 %collective-permute-start.37 = (bf16[512,512]{1,0:T(8,128)(2,1)S(1)}, bf16[512,512]{1,0:T(8,128)(2,1)S(1)}, u32[]{:S(2)}, u32[]{:S(2)}) collective-permute-start(bf16[512,512]{1,0:T(8,128)(2,1)S(1)} %join.6.refs_0_), channel_id=1, source_target_pairs={{0,2},{1,5},{2,0},{3,7},{4,6},{5,1},{6,4},{7,3},{8,10},{9,13},{10,... | collective-permute-start | bytes 1572872 | tf_op jit(solution)/shard_map/ppermute | solution.py:756
  154.2 13.3 %collective-permute-start.43 = (bf16[512,512]{1,0:T(8,128)(2,1)S(1)}, bf16[512,512]{1,0:T(8,128)(2,1)S(1)}, u32[]{:S(2)}, u32[]{:S(2)}) collective-permute-start(bf16[512,512]{1,0:T(8,128)(2,1)S(1)} %join.7.refs_1_), channel_id=1, source_target_pairs={{0,4},{1,9},{2,6},{3,11},{4,0},{5,13},{6,2},{7,15},{8,12},{9,1},{1... | collective-permute-start | bytes 1572872 | tf_op jit(solution)/shard_map/ppermute | solution.py:756
  156.5 11.1 %collective-permute-start.42 = (bf16[512,512]{1,0:T(8,128)(2,1)S(1)}, bf16[512,512]{1,0:T(8,128)(2,1)S(1)}, u32[]{:S(2)}, u32[]{:S(2)}) collective-permute-start(bf16[512,512]{1,0:T(8,128)(2,1)S(1)} %join.7.refs_1_), channel_id=1, source_target_pairs={{0,2},{1,5},{2,0},{3,7},{4,6},{5,1},{6,4},{7,3},{8,10},{9,13},{10,... | collective-permute-start | bytes 1572872 | tf_op jit(solution)/shard_map/ppermute | solution.py:756
  158.0 7.4 %collective-permute-start.36 = (bf16[64,1024]{1,0:T(8,128)(2,1)S(1)}, bf16[64,1024]{1,0:T(8,128)(2,1)S(1)}, u32[]{:S(2)}, u32[]{:S(2)}) collective-permute-start(bf16[64,1024]{1,0:T(8,128)(2,1)S(1)} %get-tuple-element.338), channel_id=1, source_target_pairs={{0,16},{1,17},{2,18},{3,19},{4,20},{5,21},{6,22},{7,23},{8,24},{9,... | collective-permute-start | bytes 393224 | tf_op jit(solution)/shard_map/ppermute | solution.py:756
  166.2 16.5 %collective-permute-start.44 = (bf16[512,512]{1,0:T(8,128)(2,1)S(1)}, bf16[512,512]{1,0:T(8,128)(2,1)S(1)}, u32[]{:S(2)}, u32[]{:S(2)}) collective-permute-start(bf16[512,512]{1,0:T(8,128)(2,1)S(1)} %collective-permute-done.38.refs_0_), channel_id=1, source_target_pairs={{0,2},{1,5},{2,0},{3,7},{4,6},{5,1},{6,4},{7,3},{8,10},{9,13},{10,... | collective-permute-start | bytes 1572872 | tf_op jit(solution)/shard_map/ppermute | solution.py:756
  167.5 10.7 %collective-permute-start.46 = (bf16[512,512]{1,0:T(8,128)(2,1)S(1)}, bf16[512,512]{1,0:T(8,128)(2,1)S(1)}, u32[]{:S(2)}, u32[]{:S(2)}) collective-permute-start(bf16[512,512]{1,0:T(8,128)(2,1)S(1)} %collective-permute-done.43.refs_1_), channel_id=1, source_target_pairs={{0,1},{1,0},{2,3},{3,2},{4,5},{5,4},{6,7},{7,6},{8,9},{9,8},{10,11... | collective-permute-start | bytes 1572872 | tf_op jit(solution)/shard_map/ppermute | solution.py:759
  167.5 15.2 %collective-permute-start.49 = (bf16[512,512]{1,0:T(8,128)(2,1)S(1)}, bf16[512,512]{1,0:T(8,128)(2,1)S(1)}, u32[]{:S(2)}, u32[]{:S(2)}) collective-permute-start(bf16[512,512]{1,0:T(8,128)(2,1)S(1)} %collective-permute-done.43.refs_1_), channel_id=1, source_target_pairs={{0,2},{1,5},{2,0},{3,7},{4,6},{5,1},{6,4},{7,3},{8,10},{9,13},{10,... | collective-permute-start | bytes 1572872 | tf_op jit(solution)/shard_map/ppermute | solution.py:756
  168.9 9.2 %collective-permute-start.47 = (bf16[512,512]{1,0:T(8,128)(2,1)S(1)}, bf16[512,512]{1,0:T(8,128)(2,1)S(1)}, u32[]{:S(2)}, u32[]{:S(2)}) collective-permute-start(bf16[512,512]{1,0:T(8,128)(2,1)S(1)} %collective-permute-done.37.refs_4_), channel_id=1, source_target_pairs={{0,1},{1,0},{2,3},{3,2},{4,5},{5,4},{6,7},{7,6},{8,9},{9,8},{10,11... | collective-permute-start | bytes 1572872 | tf_op jit(solution)/shard_map/ppermute | solution.py:759
  170.2 7.9 %collective-permute-start.48 = (bf16[512,512]{1,0:T(8,128)(2,1)S(1)}, bf16[512,512]{1,0:T(8,128)(2,1)S(1)}, u32[]{:S(2)}, u32[]{:S(2)}) collective-permute-start(bf16[512,512]{1,0:T(8,128)(2,1)S(1)} %collective-permute-done.42.refs_5_), channel_id=1, source_target_pairs={{0,1},{1,0},{2,3},{3,2},{4,5},{5,4},{6,7},{7,6},{8,9},{9,8},{10,11... | collective-permute-start | bytes 1572872 | tf_op jit(solution)/shard_map/ppermute | solution.py:759
  (38 other events, 364.4 us)

commit v5 on v4

--- a/solution.py
+++ b/solution.py
@@ -12,14 +12,15 @@
 MIB = 1 << 20
 HALO_WIDTHS = (512, 512)
 TILES = 2
+ROWS = 256
 LAST = ("q", "p")
 ORDER = (
     "K", "O", "d0", "d1", "G", "d0", "d1", "H", "B", "d0", "d1", "t", "h", "d0", "d1", "b", "t",
-    "h", "d0", "d1", "t", "h", "e", "x0", "t", "p0", "h", "x1", "p1", "t", "R", "t", "F", "P",
+    "h", "d0", "d1", "t", "h", "x0", "e", "t", "p0", "h", "x1", "p1", "t", "R", "t", "F", "P",
 )
 
 FREE = pl.CostEstimate(flops=0, bytes_accessed=0, transcendentals=0)
-LARGE = pl.CostEstimate(flops=5_000_000_000, bytes_accessed=0, transcendentals=0)
+LARGE = pl.CostEstimate(flops=4_600_000_000, bytes_accessed=0, transcendentals=0)
 HBM = pl.BlockSpec(memory_space=pltpu.HBM)
 SMEM = pl.BlockSpec(memory_space=pltpu.SMEM)
 VMEM = pl.BlockSpec(memory_space=pltpu.VMEM)
@@ -264,9 +265,10 @@
         if j < 2:
             for c in copies[j]:
                 c.wait()
-        z_ref[:, at] = (
-            mxu(mine[...], near_mine[:, at]) + mxu(other[...], near_other[:, at]) + bias[:, at]
-        )
+        for k in range(z_ref.shape[0] // ROWS):
+            rows = slice(k * ROWS, (k + 1) * ROWS)
+            z = mxu(mine[rows, :], near_mine[:, at]) + mxu(other[rows, :], near_other[:, at])
+            z_ref[rows, at] = z + bias[:, at]
         if j == 0:
             for c in grads:
                 c.wait()

time: 189 us -> 189 us (level)
  waiting for transfers between devices: 71.4 us -> 68.4 us
  starting transfers between devices: 51.5 us -> 54.3 us
    ppermute x35, starting transfers between devices: 47 us -> 49.9 us  [along(): return lax.ppermute(x, 'dom', [(i, peer(i, b)) for i in range(size)])]
    ppermute x35, waiting for transfers between devices: 68.2 us -> 65.3 us  [along(): return lax.ppermute(x, 'dom', [(i, peer(i, b)) for i in range(size)])]
where the time goes in v5:
time: 189 us; the launch traced here: 188 us
  waiting for transfers between devices  68.4 us (36%)
  starting transfers between devices  54.3 us (29%)
  Pallas kernels  52.3 us (28%)
  local copies, waits for them, and re-layouts  8.27 us (4%)
  other arithmetic  3.69 us (2%)
    ppermute x35, waiting for transfers between devices, along(): return lax.ppermute(x, 'dom', [(i, peer(i, b)) for i in range(size)])  65.3 us
    ppermute x35, starting transfers between devices, along(): return lax.ppermute(x, 'dom', [(i, peer(i, b)) for i in range(size)])  49.9 us
    pallas_call x27, Pallas kernels, run(): kernel(*[pltpu.with_memory_space_constraint(x, pltpu.HBM) if spec is HBM...  43.3 us
    pallas_call x27, Pallas kernels, run(): return kernel(*operands)  9.01 us
    unnamed x36, local copies, waits for them, and re-layouts  6.52 us
    ppermute x17, starting transfers between devices, swap(): return lax.ppermute(x, 'dom', [(i, i ^ 1) for i in range(size)])  4.48 us
  transfers between devices with their start and end apart: 52, of which 28 were waited for; matrix products, arithmetic and copies ran while one was open for 3% of the time, Pallas kernels for 23%

profile of v5, /device:TPU:0, one launch (start us, length us, event | category | flops | bytes accessed | tf_op | source)
XLA Modules:
  0.0 188.5 jit_solution(3739738874727906079)
XLA Ops:
  5.4 3.7 %collective-permute-start.2 = (bf16[64,512]{1,0:T(8,128)(2,1)S(1)}, bf16[64,512]{1,0:T(8,128)(2,1)S(1)}, u32[]{:S(2)}, u32[]{:S(2)}) collective-permute-start(bf16[64,512]{1,0:T(8,128)(2,1)S(1)} %get-tuple-element.203.own), channel_id=1, source_target_pairs={{0,16},{1,17},{2,18},{3,19},{4,20},{5,21},{6,22},{7,23},{8,24},{9,... | collective-permute-start | bytes 196616 | tf_op jit(solution)/shard_map/ppermute | solution.py:758
  10.8 2.6 %collective-permute-done.2.received = bf16[64,512]{1,0:T(8,128)(2,1)S(1)} collective-permute-done((bf16[64,512]{1,0:T(8,128)(2,1)S(1)}, bf16[64,512]{1,0:T(8,128)(2,1)S(1)}, u32[]{:S(2)}, u32[]{:S(2)}) %collective-permute-start.2) | collective-permute-done | bytes 65568 | tf_op jit(solution)/shard_map/ppermute | solution.py:758
  13.4 2.6 %collective-permute-done.1.received = bf16[64,512]{1,0:T(8,128)(2,1)S(1)} collective-permute-done((bf16[64,512]{1,0:T(8,128)(2,1)S(1)}, bf16[64,512]{1,0:T(8,128)(2,1)S(1)}, u32[]{:S(2)}, u32[]{:S(2)}) %collective-permute-start.1) | collective-permute-done | bytes 65568 | tf_op jit(solution)/shard_map/ppermute | solution.py:758
  19.1 2.6 %counts.2 = (bf16[256,1024]{1,0:T(8,128)(2,1)S(1)}, bf16[256,256]{1,0:T(8,128)(2,1)S(1)}, f32[256,128]{1,0:T(8,128)S(1)}) custom-call(s32[256,17]{1,0:T(8,128)S(1)} %copy.32.packed, s32[1,1024]{1,0:T(1,128)S(1)} %fusion.label), custom_call_target="tpu_custom_call" | custom-call | tf_op jit(solution)/shard_map/counts/pallas_call | solution.py:51
  25.2 2.6 %counts.3 = (bf16[256,1024]{1,0:T(8,128)(2,1)S(1)}, bf16[256,256]{1,0:T(8,128)(2,1)S(1)}, f32[256,128]{1,0:T(8,128)S(1)}) custom-call(s32[256,17]{1,0:T(8,128)S(1)} %collective-permute-done.3.packed, s32[1,1024]{1,0:T(1,128)S(1)} %fusion.label), custom_call_target="tpu_custom_call" | custom-call | tf_op jit(solution)/shard_map/counts/pallas_call | solution.py:51
  29.9 2.8 %collective-permute-done.10.received = bf16[256,512]{1,0:T(8,128)(2,1)S(1)} collective-permute-done((bf16[256,512]{1,0:T(8,128)(2,1)S(1)}, bf16[256,512]{1,0:T(8,128)(2,1)S(1)}, u32[]{:S(2)}, u32[]{:S(2)}) %collective-permute-start.10) | collective-permute-done | bytes 262176 | tf_op jit(solution)/shard_map/ppermute | solution.py:758
  34.3 3.2 %collective-permute-done.9.received = bf16[512,512]{1,0:T(8,128)(2,1)S(1)} collective-permute-done((bf16[512,512]{1,0:T(8,128)(2,1)S(1)}, bf16[512,512]{1,0:T(8,128)(2,1)S(1)}, u32[]{:S(2)}, u32[]{:S(2)}) %collective-permute-start.9) | collective-permute-done | bytes 524320 | tf_op jit(solution)/shard_map/ppermute | solution.py:758
  37.5 5.6 %collective-permute-done.11.received = bf16[512,512]{1,0:T(8,128)(2,1)S(1)} collective-permute-done((bf16[512,512]{1,0:T(8,128)(2,1)S(1)}, bf16[512,512]{1,0:T(8,128)(2,1)S(1)}, u32[]{:S(2)}, u32[]{:S(2)}) %collective-permute-start.11) | collective-permute-done | bytes 524320 | tf_op jit(solution)/shard_map/ppermute | solution.py:758
  43.3 2.9 %aggregate.1.mine = bf16[512,1024]{1,0:T(8,128)(2,1)S(1)} custom-call(s32[1]{0:T(128)} %bitcast.where, bf16[256,2048]{1,0:T(8,128)(2,1)} %features.3, bf16[256,2048]{1,0:T(8,128)(2,1)} %copy-done.15, bf16[256,1024]{1,0:T(8,128)(2,1)S(1)} %get-tuple-element.214.refs_0_.own, bf16[256,256]{1,0:T(8,128)(2,1)S(1)} %get-tuple-element.229.refs_1_.own, ...), custom_call_target="tpu_custom_call" | custom-call | tf_op jit(solution)/shard_map/aggregate/pallas_call | solution.py:52
  50.5 6.6 %forward.1 = (f32[512,1024]{1,0:T(8,128)}, f32[8,1024]{1,0:T(8,128)S(1)}) custom-call(s32[1]{0:T(128)} %bitcast.where, bf16[512,1024]{1,0:T(8,128)(2,1)S(1)} %aggregate.1.mine, bf16[512,1024]{1,0:T(8,128)(2,1)S(1)} %collective-permute-done.12.other, f32[3,2048]{1,0:T(4,128)S(1)} %pad_maximum_fusion.constants, ...), custom_call_target="tpu_custom_call" | custom-call | tf_op jit(solution)/shard_map/forward/pallas_call | solution.py:52
  63.2 2.9 %collective-permute-done.15.received = f32[8,1024]{1,0:T(8,128)S(1)} collective-permute-done((f32[8,1024]{1,0:T(8,128)S(1)}, f32[8,1024]{1,0:T(8,128)S(1)}, u32[]{:S(2)}, u32[]{:S(2)}) %collective-permute-start.15) | collective-permute-done | bytes 32800 | tf_op jit(solution)/shard_map/ppermute | solution.py:758
  67.7 2.9 %collective-permute-done.16.received = f32[8,1024]{1,0:T(8,128)S(1)} collective-permute-done((f32[8,1024]{1,0:T(8,128)S(1)}, f32[8,1024]{1,0:T(8,128)S(1)}, u32[]{:S(2)}, u32[]{:S(2)}) %collective-permute-start.16) | collective-permute-done | bytes 32800 | tf_op jit(solution)/shard_map/ppermute | solution.py:758
  74.7 3.2 %dz.2 = bf16[512,512]{1,0:T(8,128)(2,1)} custom-call(s32[2]{0:T(128)S(1)} %pad_add_fusion.1.where, f32[8,1024]{1,0:T(8,128)S(1)} %merge.7.stats_ref, f32[3,2048]{1,0:T(4,128)S(1)} %pad_maximum_fusion.constants, f32[256,128]{1,0:T(8,128)S(1)} %get-tuple-element.230.refs_2_.own_factors, f32[256,128]{1,0:T(8,128)S(1)} %get-tuple-element.232.refs_5_.other_factors, ...), custom_call_target="tpu_custom_call" | custom-call | tf_op jit(solution)/shard_map/dz/pallas_call | solution.py:52
  78.7 2.4 %dz.3 = bf16[512,512]{1,0:T(8,128)(2,1)S(1)} custom-call(s32[2]{0:T(128)S(1)} %pad_add_fusion.2.where, f32[8,1024]{1,0:T(8,128)S(1)} %merge.7.stats_ref, f32[3,2048]{1,0:T(4,128)S(1)} %pad_maximum_fusion.constants, f32[256,128]{1,0:T(8,128)S(1)} %get-tuple-element.230.refs_2_.own_factors, f32[256,128]{1,0:T(8,128)S(1)} %get-tuple-element.232.refs_5_.other_factors, ...), custom_call_target="tpu_custom_call" | custom-call | tf_op jit(solution)/shard_map/dz/pallas_call | solution.py:52
  82.8 4.6 %collective-permute-done.19.dz_pair = bf16[512,512]{1,0:T(8,128)(2,1)S(1)} collective-permute-done((bf16[512,512]{1,0:T(8,128)(2,1)}, bf16[512,512]{1,0:T(8,128)(2,1)S(1)}, u32[]{:S(2)}, u32[]{:S(2)}) %collective-permute-start.19) | collective-permute-done | bytes 524320 | tf_op jit(solution)/shard_map/ppermute | solution.py:758
  91.1 3.7 %outputs.1 = (bf16[512,1024]{1,0:T(8,128)(2,1)S(1)}, bf16[256,1024]{1,0:T(8,128)(2,1)S(1)}, bf16[256,1024]{1,0:T(8,128)(2,1)S(1)}, f32[8,1024]{1,0:T(8,128)S(1)}) custom-call(s32[1]{0:T(128)} %bitcast.where, f32[8,1024]{1,0:T(8,128)S(1)} %merge.7.stats_ref, f32[3,2048]{1,0:T(4,128)S(1)} %pad_maximum_fusion.constants, ...), custom_call_target="tpu_custom_call" | custom-call | tf_op jit(solution)/shard_map/outputs/pallas_call | solution.py:52
  99.8 3.2 %collective-permute-done.20.received = bf16[512,512]{1,0:T(8,128)(2,1)S(1)} collective-permute-done((bf16[512,512]{1,0:T(8,128)(2,1)S(1)}, bf16[512,512]{1,0:T(8,128)(2,1)S(1)}, u32[]{:S(2)}, u32[]{:S(2)}) %collective-permute-start.20) | collective-permute-done | bytes 524320 | tf_op jit(solution)/shard_map/ppermute | solution.py:758
  105.7 3.9 %collective-permute-done.22.received = bf16[256,512]{1,0:T(8,128)(2,1)S(1)} collective-permute-done((bf16[256,512]{1,0:T(8,128)(2,1)S(1)}, bf16[256,512]{1,0:T(8,128)(2,1)S(1)}, u32[]{:S(2)}, u32[]{:S(2)}) %collective-permute-start.22) | collective-permute-done | bytes 262176 | tf_op jit(solution)/shard_map/ppermute | solution.py:758
  114.5 7.0 %collective-permute-done.26.received = bf16[128,512]{1,0:T(8,128)(2,1)S(1)} collective-permute-done((bf16[128,512]{1,0:T(8,128)(2,1)S(1)}, bf16[128,512]{1,0:T(8,128)(2,1)S(1)}, u32[]{:S(2)}, u32[]{:S(2)}) %collective-permute-start.26) | collective-permute-done | bytes 131104 | tf_op jit(solution)/shard_map/ppermute | solution.py:758
  121.6 2.7 %collective-permute-done.25.received = bf16[128,512]{1,0:T(8,128)(2,1)S(1)} collective-permute-done((bf16[128,512]{1,0:T(8,128)(2,1)S(1)}, bf16[128,512]{1,0:T(8,128)(2,1)S(1)}, u32[]{:S(2)}, u32[]{:S(2)}) %collective-permute-start.25) | collective-permute-done | bytes 131104 | tf_op jit(solution)/shard_map/ppermute | solution.py:758
  124.9 2.6 %collective-permute-start.27 = (bf16[256,1024]{1,0:T(8,128)(2,1)S(1)}, bf16[256,1024]{1,0:T(8,128)(2,1)S(1)}, u32[]{:S(2)}, u32[]{:S(2)}) collective-permute-start(bf16[256,1024]{1,0:T(8,128)(2,1)S(1)} %get-tuple-element.316), channel_id=1, source_target_pairs={{0,4},{1,9},{2,6},{3,11},{4,0},{5,13},{6,2},{7,15},{8,12},{9,1},{1... | collective-permute-start | bytes 1572872 | tf_op jit(solution)/shard_map/ppermute | solution.py:758
  129.0 2.5 %collective-permute-done.31.received = bf16[128,512]{1,0:T(8,128)(2,1)S(1)} collective-permute-done((bf16[128,512]{1,0:T(8,128)(2,1)S(1)}, bf16[128,512]{1,0:T(8,128)(2,1)S(1)}, u32[]{:S(2)}, u32[]{:S(2)}) %collective-permute-start.31) | collective-permute-done | bytes 131104 | tf_op jit(solution)/shard_map/ppermute | solution.py:758
  131.5 4.7 %collective-permute-start.35 = (bf16[256,512]{1,0:T(8,128)(2,1)S(1)}, bf16[256,512]{1,0:T(8,128)(2,1)S(1)}, u32[]{:S(2)}, u32[]{:S(2)}) collective-permute-start(bf16[256,512]{1,0:T(8,128)(2,1)S(1)} %join.5.own), channel_id=1, source_target_pairs={{0,8},{1,3},{2,10},{3,1},{4,12},{5,7},{6,14},{7,5},{8,0},{9,11},{1... | collective-permute-start | bytes 786440 | tf_op jit(solution)/shard_map/ppermute | solution.py:758
  136.5 5.6 %collective-permute-start.33 = (bf16[128,1024]{1,0:T(8,128)(2,1)S(1)}, bf16[128,1024]{1,0:T(8,128)(2,1)S(1)}, u32[]{:S(2)}, u32[]{:S(2)}) collective-permute-start(bf16[128,1024]{1,0:T(8,128)(2,1)S(1)} %get-tuple-element.330), channel_id=1, source_target_pairs={{0,8},{1,3},{2,10},{3,1},{4,12},{5,7},{6,14},{7,5},{8,0},{9,11},{1... | collective-permute-start | bytes 786440 | tf_op jit(solution)/shard_map/ppermute | solution.py:758
  142.5 3.9 %collective-permute-done.34.received = bf16[256,512]{1,0:T(8,128)(2,1)S(1)} collective-permute-done((bf16[256,512]{1,0:T(8,128)(2,1)S(1)}, bf16[256,512]{1,0:T(8,128)(2,1)S(1)}, u32[]{:S(2)}, u32[]{:S(2)}) %collective-permute-start.34) | collective-permute-done | bytes 262176 | tf_op jit(solution)/shard_map/ppermute | solution.py:758
  146.5 2.6 %collective-permute-start.37 = (bf16[512,512]{1,0:T(8,128)(2,1)S(1)}, bf16[512,512]{1,0:T(8,128)(2,1)S(1)}, u32[]{:S(2)}, u32[]{:S(2)}) collective-permute-start(bf16[512,512]{1,0:T(8,128)(2,1)S(1)} %join.6.refs_0_), channel_id=1, source_target_pairs={{0,2},{1,5},{2,0},{3,7},{4,6},{5,1},{6,4},{7,3},{8,10},{9,13},{10,... | collective-permute-start | bytes 1572872 | tf_op jit(solution)/shard_map/ppermute | solution.py:758
  149.1 2.9 %collective-permute-done.33.received = bf16[128,1024]{1,0:T(8,128)(2,1)S(1)} collective-permute-done((bf16[128,1024]{1,0:T(8,128)(2,1)S(1)}, bf16[128,1024]{1,0:T(8,128)(2,1)S(1)}, u32[]{:S(2)}, u32[]{:S(2)}) %collective-permute-start.33) | collective-permute-done | bytes 262176 | tf_op jit(solution)/shard_map/ppermute | solution.py:758
  159.4 3.4 %place.3.refs_8_ = f32[2048,2048]{1,0:T(8,128)} custom-call(s32[12]{0:T(128)S(1)} %stack.182.where, bf16[512,512]{1,0:T(8,128)(2,1)S(1)} %join.6.refs_0_, bf16[512,512]{1,0:T(8,128)(2,1)S(1)} %join.7.refs_1_, bf16[512,512]{1,0:T(8,128)(2,1)S(1)} %copy-done.6, bf16[512,512]{1,0:T(8,128)(2,1)} %collective-permute-done.40.refs_3_), custom_call_target="tpu_custom_call" | custom-call | tf_op jit(solution)/shard_map/place/pallas_call | solution.py:52
  162.9 3.5 %collective-permute-done.36.received = bf16[64,1024]{1,0:T(8,128)(2,1)S(1)} collective-permute-done((bf16[64,1024]{1,0:T(8,128)(2,1)S(1)}, bf16[64,1024]{1,0:T(8,128)(2,1)S(1)}, u32[]{:S(2)}, u32[]{:S(2)}) %collective-permute-start.36) | collective-permute-done | bytes 131104 | tf_op jit(solution)/shard_map/ppermute | solution.py:758
  170.0 7.8 %finish.1 = (bf16[256,2048]{1,0:T(8,128)(2,1)}, bf16[256,2048]{1,0:T(8,128)(2,1)}, f32[8,2048]{1,0:T(8,128)S(1)}) custom-call(s32[1]{0:T(128)} %bitcast.where, s32[32,1]{1,0:T(8,128)S(1)} %copy.33.rows, bf16[64,1024]{1,0:T(8,128)(2,1)S(1)} %total.5.back, bf16[32,1024]{1,0:T(8,128)(2,1)S(1)} %collective-permute-done.41.back_in, ...), custom_call_target="tpu_custom_call" | custom-call | tf_op jit(solution)/shard_map/finish/pallas_call | solution.py:52
  177.9 4.5 %place.4.refs_4_ = f32[2048,2048]{1,0:T(8,128)} custom-call(s32[24]{0:T(128)S(1)} %stack.194.where, bf16[512,512]{1,0:T(8,128)(2,1)S(1)} %collective-permute-done.39.refs_0_, bf16[512,512]{1,0:T(8,128)(2,1)S(1)} %collective-permute-done.43.refs_1_, bf16[512,512]{1,0:T(8,128)(2,1)} %collective-permute-done.45.refs_2_, ...), custom_call_target="tpu_custom_call", output_to_operand_aliasing={{}: (9, {})} | custom-call | tf_op jit(solution)/shard_map/place/pallas_call | solution.py:52
  185.6 2.6 %place.5 = f32[2048,2048]{1,0:T(8,128)} custom-call(s32[12]{0:T(128)S(1)} %stack.193.where, bf16[512,512]{1,0:T(8,128)(2,1)S(1)} %collective-permute-done.44.refs_0_, bf16[512,512]{1,0:T(8,128)(2,1)S(1)} %collective-permute-done.49.refs_1_, bf16[512,512]{1,0:T(8,128)(2,1)S(1)} %collective-permute-done.50.refs_2_, ...), custom_call_target="tpu_custom_call", output_to_operand_aliasing={{}: (5, {})} | custom-call | tf_op jit(solution)/shard_map/place/pallas_call | solution.py:52
  (180 shorter events, 68.7 us)
Async XLA Ops:
  0.6 23.6 %collective-permute-start.4 = (bf16[256,2048]{1,0:T(8,128)(2,1)}, bf16[256,2048]{1,0:T(8,128)(2,1)S(1)}, u32[]{:S(2)}, u32[]{:S(2)}) collective-permute-start(bf16[256,2048]{1,0:T(8,128)(2,1)} %features.3), channel_id=1, source_target_pairs={{0,1},{1,0},{2,3},{3,2},{4,5},{5,4},{6,7},{7,6},{8,9},{9,8},{10,11... | collective-permute-start | bytes 3145736 | tf_op jit(solution)/shard_map/ppermute | solution.py:761
  1.1 24.0 %collective-permute-start.5 = (bf16[256,2048]{1,0:T(8,128)(2,1)}, bf16[256,2048]{1,0:T(8,128)(2,1)}, u32[]{:S(2)}, u32[]{:S(2)}) collective-permute-start(bf16[256,2048]{1,0:T(8,128)(2,1)} %cotangent.7), channel_id=1, source_target_pairs={{0,1},{1,0},{2,3},{3,2},{4,5},{5,4},{6,7},{7,6},{8,9},{9,8},{10,11... | collective-permute-start | bytes 3145736 | tf_op jit(solution)/shard_map/ppermute | solution.py:761
  23.5 9.3 %collective-permute-start.10 = (bf16[256,512]{1,0:T(8,128)(2,1)S(1)}, bf16[256,512]{1,0:T(8,128)(2,1)S(1)}, u32[]{:S(2)}, u32[]{:S(2)}) collective-permute-start(bf16[256,512]{1,0:T(8,128)(2,1)S(1)} %stack_rows.12.own), channel_id=1, source_target_pairs={{0,4},{1,9},{2,6},{3,11},{4,0},{5,13},{6,2},{7,15},{8,12},{9,1},{1... | collective-permute-start | bytes 786440 | tf_op jit(solution)/shard_map/ppermute | solution.py:758
  28.3 9.2 %collective-permute-start.9 = (bf16[512,512]{1,0:T(8,128)(2,1)S(1)}, bf16[512,512]{1,0:T(8,128)(2,1)S(1)}, u32[]{:S(2)}, u32[]{:S(2)}) collective-permute-start(bf16[512,512]{1,0:T(8,128)(2,1)S(1)} %stack_rows.11.own), channel_id=1, source_target_pairs={{0,2},{1,5},{2,0},{3,7},{4,6},{5,1},{6,4},{7,3},{8,10},{9,13},{10,... | collective-permute-start | bytes 1572872 | tf_op jit(solution)/shard_map/ppermute | solution.py:758
  32.8 10.4 %collective-permute-start.11 = (bf16[512,512]{1,0:T(8,128)(2,1)S(1)}, bf16[512,512]{1,0:T(8,128)(2,1)S(1)}, u32[]{:S(2)}, u32[]{:S(2)}) collective-permute-start(bf16[512,512]{1,0:T(8,128)(2,1)S(1)} %stack_rows.14.own), channel_id=1, source_target_pairs={{0,2},{1,5},{2,0},{3,7},{4,6},{5,1},{6,4},{7,3},{8,10},{9,13},{10,... | collective-permute-start | bytes 1572872 | tf_op jit(solution)/shard_map/ppermute | solution.py:758
  46.3 15.0 %collective-permute-start.14 = (bf16[512,1024]{1,0:T(8,128)(2,1)S(1)}, bf16[512,1024]{1,0:T(8,128)(2,1)}, u32[]{:S(2)}, u32[]{:S(2)}) collective-permute-start(bf16[512,1024]{1,0:T(8,128)(2,1)S(1)} %aggregate.1.mine), channel_id=1, source_target_pairs={{0,2},{1,5},{2,0},{3,7},{4,6},{5,1},{6,4},{7,3},{8,10},{9,13},{10,... | collective-permute-start | bytes 3145736 | tf_op jit(solution)/shard_map/ppermute | solution.py:758
  48.9 23.9 %collective-permute-start.18 = (bf16[512,1024]{1,0:T(8,128)(2,1)S(1)}, bf16[512,1024]{1,0:T(8,128)(2,1)}, u32[]{:S(2)}, u32[]{:S(2)}) collective-permute-start(bf16[512,1024]{1,0:T(8,128)(2,1)S(1)} %collective-permute-done.12.other), channel_id=1, source_target_pairs={{0,2},{1,5},{2,0},{3,7},{4,6},{5,1},{6,4},{7,3},{8,10},{9,13},{10,... | collective-permute-start | bytes 3145736 | tf_op jit(solution)/shard_map/ppermute | solution.py:758
  77.9 9.5 %collective-permute-start.19 = (bf16[512,512]{1,0:T(8,128)(2,1)}, bf16[512,512]{1,0:T(8,128)(2,1)S(1)}, u32[]{:S(2)}, u32[]{:S(2)}) collective-permute-start(bf16[512,512]{1,0:T(8,128)(2,1)} %dz.2), channel_id=1, source_target_pairs={{0,2},{1,5},{2,0},{3,7},{4,6},{5,1},{6,4},{7,3},{8,10},{9,13},{10,... | collective-permute-start | bytes 1572872 | tf_op jit(solution)/shard_map/ppermute | solution.py:758
  88.1 10.5 %collective-permute-start.21 = (bf16[512,512]{1,0:T(8,128)(2,1)S(1)}, bf16[512,512]{1,0:T(8,128)(2,1)S(1)}, u32[]{:S(2)}, u32[]{:S(2)}) collective-permute-start(bf16[512,512]{1,0:T(8,128)(2,1)S(1)} %weight_part.7), channel_id=1, source_target_pairs={{0,4},{1,9},{2,6},{3,11},{4,0},{5,13},{6,2},{7,15},{8,12},{9,1},{1... | collective-permute-start | bytes 1572872 | tf_op jit(solution)/shard_map/ppermute | solution.py:758
  90.4 12.6 %collective-permute-start.20 = (bf16[512,512]{1,0:T(8,128)(2,1)S(1)}, bf16[512,512]{1,0:T(8,128)(2,1)S(1)}, u32[]{:S(2)}, u32[]{:S(2)}) collective-permute-start(bf16[512,512]{1,0:T(8,128)(2,1)S(1)} %weight_part.6), channel_id=1, source_target_pairs={{0,4},{1,9},{2,6},{3,11},{4,0},{5,13},{6,2},{7,15},{8,12},{9,1},{1... | collective-permute-start | bytes 1572872 | tf_op jit(solution)/shard_map/ppermute | solution.py:758
  109.6 15.1 %collective-permute-start.24 = (bf16[512,1024]{1,0:T(8,128)(2,1)S(1)}, bf16[512,1024]{1,0:T(8,128)(2,1)S(1)}, u32[]{:S(2)}, u32[]{:S(2)}) collective-permute-start(bf16[512,1024]{1,0:T(8,128)(2,1)S(1)} %back_part.2), channel_id=1, source_target_pairs={{0,2},{1,5},{2,0},{3,7},{4,6},{5,1},{6,4},{7,3},{8,10},{9,13},{10,... | collective-permute-start | bytes 3145736 | tf_op jit(solution)/shard_map/ppermute | solution.py:758
  110.3 11.2 %collective-permute-start.26 = (bf16[128,512]{1,0:T(8,128)(2,1)S(1)}, bf16[128,512]{1,0:T(8,128)(2,1)S(1)}, u32[]{:S(2)}, u32[]{:S(2)}) collective-permute-start(bf16[128,512]{1,0:T(8,128)(2,1)S(1)} %get-tuple-element.305), channel_id=1, source_target_pairs={{0,16},{1,17},{2,18},{3,19},{4,20},{5,21},{6,22},{7,23},{8,24},{9,... | collective-permute-start | bytes 393224 | tf_op jit(solution)/shard_map/ppermute | solution.py:758
  112.7 11.6 %collective-permute-start.25 = (bf16[128,512]{1,0:T(8,128)(2,1)S(1)}, bf16[128,512]{1,0:T(8,128)(2,1)S(1)}, u32[]{:S(2)}, u32[]{:S(2)}) collective-permute-start(bf16[128,512]{1,0:T(8,128)(2,1)S(1)} %get-tuple-element.302), channel_id=1, source_target_pairs={{0,16},{1,17},{2,18},{3,19},{4,20},{5,21},{6,22},{7,23},{8,24},{9,... | collective-permute-start | bytes 393224 | tf_op jit(solution)/shard_map/ppermute | solution.py:758
  113.4 22.7 %collective-permute-start.29 = (bf16[256,1024]{1,0:T(8,128)(2,1)S(1)}, bf16[256,1024]{1,0:T(8,128)(2,1)S(1)}, u32[]{:S(2)}, u32[]{:S(2)}) collective-permute-start(bf16[256,1024]{1,0:T(8,128)(2,1)S(1)} %get-tuple-element.318), channel_id=1, source_target_pairs={{0,1},{1,0},{2,3},{3,2},{4,5},{5,4},{6,7},{7,6},{8,9},{9,8},{10,11... | collective-permute-start | bytes 1572872 | tf_op jit(solution)/shard_map/ppermute | solution.py:761
  113.9 22.3 %collective-permute-start.28 = (bf16[256,1024]{1,0:T(8,128)(2,1)S(1)}, bf16[256,1024]{1,0:T(8,128)(2,1)S(1)}, u32[]{:S(2)}, u32[]{:S(2)}) collective-permute-start(bf16[256,1024]{1,0:T(8,128)(2,1)S(1)} %get-tuple-element.317), channel_id=1, source_target_pairs={{0,1},{1,0},{2,3},{3,2},{4,5},{5,4},{6,7},{7,6},{8,9},{9,8},{10,11... | collective-permute-start | bytes 1572872 | tf_op jit(solution)/shard_map/ppermute | solution.py:761
  124.9 11.4 %collective-permute-start.27 = (bf16[256,1024]{1,0:T(8,128)(2,1)S(1)}, bf16[256,1024]{1,0:T(8,128)(2,1)S(1)}, u32[]{:S(2)}, u32[]{:S(2)}) collective-permute-start(bf16[256,1024]{1,0:T(8,128)(2,1)S(1)} %get-tuple-element.316), channel_id=1, source_target_pairs={{0,4},{1,9},{2,6},{3,11},{4,0},{5,13},{6,2},{7,15},{8,12},{9,1},{1... | collective-permute-start | bytes 1572872 | tf_op jit(solution)/shard_map/ppermute | solution.py:758
  131.5 10.6 %collective-permute-start.35 = (bf16[256,512]{1,0:T(8,128)(2,1)S(1)}, bf16[256,512]{1,0:T(8,128)(2,1)S(1)}, u32[]{:S(2)}, u32[]{:S(2)}) collective-permute-start(bf16[256,512]{1,0:T(8,128)(2,1)S(1)} %join.5.own), channel_id=1, source_target_pairs={{0,8},{1,3},{2,10},{3,1},{4,12},{5,7},{6,14},{7,5},{8,0},{9,11},{1... | collective-permute-start | bytes 786440 | tf_op jit(solution)/shard_map/ppermute | solution.py:758
  136.2 10.2 %collective-permute-start.34 = (bf16[256,512]{1,0:T(8,128)(2,1)S(1)}, bf16[256,512]{1,0:T(8,128)(2,1)S(1)}, u32[]{:S(2)}, u32[]{:S(2)}) collective-permute-start(bf16[256,512]{1,0:T(8,128)(2,1)S(1)} %join.4.own), channel_id=1, source_target_pairs={{0,8},{1,3},{2,10},{3,1},{4,12},{5,7},{6,14},{7,5},{8,0},{9,11},{1... | collective-permute-start | bytes 786440 | tf_op jit(solution)/shard_map/ppermute | solution.py:758
  136.5 15.6 %collective-permute-start.33 = (bf16[128,1024]{1,0:T(8,128)(2,1)S(1)}, bf16[128,1024]{1,0:T(8,128)(2,1)S(1)}, u32[]{:S(2)}, u32[]{:S(2)}) collective-permute-start(bf16[128,1024]{1,0:T(8,128)(2,1)S(1)} %get-tuple-element.330), channel_id=1, source_target_pairs={{0,8},{1,3},{2,10},{3,1},{4,12},{5,7},{6,14},{7,5},{8,0},{9,11},{1... | collective-permute-start | bytes 786440 | tf_op jit(solution)/shard_map/ppermute | solution.py:758
  142.1 10.9 %collective-permute-start.39 = (bf16[512,512]{1,0:T(8,128)(2,1)S(1)}, bf16[512,512]{1,0:T(8,128)(2,1)S(1)}, u32[]{:S(2)}, u32[]{:S(2)}) collective-permute-start(bf16[512,512]{1,0:T(8,128)(2,1)S(1)} %join.6.refs_0_), channel_id=1, source_target_pairs={{0,4},{1,9},{2,6},{3,11},{4,0},{5,13},{6,2},{7,15},{8,12},{9,1},{1... | collective-permute-start | bytes 1572872 | tf_op jit(solution)/shard_map/ppermute | solution.py:758
  142.5 12.2 %collective-permute-start.38 = (bf16[512,512]{1,0:T(8,128)(2,1)S(1)}, bf16[512,512]{1,0:T(8,128)(2,1)S(1)}, u32[]{:S(2)}, u32[]{:S(2)}) collective-permute-start(bf16[512,512]{1,0:T(8,128)(2,1)S(1)} %join.6.refs_0_), channel_id=1, source_target_pairs={{0,1},{1,0},{2,3},{3,2},{4,5},{5,4},{6,7},{7,6},{8,9},{9,8},{10,11... | collective-permute-start | bytes 1572872 | tf_op jit(solution)/shard_map/ppermute | solution.py:761
  146.5 10.2 %collective-permute-start.40 = (bf16[512,512]{1,0:T(8,128)(2,1)S(1)}, bf16[512,512]{1,0:T(8,128)(2,1)}, u32[]{:S(2)}, u32[]{:S(2)}) collective-permute-start(bf16[512,512]{1,0:T(8,128)(2,1)S(1)} %join.7.refs_1_), channel_id=1, source_target_pairs={{0,1},{1,0},{2,3},{3,2},{4,5},{5,4},{6,7},{7,6},{8,9},{9,8},{10,11... | collective-permute-start | bytes 1572872 | tf_op jit(solution)/shard_map/ppermute | solution.py:761
  146.5 16.3 %collective-permute-start.37 = (bf16[512,512]{1,0:T(8,128)(2,1)S(1)}, bf16[512,512]{1,0:T(8,128)(2,1)S(1)}, u32[]{:S(2)}, u32[]{:S(2)}) collective-permute-start(bf16[512,512]{1,0:T(8,128)(2,1)S(1)} %join.6.refs_0_), channel_id=1, source_target_pairs={{0,2},{1,5},{2,0},{3,7},{4,6},{5,1},{6,4},{7,3},{8,10},{9,13},{10,... | collective-permute-start | bytes 1572872 | tf_op jit(solution)/shard_map/ppermute | solution.py:758
  152.7 14.9 %collective-permute-start.43 = (bf16[512,512]{1,0:T(8,128)(2,1)S(1)}, bf16[512,512]{1,0:T(8,128)(2,1)S(1)}, u32[]{:S(2)}, u32[]{:S(2)}) collective-permute-start(bf16[512,512]{1,0:T(8,128)(2,1)S(1)} %join.7.refs_1_), channel_id=1, source_target_pairs={{0,4},{1,9},{2,6},{3,11},{4,0},{5,13},{6,2},{7,15},{8,12},{9,1},{1... | collective-permute-start | bytes 1572872 | tf_op jit(solution)/shard_map/ppermute | solution.py:758
  152.9 16.0 %collective-permute-start.42 = (bf16[512,512]{1,0:T(8,128)(2,1)S(1)}, bf16[512,512]{1,0:T(8,128)(2,1)S(1)}, u32[]{:S(2)}, u32[]{:S(2)}) collective-permute-start(bf16[512,512]{1,0:T(8,128)(2,1)S(1)} %join.7.refs_1_), channel_id=1, source_target_pairs={{0,2},{1,5},{2,0},{3,7},{4,6},{5,1},{6,4},{7,3},{8,10},{9,13},{10,... | collective-permute-start | bytes 1572872 | tf_op jit(solution)/shard_map/ppermute | solution.py:758
  155.5 14.0 %collective-permute-start.45 = (bf16[512,512]{1,0:T(8,128)(2,1)S(1)}, bf16[512,512]{1,0:T(8,128)(2,1)}, u32[]{:S(2)}, u32[]{:S(2)}) collective-permute-start(bf16[512,512]{1,0:T(8,128)(2,1)S(1)} %collective-permute-done.39.refs_0_), channel_id=1, source_target_pairs={{0,1},{1,0},{2,3},{3,2},{4,5},{5,4},{6,7},{7,6},{8,9},{9,8},{10,11... | collective-permute-start | bytes 1572872 | tf_op jit(solution)/shard_map/ppermute | solution.py:761
  156.7 9.7 %collective-permute-start.36 = (bf16[64,1024]{1,0:T(8,128)(2,1)S(1)}, bf16[64,1024]{1,0:T(8,128)(2,1)S(1)}, u32[]{:S(2)}, u32[]{:S(2)}) collective-permute-start(bf16[64,1024]{1,0:T(8,128)(2,1)S(1)} %get-tuple-element.338), channel_id=1, source_target_pairs={{0,16},{1,17},{2,18},{3,19},{4,20},{5,21},{6,22},{7,23},{8,24},{9,... | collective-permute-start | bytes 393224 | tf_op jit(solution)/shard_map/ppermute | solution.py:758
  166.7 15.7 %collective-permute-start.44 = (bf16[512,512]{1,0:T(8,128)(2,1)S(1)}, bf16[512,512]{1,0:T(8,128)(2,1)S(1)}, u32[]{:S(2)}, u32[]{:S(2)}) collective-permute-start(bf16[512,512]{1,0:T(8,128)(2,1)S(1)} %collective-permute-done.39.refs_0_), channel_id=1, source_target_pairs={{0,2},{1,5},{2,0},{3,7},{4,6},{5,1},{6,4},{7,3},{8,10},{9,13},{10,... | collective-permute-start | bytes 1572872 | tf_op jit(solution)/shard_map/ppermute | solution.py:758
  167.6 10.3 %collective-permute-start.46 = (bf16[512,512]{1,0:T(8,128)(2,1)S(1)}, bf16[512,512]{1,0:T(8,128)(2,1)S(1)}, u32[]{:S(2)}, u32[]{:S(2)}) collective-permute-start(bf16[512,512]{1,0:T(8,128)(2,1)S(1)} %collective-permute-done.43.refs_1_), channel_id=1, source_target_pairs={{0,1},{1,0},{2,3},{3,2},{4,5},{5,4},{6,7},{7,6},{8,9},{9,8},{10,11... | collective-permute-start | bytes 1572872 | tf_op jit(solution)/shard_map/ppermute | solution.py:761
  169.0 13.5 %collective-permute-start.49 = (bf16[512,512]{1,0:T(8,128)(2,1)S(1)}, bf16[512,512]{1,0:T(8,128)(2,1)S(1)}, u32[]{:S(2)}, u32[]{:S(2)}) collective-permute-start(bf16[512,512]{1,0:T(8,128)(2,1)S(1)} %collective-permute-done.43.refs_1_), channel_id=1, source_target_pairs={{0,2},{1,5},{2,0},{3,7},{4,6},{5,1},{6,4},{7,3},{8,10},{9,13},{10,... | collective-permute-start | bytes 1572872 | tf_op jit(solution)/shard_map/ppermute | solution.py:758
  169.5 8.4 %collective-permute-start.47 = (bf16[512,512]{1,0:T(8,128)(2,1)S(1)}, bf16[512,512]{1,0:T(8,128)(2,1)S(1)}, u32[]{:S(2)}, u32[]{:S(2)}) collective-permute-start(bf16[512,512]{1,0:T(8,128)(2,1)S(1)} %collective-permute-done.37.refs_4_), channel_id=1, source_target_pairs={{0,1},{1,0},{2,3},{3,2},{4,5},{5,4},{6,7},{7,6},{8,9},{9,8},{10,11... | collective-permute-start | bytes 1572872 | tf_op jit(solution)/shard_map/ppermute | solution.py:761
  169.5 8.4 %collective-permute-start.48 = (bf16[512,512]{1,0:T(8,128)(2,1)S(1)}, bf16[512,512]{1,0:T(8,128)(2,1)S(1)}, u32[]{:S(2)}, u32[]{:S(2)}) collective-permute-start(bf16[512,512]{1,0:T(8,128)(2,1)S(1)} %collective-permute-done.42.refs_5_), channel_id=1, source_target_pairs={{0,1},{1,0},{2,3},{3,2},{4,5},{5,4},{6,7},{7,6},{8,9},{9,8},{10,11... | collective-permute-start | bytes 1572872 | tf_op jit(solution)/shard_map/ppermute | solution.py:761
  (38 other events, 381.1 us)

commit v6 on v5

--- a/solution.py
+++ b/solution.py
@@ -176,7 +176,7 @@
 
 def aggregate_kernel(n, where, features, features_in, *refs):
     own, sibling, halos = refs[:3], refs[3:6], refs[6 : 6 + n]
-    out, near, sem = refs[6 + n :]
+    out, near, sums, sem = refs[6 + n :]
     _, nodes, half = near.shape
     core = where[0]
     here = pl.ds(pl.multiple_of(core * half, half), half)
@@ -186,17 +186,16 @@
     ]
     for c in copies:
         c.start()
-    for k, (halo_count, own_count, factors) in enumerate((own, sibling)):
+    for k, (halo_count, _, _) in enumerate((own, sibling)):
+        start = 0
+        for halo in halos:
+            sums[k, :, start : start + halo.shape[1]] = mxu(halo_count[...], halo[...])
+            start += halo.shape[1]
+    for k, (_, own_count, factors) in enumerate((own, sibling)):
         rows = pl.ds(pl.multiple_of((core if k == 0 else 1 - core) * nodes, nodes), nodes)
-        start = 0
-        for i, halo in enumerate(halos):
-            part = slice(start, start + halo.shape[1])
-            total = mxu(halo_count[...], halo[...])
-            if i == 0:
-                copies[k].wait()
-            total = total + mxu(own_count[...], near[k][:, part])
-            out[rows, part] = (total * factors[:, 1:2]).astype(BF)
-            start += halo.shape[1]
+        copies[k].wait()
+        total = sums[k] + mxu(own_count[...], near[k])
+        out[rows, :] = (total * factors[:, 1:2]).astype(BF)
 
 
 def aggregate(core, features, features_in, own, sibling, halos):
@@ -207,7 +206,11 @@
         shape_of((2 * rows, half), BF),
         "aggregate",
         in_specs=[SMEM, HBM, HBM] + [VMEM] * (6 + len(halos)),
-        scratch_shapes=[pltpu.VMEM((2, rows, half), BF), pltpu.SemaphoreType.DMA((2,))],
+        scratch_shapes=[
+            pltpu.VMEM((2, rows, half), BF),
+            pltpu.VMEM((2, rows, half), F32),
+            pltpu.SemaphoreType.DMA((2,)),
+        ],
     )(scalars(core), features, features_in, *own, *sibling, *halos)
 
 

time: 189 us -> 189 us (level)
  transfers between devices with their start and end apart: 52 -> 52, of which waited for: 28 -> 26; matrix products, arithmetic and copies ran while one was open for 3% -> 3% of each run, Pallas kernels for 23% -> 23%
where the time goes in v6:
time: 189 us; the launch traced here: 188 us
  waiting for transfers between devices  67.8 us (36%)
  starting transfers between devices  55 us (29%)
  Pallas kernels  52 us (28%)
  local copies, waits for them, and re-layouts  8.27 us (4%)
  other arithmetic  3.69 us (2%)
    ppermute x35, waiting for transfers between devices, along(): return lax.ppermute(x, 'dom', [(i, peer(i, b)) for i in range(size)])  64.7 us
    ppermute x35, starting transfers between devices, along(): return lax.ppermute(x, 'dom', [(i, peer(i, b)) for i in range(size)])  50.8 us
    pallas_call x27, Pallas kernels, run(): kernel(*[pltpu.with_memory_space_constraint(x, pltpu.HBM) if spec is HBM...  43 us
    pallas_call x27, Pallas kernels, run(): return kernel(*operands)  9.01 us
    unnamed x36, local copies, waits for them, and re-layouts  6.52 us
    ppermute x17, starting transfers between devices, swap(): return lax.ppermute(x, 'dom', [(i, i ^ 1) for i in range(size)])  4.18 us
  transfers between devices with their start and end apart: 52, of which 26 were waited for; matrix products, arithmetic and copies ran while one was open for 3% of the time, Pallas kernels for 23%

profile of v6, /device:TPU:0, one launch (start us, length us, event | category | flops | bytes accessed | tf_op | source)
XLA Modules:
  0.0 188.2 jit_solution(2344571580038441655)
XLA Ops:
  5.4 3.7 %collective-permute-start.2 = (bf16[64,512]{1,0:T(8,128)(2,1)S(1)}, bf16[64,512]{1,0:T(8,128)(2,1)S(1)}, u32[]{:S(2)}, u32[]{:S(2)}) collective-permute-start(bf16[64,512]{1,0:T(8,128)(2,1)S(1)} %get-tuple-element.203.own), channel_id=1, source_target_pairs={{0,16},{1,17},{2,18},{3,19},{4,20},{5,21},{6,22},{7,23},{8,24},{9,... | collective-permute-start | bytes 196616 | tf_op jit(solution)/shard_map/ppermute | solution.py:761
  10.8 2.6 %collective-permute-done.2.received = bf16[64,512]{1,0:T(8,128)(2,1)S(1)} collective-permute-done((bf16[64,512]{1,0:T(8,128)(2,1)S(1)}, bf16[64,512]{1,0:T(8,128)(2,1)S(1)}, u32[]{:S(2)}, u32[]{:S(2)}) %collective-permute-start.2) | collective-permute-done | bytes 65568 | tf_op jit(solution)/shard_map/ppermute | solution.py:761
  13.4 2.6 %collective-permute-done.1.received = bf16[64,512]{1,0:T(8,128)(2,1)S(1)} collective-permute-done((bf16[64,512]{1,0:T(8,128)(2,1)S(1)}, bf16[64,512]{1,0:T(8,128)(2,1)S(1)}, u32[]{:S(2)}, u32[]{:S(2)}) %collective-permute-start.1) | collective-permute-done | bytes 65568 | tf_op jit(solution)/shard_map/ppermute | solution.py:761
  19.1 2.6 %counts.2 = (bf16[256,1024]{1,0:T(8,128)(2,1)S(1)}, bf16[256,256]{1,0:T(8,128)(2,1)S(1)}, f32[256,128]{1,0:T(8,128)S(1)}) custom-call(s32[256,17]{1,0:T(8,128)S(1)} %copy.32.packed, s32[1,1024]{1,0:T(1,128)S(1)} %fusion.label), custom_call_target="tpu_custom_call" | custom-call | tf_op jit(solution)/shard_map/counts/pallas_call | solution.py:51
  25.2 2.6 %counts.3 = (bf16[256,1024]{1,0:T(8,128)(2,1)S(1)}, bf16[256,256]{1,0:T(8,128)(2,1)S(1)}, f32[256,128]{1,0:T(8,128)S(1)}) custom-call(s32[256,17]{1,0:T(8,128)S(1)} %collective-permute-done.3.packed, s32[1,1024]{1,0:T(1,128)S(1)} %fusion.label), custom_call_target="tpu_custom_call" | custom-call | tf_op jit(solution)/shard_map/counts/pallas_call | solution.py:51
  29.9 2.8 %collective-permute-done.10.received = bf16[256,512]{1,0:T(8,128)(2,1)S(1)} collective-permute-done((bf16[256,512]{1,0:T(8,128)(2,1)S(1)}, bf16[256,512]{1,0:T(8,128)(2,1)S(1)}, u32[]{:S(2)}, u32[]{:S(2)}) %collective-permute-start.10) | collective-permute-done | bytes 262176 | tf_op jit(solution)/shard_map/ppermute | solution.py:761
  34.3 3.2 %collective-permute-done.9.received = bf16[512,512]{1,0:T(8,128)(2,1)S(1)} collective-permute-done((bf16[512,512]{1,0:T(8,128)(2,1)S(1)}, bf16[512,512]{1,0:T(8,128)(2,1)S(1)}, u32[]{:S(2)}, u32[]{:S(2)}) %collective-permute-start.9) | collective-permute-done | bytes 524320 | tf_op jit(solution)/shard_map/ppermute | solution.py:761
  37.5 5.6 %collective-permute-done.11.received = bf16[512,512]{1,0:T(8,128)(2,1)S(1)} collective-permute-done((bf16[512,512]{1,0:T(8,128)(2,1)S(1)}, bf16[512,512]{1,0:T(8,128)(2,1)S(1)}, u32[]{:S(2)}, u32[]{:S(2)}) %collective-permute-start.11) | collective-permute-done | bytes 524320 | tf_op jit(solution)/shard_map/ppermute | solution.py:761
  43.3 2.7 %aggregate.1.mine = bf16[512,1024]{1,0:T(8,128)(2,1)S(1)} custom-call(s32[1]{0:T(128)} %bitcast.where, bf16[256,2048]{1,0:T(8,128)(2,1)} %features.3, bf16[256,2048]{1,0:T(8,128)(2,1)} %copy-done.15, bf16[256,1024]{1,0:T(8,128)(2,1)S(1)} %get-tuple-element.214.refs_0_.own, bf16[256,256]{1,0:T(8,128)(2,1)S(1)} %get-tuple-element.229.refs_1_.own, ...), custom_call_target="tpu_custom_call" | custom-call | tf_op jit(solution)/shard_map/aggregate/pallas_call | solution.py:52
  50.3 6.5 %forward.1 = (f32[512,1024]{1,0:T(8,128)}, f32[8,1024]{1,0:T(8,128)S(1)}) custom-call(s32[1]{0:T(128)} %bitcast.where, bf16[512,1024]{1,0:T(8,128)(2,1)S(1)} %aggregate.1.mine, bf16[512,1024]{1,0:T(8,128)(2,1)S(1)} %collective-permute-done.12.other, f32[3,2048]{1,0:T(4,128)S(1)} %pad_maximum_fusion.constants, ...), custom_call_target="tpu_custom_call" | custom-call | tf_op jit(solution)/shard_map/forward/pallas_call | solution.py:52
  56.8 2.3 %collective-permute-start.13 = (f32[8,1024]{1,0:T(8,128)S(1)}, f32[8,1024]{1,0:T(8,128)S(1)}, u32[]{:S(2)}, u32[]{:S(2)}) collective-permute-start(f32[8,1024]{1,0:T(8,128)S(1)} %get-tuple-element.247.own), channel_id=1, source_target_pairs={{0,16},{1,17},{2,18},{3,19},{4,20},{5,21},{6,22},{7,23},{8,24},{9,... | collective-permute-start | bytes 98312 | tf_op jit(solution)/shard_map/ppermute | solution.py:761
  62.9 2.9 %collective-permute-done.15.received = f32[8,1024]{1,0:T(8,128)S(1)} collective-permute-done((f32[8,1024]{1,0:T(8,128)S(1)}, f32[8,1024]{1,0:T(8,128)S(1)}, u32[]{:S(2)}, u32[]{:S(2)}) %collective-permute-start.15) | collective-permute-done | bytes 32800 | tf_op jit(solution)/shard_map/ppermute | solution.py:761
  67.4 2.9 %collective-permute-done.16.received = f32[8,1024]{1,0:T(8,128)S(1)} collective-permute-done((f32[8,1024]{1,0:T(8,128)S(1)}, f32[8,1024]{1,0:T(8,128)S(1)}, u32[]{:S(2)}, u32[]{:S(2)}) %collective-permute-start.16) | collective-permute-done | bytes 32800 | tf_op jit(solution)/shard_map/ppermute | solution.py:761
  74.4 3.2 %dz.2 = bf16[512,512]{1,0:T(8,128)(2,1)} custom-call(s32[2]{0:T(128)S(1)} %pad_add_fusion.1.where, f32[8,1024]{1,0:T(8,128)S(1)} %merge.7.stats_ref, f32[3,2048]{1,0:T(4,128)S(1)} %pad_maximum_fusion.constants, f32[256,128]{1,0:T(8,128)S(1)} %get-tuple-element.230.refs_2_.own_factors, f32[256,128]{1,0:T(8,128)S(1)} %get-tuple-element.232.refs_5_.other_factors, ...), custom_call_target="tpu_custom_call" | custom-call | tf_op jit(solution)/shard_map/dz/pallas_call | solution.py:52
  78.6 2.4 %dz.3 = bf16[512,512]{1,0:T(8,128)(2,1)S(1)} custom-call(s32[2]{0:T(128)S(1)} %pad_add_fusion.2.where, f32[8,1024]{1,0:T(8,128)S(1)} %merge.7.stats_ref, f32[3,2048]{1,0:T(4,128)S(1)} %pad_maximum_fusion.constants, f32[256,128]{1,0:T(8,128)S(1)} %get-tuple-element.230.refs_2_.own_factors, f32[256,128]{1,0:T(8,128)S(1)} %get-tuple-element.232.refs_5_.other_factors, ...), custom_call_target="tpu_custom_call" | custom-call | tf_op jit(solution)/shard_map/dz/pallas_call | solution.py:52
  82.6 4.5 %collective-permute-done.19.dz_pair = bf16[512,512]{1,0:T(8,128)(2,1)S(1)} collective-permute-done((bf16[512,512]{1,0:T(8,128)(2,1)}, bf16[512,512]{1,0:T(8,128)(2,1)S(1)}, u32[]{:S(2)}, u32[]{:S(2)}) %collective-permute-start.19) | collective-permute-done | bytes 524320 | tf_op jit(solution)/shard_map/ppermute | solution.py:761
  90.8 3.7 %outputs.1 = (bf16[512,1024]{1,0:T(8,128)(2,1)S(1)}, bf16[256,1024]{1,0:T(8,128)(2,1)S(1)}, bf16[256,1024]{1,0:T(8,128)(2,1)S(1)}, f32[8,1024]{1,0:T(8,128)S(1)}) custom-call(s32[1]{0:T(128)} %bitcast.where, f32[8,1024]{1,0:T(8,128)S(1)} %merge.7.stats_ref, f32[3,2048]{1,0:T(4,128)S(1)} %pad_maximum_fusion.constants, ...), custom_call_target="tpu_custom_call" | custom-call | tf_op jit(solution)/shard_map/outputs/pallas_call | solution.py:52
  99.5 3.2 %collective-permute-done.20.received = bf16[512,512]{1,0:T(8,128)(2,1)S(1)} collective-permute-done((bf16[512,512]{1,0:T(8,128)(2,1)S(1)}, bf16[512,512]{1,0:T(8,128)(2,1)S(1)}, u32[]{:S(2)}, u32[]{:S(2)}) %collective-permute-start.20) | collective-permute-done | bytes 524320 | tf_op jit(solution)/shard_map/ppermute | solution.py:761
  105.4 3.9 %collective-permute-done.22.received = bf16[256,512]{1,0:T(8,128)(2,1)S(1)} collective-permute-done((bf16[256,512]{1,0:T(8,128)(2,1)S(1)}, bf16[256,512]{1,0:T(8,128)(2,1)S(1)}, u32[]{:S(2)}, u32[]{:S(2)}) %collective-permute-start.22) | collective-permute-done | bytes 262176 | tf_op jit(solution)/shard_map/ppermute | solution.py:761
  114.3 4.0 %collective-permute-done.26.received = bf16[128,512]{1,0:T(8,128)(2,1)S(1)} collective-permute-done((bf16[128,512]{1,0:T(8,128)(2,1)S(1)}, bf16[128,512]{1,0:T(8,128)(2,1)S(1)}, u32[]{:S(2)}, u32[]{:S(2)}) %collective-permute-start.26) | collective-permute-done | bytes 131104 | tf_op jit(solution)/shard_map/ppermute | solution.py:761
  118.5 5.4 %collective-permute-done.25.received = bf16[128,512]{1,0:T(8,128)(2,1)S(1)} collective-permute-done((bf16[128,512]{1,0:T(8,128)(2,1)S(1)}, bf16[128,512]{1,0:T(8,128)(2,1)S(1)}, u32[]{:S(2)}, u32[]{:S(2)}) %collective-permute-start.25) | collective-permute-done | bytes 131104 | tf_op jit(solution)/shard_map/ppermute | solution.py:761
  124.4 2.7 %collective-permute-start.27 = (bf16[256,1024]{1,0:T(8,128)(2,1)S(1)}, bf16[256,1024]{1,0:T(8,128)(2,1)S(1)}, u32[]{:S(2)}, u32[]{:S(2)}) collective-permute-start(bf16[256,1024]{1,0:T(8,128)(2,1)S(1)} %get-tuple-element.316), channel_id=1, source_target_pairs={{0,4},{1,9},{2,6},{3,11},{4,0},{5,13},{6,2},{7,15},{8,12},{9,1},{1... | collective-permute-start | bytes 1572872 | tf_op jit(solution)/shard_map/ppermute | solution.py:761
  127.1 3.3 %collective-permute-done.31.received = bf16[128,512]{1,0:T(8,128)(2,1)S(1)} collective-permute-done((bf16[128,512]{1,0:T(8,128)(2,1)S(1)}, bf16[128,512]{1,0:T(8,128)(2,1)S(1)}, u32[]{:S(2)}, u32[]{:S(2)}) %collective-permute-start.31) | collective-permute-done | bytes 131104 | tf_op jit(solution)/shard_map/ppermute | solution.py:761
  130.4 5.9 %collective-permute-start.35 = (bf16[256,512]{1,0:T(8,128)(2,1)S(1)}, bf16[256,512]{1,0:T(8,128)(2,1)S(1)}, u32[]{:S(2)}, u32[]{:S(2)}) collective-permute-start(bf16[256,512]{1,0:T(8,128)(2,1)S(1)} %join.5.own), channel_id=1, source_target_pairs={{0,8},{1,3},{2,10},{3,1},{4,12},{5,7},{6,14},{7,5},{8,0},{9,11},{1... | collective-permute-start | bytes 786440 | tf_op jit(solution)/shard_map/ppermute | solution.py:761
  136.6 5.0 %collective-permute-start.33 = (bf16[128,1024]{1,0:T(8,128)(2,1)S(1)}, bf16[128,1024]{1,0:T(8,128)(2,1)S(1)}, u32[]{:S(2)}, u32[]{:S(2)}) collective-permute-start(bf16[128,1024]{1,0:T(8,128)(2,1)S(1)} %get-tuple-element.330), channel_id=1, source_target_pairs={{0,8},{1,3},{2,10},{3,1},{4,12},{5,7},{6,14},{7,5},{8,0},{9,11},{1... | collective-permute-start | bytes 786440 | tf_op jit(solution)/shard_map/ppermute | solution.py:761
  142.7 3.7 %collective-permute-done.34.received = bf16[256,512]{1,0:T(8,128)(2,1)S(1)} collective-permute-done((bf16[256,512]{1,0:T(8,128)(2,1)S(1)}, bf16[256,512]{1,0:T(8,128)(2,1)S(1)}, u32[]{:S(2)}, u32[]{:S(2)}) %collective-permute-start.34) | collective-permute-done | bytes 262176 | tf_op jit(solution)/shard_map/ppermute | solution.py:761
  148.4 3.7 %collective-permute-done.33.received = bf16[128,1024]{1,0:T(8,128)(2,1)S(1)} collective-permute-done((bf16[128,1024]{1,0:T(8,128)(2,1)S(1)}, bf16[128,1024]{1,0:T(8,128)(2,1)S(1)}, u32[]{:S(2)}, u32[]{:S(2)}) %collective-permute-start.33) | collective-permute-done | bytes 262176 | tf_op jit(solution)/shard_map/ppermute | solution.py:761
  159.3 3.4 %place.3.refs_8_ = f32[2048,2048]{1,0:T(8,128)} custom-call(s32[12]{0:T(128)S(1)} %stack.182.where, bf16[512,512]{1,0:T(8,128)(2,1)S(1)} %join.6.refs_0_, bf16[512,512]{1,0:T(8,128)(2,1)S(1)} %join.7.refs_1_, bf16[512,512]{1,0:T(8,128)(2,1)S(1)} %copy-done.6, bf16[512,512]{1,0:T(8,128)(2,1)} %collective-permute-done.40.refs_3_), custom_call_target="tpu_custom_call" | custom-call | tf_op jit(solution)/shard_map/place/pallas_call | solution.py:52
  162.7 3.4 %collective-permute-done.36.received = bf16[64,1024]{1,0:T(8,128)(2,1)S(1)} collective-permute-done((bf16[64,1024]{1,0:T(8,128)(2,1)S(1)}, bf16[64,1024]{1,0:T(8,128)(2,1)S(1)}, u32[]{:S(2)}, u32[]{:S(2)}) %collective-permute-start.36) | collective-permute-done | bytes 131104 | tf_op jit(solution)/shard_map/ppermute | solution.py:761
  169.8 7.8 %finish.1 = (bf16[256,2048]{1,0:T(8,128)(2,1)}, bf16[256,2048]{1,0:T(8,128)(2,1)}, f32[8,2048]{1,0:T(8,128)S(1)}) custom-call(s32[1]{0:T(128)} %bitcast.where, s32[32,1]{1,0:T(8,128)S(1)} %copy.33.rows, bf16[64,1024]{1,0:T(8,128)(2,1)S(1)} %total.5.back, bf16[32,1024]{1,0:T(8,128)(2,1)S(1)} %collective-permute-done.41.back_in, ...), custom_call_target="tpu_custom_call" | custom-call | tf_op jit(solution)/shard_map/finish/pallas_call | solution.py:52
  177.7 4.5 %place.4.refs_4_ = f32[2048,2048]{1,0:T(8,128)} custom-call(s32[24]{0:T(128)S(1)} %stack.194.where, bf16[512,512]{1,0:T(8,128)(2,1)S(1)} %collective-permute-done.39.refs_0_, bf16[512,512]{1,0:T(8,128)(2,1)S(1)} %collective-permute-done.43.refs_1_, bf16[512,512]{1,0:T(8,128)(2,1)} %collective-permute-done.45.refs_2_, ...), custom_call_target="tpu_custom_call", output_to_operand_aliasing={{}: (9, {})} | custom-call | tf_op jit(solution)/shard_map/place/pallas_call | solution.py:52
  185.4 2.6 %place.5 = f32[2048,2048]{1,0:T(8,128)} custom-call(s32[12]{0:T(128)S(1)} %stack.193.where, bf16[512,512]{1,0:T(8,128)(2,1)S(1)} %collective-permute-done.44.refs_0_, bf16[512,512]{1,0:T(8,128)(2,1)S(1)} %collective-permute-done.49.refs_1_, bf16[512,512]{1,0:T(8,128)(2,1)S(1)} %collective-permute-done.50.refs_2_, ...), custom_call_target="tpu_custom_call", output_to_operand_aliasing={{}: (5, {})} | custom-call | tf_op jit(solution)/shard_map/place/pallas_call | solution.py:52
  (180 shorter events, 67.3 us)
Async XLA Ops:
  0.6 23.6 %collective-permute-start.4 = (bf16[256,2048]{1,0:T(8,128)(2,1)}, bf16[256,2048]{1,0:T(8,128)(2,1)S(1)}, u32[]{:S(2)}, u32[]{:S(2)}) collective-permute-start(bf16[256,2048]{1,0:T(8,128)(2,1)} %features.3), channel_id=1, source_target_pairs={{0,1},{1,0},{2,3},{3,2},{4,5},{5,4},{6,7},{7,6},{8,9},{9,8},{10,11... | collective-permute-start | bytes 3145736 | tf_op jit(solution)/shard_map/ppermute | solution.py:764
  1.1 24.0 %collective-permute-start.5 = (bf16[256,2048]{1,0:T(8,128)(2,1)}, bf16[256,2048]{1,0:T(8,128)(2,1)}, u32[]{:S(2)}, u32[]{:S(2)}) collective-permute-start(bf16[256,2048]{1,0:T(8,128)(2,1)} %cotangent.7), channel_id=1, source_target_pairs={{0,1},{1,0},{2,3},{3,2},{4,5},{5,4},{6,7},{7,6},{8,9},{9,8},{10,11... | collective-permute-start | bytes 3145736 | tf_op jit(solution)/shard_map/ppermute | solution.py:764
  23.5 9.3 %collective-permute-start.10 = (bf16[256,512]{1,0:T(8,128)(2,1)S(1)}, bf16[256,512]{1,0:T(8,128)(2,1)S(1)}, u32[]{:S(2)}, u32[]{:S(2)}) collective-permute-start(bf16[256,512]{1,0:T(8,128)(2,1)S(1)} %stack_rows.12.own), channel_id=1, source_target_pairs={{0,4},{1,9},{2,6},{3,11},{4,0},{5,13},{6,2},{7,15},{8,12},{9,1},{1... | collective-permute-start | bytes 786440 | tf_op jit(solution)/shard_map/ppermute | solution.py:761
  28.3 9.2 %collective-permute-start.9 = (bf16[512,512]{1,0:T(8,128)(2,1)S(1)}, bf16[512,512]{1,0:T(8,128)(2,1)S(1)}, u32[]{:S(2)}, u32[]{:S(2)}) collective-permute-start(bf16[512,512]{1,0:T(8,128)(2,1)S(1)} %stack_rows.11.own), channel_id=1, source_target_pairs={{0,2},{1,5},{2,0},{3,7},{4,6},{5,1},{6,4},{7,3},{8,10},{9,13},{10,... | collective-permute-start | bytes 1572872 | tf_op jit(solution)/shard_map/ppermute | solution.py:761
  32.8 10.4 %collective-permute-start.11 = (bf16[512,512]{1,0:T(8,128)(2,1)S(1)}, bf16[512,512]{1,0:T(8,128)(2,1)S(1)}, u32[]{:S(2)}, u32[]{:S(2)}) collective-permute-start(bf16[512,512]{1,0:T(8,128)(2,1)S(1)} %stack_rows.14.own), channel_id=1, source_target_pairs={{0,2},{1,5},{2,0},{3,7},{4,6},{5,1},{6,4},{7,3},{8,10},{9,13},{10,... | collective-permute-start | bytes 1572872 | tf_op jit(solution)/shard_map/ppermute | solution.py:761
  46.1 15.0 %collective-permute-start.14 = (bf16[512,1024]{1,0:T(8,128)(2,1)S(1)}, bf16[512,1024]{1,0:T(8,128)(2,1)}, u32[]{:S(2)}, u32[]{:S(2)}) collective-permute-start(bf16[512,1024]{1,0:T(8,128)(2,1)S(1)} %aggregate.1.mine), channel_id=1, source_target_pairs={{0,2},{1,5},{2,0},{3,7},{4,6},{5,1},{6,4},{7,3},{8,10},{9,13},{10,... | collective-permute-start | bytes 3145736 | tf_op jit(solution)/shard_map/ppermute | solution.py:761
  48.7 23.9 %collective-permute-start.18 = (bf16[512,1024]{1,0:T(8,128)(2,1)S(1)}, bf16[512,1024]{1,0:T(8,128)(2,1)}, u32[]{:S(2)}, u32[]{:S(2)}) collective-permute-start(bf16[512,1024]{1,0:T(8,128)(2,1)S(1)} %collective-permute-done.12.other), channel_id=1, source_target_pairs={{0,2},{1,5},{2,0},{3,7},{4,6},{5,1},{6,4},{7,3},{8,10},{9,13},{10,... | collective-permute-start | bytes 3145736 | tf_op jit(solution)/shard_map/ppermute | solution.py:761
  77.6 9.5 %collective-permute-start.19 = (bf16[512,512]{1,0:T(8,128)(2,1)}, bf16[512,512]{1,0:T(8,128)(2,1)S(1)}, u32[]{:S(2)}, u32[]{:S(2)}) collective-permute-start(bf16[512,512]{1,0:T(8,128)(2,1)} %dz.2), channel_id=1, source_target_pairs={{0,2},{1,5},{2,0},{3,7},{4,6},{5,1},{6,4},{7,3},{8,10},{9,13},{10,... | collective-permute-start | bytes 1572872 | tf_op jit(solution)/shard_map/ppermute | solution.py:761
  87.9 10.5 %collective-permute-start.21 = (bf16[512,512]{1,0:T(8,128)(2,1)S(1)}, bf16[512,512]{1,0:T(8,128)(2,1)S(1)}, u32[]{:S(2)}, u32[]{:S(2)}) collective-permute-start(bf16[512,512]{1,0:T(8,128)(2,1)S(1)} %weight_part.7), channel_id=1, source_target_pairs={{0,4},{1,9},{2,6},{3,11},{4,0},{5,13},{6,2},{7,15},{8,12},{9,1},{1... | collective-permute-start | bytes 1572872 | tf_op jit(solution)/shard_map/ppermute | solution.py:761
  90.1 12.6 %collective-permute-start.20 = (bf16[512,512]{1,0:T(8,128)(2,1)S(1)}, bf16[512,512]{1,0:T(8,128)(2,1)S(1)}, u32[]{:S(2)}, u32[]{:S(2)}) collective-permute-start(bf16[512,512]{1,0:T(8,128)(2,1)S(1)} %weight_part.6), channel_id=1, source_target_pairs={{0,4},{1,9},{2,6},{3,11},{4,0},{5,13},{6,2},{7,15},{8,12},{9,1},{1... | collective-permute-start | bytes 1572872 | tf_op jit(solution)/shard_map/ppermute | solution.py:761
  109.3 14.8 %collective-permute-start.24 = (bf16[512,1024]{1,0:T(8,128)(2,1)S(1)}, bf16[512,1024]{1,0:T(8,128)(2,1)S(1)}, u32[]{:S(2)}, u32[]{:S(2)}) collective-permute-start(bf16[512,1024]{1,0:T(8,128)(2,1)S(1)} %back_part.2), channel_id=1, source_target_pairs={{0,2},{1,5},{2,0},{3,7},{4,6},{5,1},{6,4},{7,3},{8,10},{9,13},{10,... | collective-permute-start | bytes 3145736 | tf_op jit(solution)/shard_map/ppermute | solution.py:761
  112.5 11.4 %collective-permute-start.25 = (bf16[128,512]{1,0:T(8,128)(2,1)S(1)}, bf16[128,512]{1,0:T(8,128)(2,1)S(1)}, u32[]{:S(2)}, u32[]{:S(2)}) collective-permute-start(bf16[128,512]{1,0:T(8,128)(2,1)S(1)} %get-tuple-element.302), channel_id=1, source_target_pairs={{0,16},{1,17},{2,18},{3,19},{4,20},{5,21},{6,22},{7,23},{8,24},{9,... | collective-permute-start | bytes 393224 | tf_op jit(solution)/shard_map/ppermute | solution.py:761
  113.3 23.0 %collective-permute-start.29 = (bf16[256,1024]{1,0:T(8,128)(2,1)S(1)}, bf16[256,1024]{1,0:T(8,128)(2,1)S(1)}, u32[]{:S(2)}, u32[]{:S(2)}) collective-permute-start(bf16[256,1024]{1,0:T(8,128)(2,1)S(1)} %get-tuple-element.318), channel_id=1, source_target_pairs={{0,1},{1,0},{2,3},{3,2},{4,5},{5,4},{6,7},{7,6},{8,9},{9,8},{10,11... | collective-permute-start | bytes 1572872 | tf_op jit(solution)/shard_map/ppermute | solution.py:764
  113.8 22.5 %collective-permute-start.28 = (bf16[256,1024]{1,0:T(8,128)(2,1)S(1)}, bf16[256,1024]{1,0:T(8,128)(2,1)S(1)}, u32[]{:S(2)}, u32[]{:S(2)}) collective-permute-start(bf16[256,1024]{1,0:T(8,128)(2,1)S(1)} %get-tuple-element.317), channel_id=1, source_target_pairs={{0,1},{1,0},{2,3},{3,2},{4,5},{5,4},{6,7},{7,6},{8,9},{9,8},{10,11... | collective-permute-start | bytes 1572872 | tf_op jit(solution)/shard_map/ppermute | solution.py:764
  118.4 8.6 %collective-permute-start.32 = (bf16[128,512]{1,0:T(8,128)(2,1)S(1)}, bf16[128,512]{1,0:T(8,128)(2,1)S(1)}, u32[]{:S(2)}, u32[]{:S(2)}) collective-permute-start(bf16[128,512]{1,0:T(8,128)(2,1)S(1)} %total.4.own), channel_id=1, source_target_pairs={{0,16},{1,17},{2,18},{3,19},{4,20},{5,21},{6,22},{7,23},{8,24},{9,... | collective-permute-start | bytes 393224 | tf_op jit(solution)/shard_map/ppermute | solution.py:761
  124.4 12.1 %collective-permute-start.27 = (bf16[256,1024]{1,0:T(8,128)(2,1)S(1)}, bf16[256,1024]{1,0:T(8,128)(2,1)S(1)}, u32[]{:S(2)}, u32[]{:S(2)}) collective-permute-start(bf16[256,1024]{1,0:T(8,128)(2,1)S(1)} %get-tuple-element.316), channel_id=1, source_target_pairs={{0,4},{1,9},{2,6},{3,11},{4,0},{5,13},{6,2},{7,15},{8,12},{9,1},{1... | collective-permute-start | bytes 1572872 | tf_op jit(solution)/shard_map/ppermute | solution.py:761
  127.0 9.2 %collective-permute-start.30 = (f32[8,1024]{1,0:T(8,128)S(1)}, f32[8,1024]{1,0:T(8,128)S(1)}, u32[]{:S(2)}, u32[]{:S(2)}) collective-permute-start(f32[8,1024]{1,0:T(8,128)S(1)} %get-tuple-element.319.vec), channel_id=1, source_target_pairs={{0,1},{1,0},{2,3},{3,2},{4,5},{5,4},{6,7},{7,6},{8,9},{9,8},{10,11... | collective-permute-start | bytes 98312 | tf_op jit(solution)/shard_map/ppermute | solution.py:764
  130.4 11.1 %collective-permute-start.35 = (bf16[256,512]{1,0:T(8,128)(2,1)S(1)}, bf16[256,512]{1,0:T(8,128)(2,1)S(1)}, u32[]{:S(2)}, u32[]{:S(2)}) collective-permute-start(bf16[256,512]{1,0:T(8,128)(2,1)S(1)} %join.5.own), channel_id=1, source_target_pairs={{0,8},{1,3},{2,10},{3,1},{4,12},{5,7},{6,14},{7,5},{8,0},{9,11},{1... | collective-permute-start | bytes 786440 | tf_op jit(solution)/shard_map/ppermute | solution.py:761
  136.3 10.1 %collective-permute-start.34 = (bf16[256,512]{1,0:T(8,128)(2,1)S(1)}, bf16[256,512]{1,0:T(8,128)(2,1)S(1)}, u32[]{:S(2)}, u32[]{:S(2)}) collective-permute-start(bf16[256,512]{1,0:T(8,128)(2,1)S(1)} %join.4.own), channel_id=1, source_target_pairs={{0,8},{1,3},{2,10},{3,1},{4,12},{5,7},{6,14},{7,5},{8,0},{9,11},{1... | collective-permute-start | bytes 786440 | tf_op jit(solution)/shard_map/ppermute | solution.py:761
  136.6 15.5 %collective-permute-start.33 = (bf16[128,1024]{1,0:T(8,128)(2,1)S(1)}, bf16[128,1024]{1,0:T(8,128)(2,1)S(1)}, u32[]{:S(2)}, u32[]{:S(2)}) collective-permute-start(bf16[128,1024]{1,0:T(8,128)(2,1)S(1)} %get-tuple-element.330), channel_id=1, source_target_pairs={{0,8},{1,3},{2,10},{3,1},{4,12},{5,7},{6,14},{7,5},{8,0},{9,11},{1... | collective-permute-start | bytes 786440 | tf_op jit(solution)/shard_map/ppermute | solution.py:761
  141.6 11.2 %collective-permute-start.39 = (bf16[512,512]{1,0:T(8,128)(2,1)S(1)}, bf16[512,512]{1,0:T(8,128)(2,1)S(1)}, u32[]{:S(2)}, u32[]{:S(2)}) collective-permute-start(bf16[512,512]{1,0:T(8,128)(2,1)S(1)} %join.6.refs_0_), channel_id=1, source_target_pairs={{0,4},{1,9},{2,6},{3,11},{4,0},{5,13},{6,2},{7,15},{8,12},{9,1},{1... | collective-permute-start | bytes 1572872 | tf_op jit(solution)/shard_map/ppermute | solution.py:761
  142.7 11.8 %collective-permute-start.38 = (bf16[512,512]{1,0:T(8,128)(2,1)S(1)}, bf16[512,512]{1,0:T(8,128)(2,1)S(1)}, u32[]{:S(2)}, u32[]{:S(2)}) collective-permute-start(bf16[512,512]{1,0:T(8,128)(2,1)S(1)} %join.6.refs_0_), channel_id=1, source_target_pairs={{0,1},{1,0},{2,3},{3,2},{4,5},{5,4},{6,7},{7,6},{8,9},{9,8},{10,11... | collective-permute-start | bytes 1572872 | tf_op jit(solution)/shard_map/ppermute | solution.py:764
  146.5 9.9 %collective-permute-start.40 = (bf16[512,512]{1,0:T(8,128)(2,1)S(1)}, bf16[512,512]{1,0:T(8,128)(2,1)}, u32[]{:S(2)}, u32[]{:S(2)}) collective-permute-start(bf16[512,512]{1,0:T(8,128)(2,1)S(1)} %join.7.refs_1_), channel_id=1, source_target_pairs={{0,1},{1,0},{2,3},{3,2},{4,5},{5,4},{6,7},{7,6},{8,9},{9,8},{10,11... | collective-permute-start | bytes 1572872 | tf_op jit(solution)/shard_map/ppermute | solution.py:764
  146.6 16.1 %collective-permute-start.37 = (bf16[512,512]{1,0:T(8,128)(2,1)S(1)}, bf16[512,512]{1,0:T(8,128)(2,1)S(1)}, u32[]{:S(2)}, u32[]{:S(2)}) collective-permute-start(bf16[512,512]{1,0:T(8,128)(2,1)S(1)} %join.6.refs_0_), channel_id=1, source_target_pairs={{0,2},{1,5},{2,0},{3,7},{4,6},{5,1},{6,4},{7,3},{8,10},{9,13},{10,... | collective-permute-start | bytes 1572872 | tf_op jit(solution)/shard_map/ppermute | solution.py:761
  152.8 14.9 %collective-permute-start.43 = (bf16[512,512]{1,0:T(8,128)(2,1)S(1)}, bf16[512,512]{1,0:T(8,128)(2,1)S(1)}, u32[]{:S(2)}, u32[]{:S(2)}) collective-permute-start(bf16[512,512]{1,0:T(8,128)(2,1)S(1)} %join.7.refs_1_), channel_id=1, source_target_pairs={{0,4},{1,9},{2,6},{3,11},{4,0},{5,13},{6,2},{7,15},{8,12},{9,1},{1... | collective-permute-start | bytes 1572872 | tf_op jit(solution)/shard_map/ppermute | solution.py:761
  152.8 15.9 %collective-permute-start.42 = (bf16[512,512]{1,0:T(8,128)(2,1)S(1)}, bf16[512,512]{1,0:T(8,128)(2,1)S(1)}, u32[]{:S(2)}, u32[]{:S(2)}) collective-permute-start(bf16[512,512]{1,0:T(8,128)(2,1)S(1)} %join.7.refs_1_), channel_id=1, source_target_pairs={{0,2},{1,5},{2,0},{3,7},{4,6},{5,1},{6,4},{7,3},{8,10},{9,13},{10,... | collective-permute-start | bytes 1572872 | tf_op jit(solution)/shard_map/ppermute | solution.py:761
  155.3 14.0 %collective-permute-start.45 = (bf16[512,512]{1,0:T(8,128)(2,1)S(1)}, bf16[512,512]{1,0:T(8,128)(2,1)}, u32[]{:S(2)}, u32[]{:S(2)}) collective-permute-start(bf16[512,512]{1,0:T(8,128)(2,1)S(1)} %collective-permute-done.39.refs_0_), channel_id=1, source_target_pairs={{0,1},{1,0},{2,3},{3,2},{4,5},{5,4},{6,7},{7,6},{8,9},{9,8},{10,11... | collective-permute-start | bytes 1572872 | tf_op jit(solution)/shard_map/ppermute | solution.py:764
  156.4 9.7 %collective-permute-start.36 = (bf16[64,1024]{1,0:T(8,128)(2,1)S(1)}, bf16[64,1024]{1,0:T(8,128)(2,1)S(1)}, u32[]{:S(2)}, u32[]{:S(2)}) collective-permute-start(bf16[64,1024]{1,0:T(8,128)(2,1)S(1)} %get-tuple-element.338), channel_id=1, source_target_pairs={{0,16},{1,17},{2,18},{3,19},{4,20},{5,21},{6,22},{7,23},{8,24},{9,... | collective-permute-start | bytes 393224 | tf_op jit(solution)/shard_map/ppermute | solution.py:761
  166.5 15.7 %collective-permute-start.44 = (bf16[512,512]{1,0:T(8,128)(2,1)S(1)}, bf16[512,512]{1,0:T(8,128)(2,1)S(1)}, u32[]{:S(2)}, u32[]{:S(2)}) collective-permute-start(bf16[512,512]{1,0:T(8,128)(2,1)S(1)} %collective-permute-done.39.refs_0_), channel_id=1, source_target_pairs={{0,2},{1,5},{2,0},{3,7},{4,6},{5,1},{6,4},{7,3},{8,10},{9,13},{10,... | collective-permute-start | bytes 1572872 | tf_op jit(solution)/shard_map/ppermute | solution.py:761
  167.6 10.0 %collective-permute-start.46 = (bf16[512,512]{1,0:T(8,128)(2,1)S(1)}, bf16[512,512]{1,0:T(8,128)(2,1)S(1)}, u32[]{:S(2)}, u32[]{:S(2)}) collective-permute-start(bf16[512,512]{1,0:T(8,128)(2,1)S(1)} %collective-permute-done.43.refs_1_), channel_id=1, source_target_pairs={{0,1},{1,0},{2,3},{3,2},{4,5},{5,4},{6,7},{7,6},{8,9},{9,8},{10,11... | collective-permute-start | bytes 1572872 | tf_op jit(solution)/shard_map/ppermute | solution.py:764
  168.7 13.5 %collective-permute-start.49 = (bf16[512,512]{1,0:T(8,128)(2,1)S(1)}, bf16[512,512]{1,0:T(8,128)(2,1)S(1)}, u32[]{:S(2)}, u32[]{:S(2)}) collective-permute-start(bf16[512,512]{1,0:T(8,128)(2,1)S(1)} %collective-permute-done.43.refs_1_), channel_id=1, source_target_pairs={{0,2},{1,5},{2,0},{3,7},{4,6},{5,1},{6,4},{7,3},{8,10},{9,13},{10,... | collective-permute-start | bytes 1572872 | tf_op jit(solution)/shard_map/ppermute | solution.py:761
  169.3 8.4 %collective-permute-start.48 = (bf16[512,512]{1,0:T(8,128)(2,1)S(1)}, bf16[512,512]{1,0:T(8,128)(2,1)S(1)}, u32[]{:S(2)}, u32[]{:S(2)}) collective-permute-start(bf16[512,512]{1,0:T(8,128)(2,1)S(1)} %collective-permute-done.42.refs_5_), channel_id=1, source_target_pairs={{0,1},{1,0},{2,3},{3,2},{4,5},{5,4},{6,7},{7,6},{8,9},{9,8},{10,11... | collective-permute-start | bytes 1572872 | tf_op jit(solution)/shard_map/ppermute | solution.py:764
  (38 other events, 382.1 us)
